TPU v7x, 32 devices: a whole 2x2x4 slice. The times are simulated.
32 devices in a mesh: pair: 8 (over z, core), red: 4 (over y, x).
Axes of the slice: x: 2, y: 2, z: 4, core: 2. Of those that a mesh axis runs over, the one named last changes fastest.
Arguments:
- three_center: bfloat16 [2304, 32, 256], P('pair', 'red'), may hold values from -0.375 to 0.375
- occ_src: int32 [32, 8], P('red'), may hold values from 0 to 7, as said below
- occ_block: int32 [32, 8], P('red'), may hold values from 0 to 15
- occ_blocks: bfloat16 [64, 256], P('red'), may hold values from -0.5 to 0.5
- virt_block: int32 [4, 8, 1], P('red'), may hold values from 0 to 15, as said below
- virt_blocks: bfloat16 [4, 16, 256], P('red', 'pair'), may hold values from -1.5 to 1.5
Outputs:
- chi: float32 [2304, 2304], P('pair', 'red')
Inputs may be any that keep to these rules, and one draw needn't show every extreme that they name: `occ_src`: the 8 entries of a row are distinct. `virt_block`: every block listed for tile t of a red group lies from (t) * 2 to (t) * 2 + 1.
All inputs are finite; a program needn't handle non-finite values.
Results may differ from a plain program's by a relative error of at most 0.0041.
Values may be sent and summed in bfloat16 or wider, within the bound.
No kernel may reach another device: no remote copies, remote signals or barrier semaphores. Data moves between devices by JAX's collectives and lax.ppermute only.
A program may use at most 128 MiB of HBM per device.

v0:
```python
import jax
import jax.numpy as jnp
from jax import lax
from jax.sharding import PartitionSpec as P

BLK = 16
TPD = 1


def occupied(three_center, occ_src, occ_block, occ_blocks):
    aux_rows, ntiles, area = three_center.shape
    nblocks = occ_blocks.shape[0]
    block_hot = (
        occ_block[:, :, None] == jnp.arange(nblocks, dtype=jnp.int32)[None, None, :]
    ).astype(jnp.bfloat16)
    picked = jnp.einsum(
        "tsb,bk->tsk", block_hot, occ_blocks, preferred_element_type=jnp.float32
    ).astype(jnp.bfloat16)
    source_hot = (occ_src[:, :, None] == jnp.arange(ntiles, dtype=jnp.int32)[None, None, :]).astype(
        jnp.bfloat16
    )
    mixing = jnp.einsum(
        "tsk,tsa->tka", source_hot, picked, preferred_element_type=jnp.float32
    ).astype(jnp.bfloat16)
    mixing = mixing.reshape(ntiles, ntiles, BLK, BLK)
    blocks = three_center.reshape(aux_rows, ntiles, BLK, BLK)
    half = jnp.einsum("tkml,pkln->ptmn", mixing, blocks, preferred_element_type=jnp.float32)
    return half.reshape(aux_rows, ntiles, area).astype(jnp.bfloat16)


def virtual(half, listed, blocks):
    aux_rows, ntiles, area = half.shape
    owners = listed.shape[0]
    nblocks = blocks.shape[0]
    block_hot = (listed[..., None] == jnp.arange(nblocks, dtype=jnp.int32)).astype(jnp.bfloat16)
    picked = jnp.einsum(
        "oijb,bk->oijk", block_hot, blocks, preferred_element_type=jnp.float32
    ).astype(jnp.bfloat16)
    picked = picked.reshape(owners, TPD, TPD, BLK, BLK)
    grouped = half.reshape(aux_rows, owners, TPD, BLK, BLK)
    kernel = jnp.einsum("pojml,oijln->poimn", grouped, picked, preferred_element_type=jnp.float32)
    return kernel.reshape(aux_rows, ntiles, area).astype(jnp.bfloat16)


def shards(three_center, occ_src, occ_block, occ_blocks, virt_block, virt_blocks):
    aux_rows, ntiles, area = three_center.shape
    half = occupied(three_center, occ_src, occ_block, occ_blocks)
    own_blocks = virt_blocks[0]
    listed = virt_block[0]
    all_blocks = lax.all_gather(own_blocks, "pair", axis=0, tiled=True)
    kernel = virtual(half, listed.reshape(ntiles // TPD, TPD, TPD), all_blocks)
    flat_tiles = three_center.reshape(aux_rows, ntiles * area)
    piece = lax.all_gather(kernel, "pair", axis=0, tiled=True)
    flat_piece = piece.reshape(piece.shape[0], ntiles * area)
    partial_value = lax.dot_general(
        flat_tiles, flat_piece, (((1,), (1,)), ((), ())), preferred_element_type=jnp.float32
    )
    return lax.psum_scatter(partial_value, "red", scatter_dimension=1, tiled=True)


def solution(mesh):
    placed = (
        P("pair", "red", None),
        P("red", None),
        P("red", None),
        P("red", None),
        P("red", None, None),
        P("red", "pair", None),
    )
    return jax.shard_map(
        shards, mesh=mesh, in_specs=placed, out_specs=P("pair", "red"), check_vma=False
    )
```

profile of v0, /device:TPU:7, one launch (start us, length us, event | category | flops | bytes accessed | tf_op | source)
XLA Modules:
  0.0 182.2 jit_solution(6115198022241470797)
XLA Ops:
  6.5 0.0 copy-start
  6.5 0.0 all-gather.3.cloned.1.call-start
  6.5 0.7 copy.21
  7.2 13.4 %all-gather = bf16[1,16,256]{2,0,1:T(2,128)(2,1)S(1)} all-gather(bf16[1,2,256]{2,0,1:T(2,128)(2,1)S(1)} %copy.21), channel_id=2, replica_groups=mesh['pair'=8,'red'=4] {'pair'}, dimensions={1}, use_global_device_ids=true | all-gather | bytes 9216 | tf_op jit(solution)/shard_map/all_gather | solution.py:50
  20.6 0.8 convolution_convert_fusion.3
  21.5 0.1 reshape.42
  21.6 0.0 copy-done
  21.6 1.0 convolution_convert_fusion.1
  22.6 0.2 reshape.47
  22.8 1.9 %copy.22 = bf16[288,8,256]{0,2,1:T(8,128)(2,1)S(1)} copy(bf16[288,8,256]{2,1,0:T(8,128)(2,1)} %param.6) | data formatting | bytes 2359296 | tf_op args[0]
  24.8 0.0 copy-start.1
  24.8 1.2 copy-done.1
  25.9 1.0 fusion.3
  27.0 0.6 convolution_convert_fusion
  27.6 1.6 copy.26
  29.2 0.0 all-gather.3.cloned.1.call-update
  29.2 0.0 reduce-scatter.4.cloned.1.call-start
  29.2 90.5 %all-gather.3.cloned.1.call-done = bf16[2304,8,256]{2,0,1:T(8,128)(2,1)} async-done(((bf16[288,8,256]{2,0,1:T(8,128)(2,1)}), bf16[2304,8,256]{2,0,1:T(8,128)(2,1)}) %all-gather.3.cloned.1.call-update) | async-done | bytes 9437200 | tf_op jit(solution)/shard_map/all_gather | solution.py:53
  119.7 6.4 %convolution_bitcast_fusion = f32[288,2304]{1,0:T(8,128)S(1)} fusion(bf16[2304,8,256]{2,0,1:T(8,128)(2,1)} %all-gather.3.cloned.1.call-done, bf16[288,8,256]{0,2,1:T(8,128)(2,1)} %copy-done.1), kind=kOutput, calls=%fused_computation | convolution fusion | flops 2717908992 | bytes 13271040 | tf_op jit(solution)/shard_map/dot_general | solution.py:55
  126.1 2.5 %copy.33 = f32[288,2304]{0,1:T(8,128)} copy(f32[288,2304]{1,0:T(8,128)S(1)} %convolution_bitcast_fusion) | data formatting | bytes 5308416
  128.6 0.0 reduce-scatter.4.cloned.1.call-update
  128.6 44.5 %reduce-scatter.4.cloned.1.call-done = f32[576,288]{1,0:T(8,128)} async-done(((f32[2304,288]{1,0:T(8,128)}), f32[576,288]{1,0:T(8,128)}) %reduce-scatter.4.cloned.1.call-update) | async-done | bytes 663568
  173.1 2.3 %copy.34 = f32[288,576]{1,0:T(8,128)} copy(f32[288,576]{0,1:T(8,128)} %bitcast.45) | data formatting | bytes 1327104
Async XLA Ops:
  6.5 15.0 %copy-start = (bf16[16,256]{1,0:T(8,128)(2,1)S(1)}, bf16[16,256]{1,0:T(8,128)(2,1)}, u32[]{:S(2)}) copy-start(bf16[16,256]{1,0:T(8,128)(2,1)} %param.9) | copy-start | bytes 24580
  6.5 113.2 %all-gather.3.cloned.1.call-start = ((), (), s32[]{:S(2)}) async-start(), calls=%async_computation.1 | async-start | bytes 10616832 | tf_op jit(solution)/shard_map/all_gather | solution.py:53
  24.8 1.2 copy-start.1
  29.2 143.9 %reduce-scatter.4.cloned.1.call-start = ((), (), s32[]{:S(2)}) async-start(), calls=%async_computation.2 | async-start | bytes 4423680
Sparse Core Ops, SparseCore 0:
  29.3 90.3 all-gather.2
  128.7 44.2 reduce-scatter.3
where the time goes:
time: 185 us; the launch traced here: 182 us
  waiting for transfers between devices  135 us (73%)
  between operations  13.5 us (7%)
  blocking collectives  13.4 us (7%)
  local copies, waits for them, and re-layouts  10.5 us (6%)
  matrix products  9.88 us (5%)
    all_gather x1, waiting for transfers between devices, shards(): piece = lax.all_gather(kernel, 'pair', axis=0, tiled=True)  90.5 us
    unnamed x3, waiting for transfers between devices  44.5 us
    all_gather x1, blocking collectives, shards(): all_blocks = lax.all_gather(own_blocks, 'pair', axis=0, tiled=True)  13.4 us
    unnamed x8, local copies, waits for them, and re-layouts  8.61 us
    dot_general x1, matrix products, shards(): lax.dot_general(flat_tiles, flat_piece, (((1,), (1,)), ((), ())), preferr...  6.37 us
  transfers between devices with their start and end apart: 2, of which 2 were waited for; matrix products, arithmetic and copies ran while one was open for 0% of the time, Pallas kernels for 0%

commit v1 on v0

v1 whole, which is shorter than its diff:
```python
import functools

import jax
import jax.numpy as jnp
from jax import lax
from jax.experimental import pallas as pl
from jax.experimental.pallas import tpu as pltpu
from jax.sharding import PartitionSpec as P

BLK = 16
AREA = BLK * BLK
VMEM_BYTES = 48 * 1024 * 1024
CORES = 2
BF16 = jnp.bfloat16
F32 = jnp.float32


def mixing_of(occ_src, occ_block, occ_blocks, ntiles):
    nblocks = occ_blocks.shape[0]
    block_hot = (occ_block[:, :, None] == jnp.arange(nblocks, dtype=jnp.int32)).astype(BF16)
    picked = jnp.einsum("tsb,bk->tsk", block_hot, occ_blocks, preferred_element_type=F32).astype(BF16)
    source_hot = (occ_src[:, :, None] == jnp.arange(ntiles, dtype=jnp.int32)).astype(BF16)
    mixing = jnp.einsum("tsk,tsa->tka", source_hot, picked, preferred_element_type=F32).astype(BF16)
    return mixing.reshape(ntiles, ntiles, BLK, BLK)


def gather_plan(three_center, occ_src, occ_block, occ_blocks, virt_block, virt_blocks):
    aux_rows, ntiles, area = three_center.shape
    tpd = virt_block.shape[2]
    mixing = mixing_of(occ_src, occ_block, occ_blocks, ntiles)
    blocks = three_center.reshape(aux_rows, ntiles, BLK, BLK)
    half = jnp.einsum("tkml,pkln->ptmn", mixing, blocks, preferred_element_type=F32).astype(BF16)
    all_blocks = lax.all_gather(virt_blocks[0], "pair", axis=0, tiled=True)
    listed = virt_block[0].reshape(ntiles // tpd, tpd, tpd)
    block_hot = (listed[..., None] == jnp.arange(all_blocks.shape[0], dtype=jnp.int32)).astype(BF16)
    picked = jnp.einsum("oijb,bk->oijk", block_hot, all_blocks, preferred_element_type=F32).astype(BF16)
    picked = picked.reshape(ntiles // tpd, tpd, tpd, BLK, BLK)
    grouped = half.reshape(aux_rows, ntiles // tpd, tpd, BLK, BLK)
    kernel = jnp.einsum("pojml,oijln->poimn", grouped, picked, preferred_element_type=F32)
    kernel = kernel.reshape(aux_rows, ntiles, area).astype(BF16)
    piece = lax.all_gather(kernel, "pair", axis=0, tiled=True)
    partial_value = lax.dot_general(
        three_center.reshape(aux_rows, ntiles * area),
        piece.reshape(piece.shape[0], ntiles * area),
        (((1,), (1,)), ((), ())),
        preferred_element_type=F32,
    )
    return lax.psum_scatter(partial_value, "red", scatter_dimension=1, tiled=True)


def iota2(shape, dim):
    return lax.broadcasted_iota(jnp.int32, shape, dim)


def prep_body(virt_ref, wide_ref):
    ntiles = wide_ref.shape[0]
    spread_rows = (iota2((AREA, BLK), 0) % BLK == iota2((AREA, BLK), 1)).astype(BF16)
    spread_cols = (iota2((BLK, AREA), 1) // BLK == iota2((BLK, AREA), 0)).astype(BF16)
    same = iota2((AREA, AREA), 0) // BLK == iota2((AREA, AREA), 1) % BLK
    for t in range(ntiles):
        block = virt_ref[t * BLK:(t + 1) * BLK, :]
        rows = lax.dot_general(spread_rows, block, (((1,), (1,)), ((), ())), preferred_element_type=F32)
        full = jnp.dot(rows.astype(BF16), spread_cols, preferred_element_type=F32)
        wide_ref[t] = jnp.where(same, full, 0.0).astype(BF16)


def kernel_rows(tile_ref, mix_ref, wide_ref, out_ref, mixed, halves):
    ntiles = wide_ref.shape[0]
    rows = iota2((AREA, AREA), 0)
    cols = iota2((AREA, AREA), 1)
    swap = ((rows % BLK == cols // BLK) & (rows // BLK == cols % BLK)).astype(BF16)
    for k in range(ntiles):
        turned = lax.dot_general(
            swap, tile_ref[:, k * AREA:(k + 1) * AREA], (((1,), (1,)), ((), ())), preferred_element_type=F32
        ).astype(BF16)
        for n in range(BLK):
            mixed[n, k * BLK:(k + 1) * BLK, :] = turned[n * BLK:(n + 1) * BLK, :]
    mix = mix_ref[...]
    for n in range(BLK):
        half = jnp.dot(mix, mixed[n], preferred_element_type=F32).astype(BF16)
        for t in range(ntiles):
            halves[t, n * BLK:(n + 1) * BLK, :] = half[t * BLK:(t + 1) * BLK, :]
    for t in range(ntiles):
        out_ref[t * AREA:(t + 1) * AREA, :] = jnp.dot(
            wide_ref[t], halves[t], preferred_element_type=F32
        ).astype(BF16)


def k_body(tile_ref, mix_ref, wide_ref, out_ref, mixed, halves):
    kernel_rows(tile_ref, mix_ref, wide_ref, out_ref, mixed, halves)


def early_body(pick_ref, o_ref, p_ref, e_ref, f_ref, ko_ref, ke_ref, kb_ref, own_ref, s1, s2, s3, s4, terms):
    aux = o_ref.shape[0]
    for at, (upper, lower, right) in enumerate(
        ((o_ref, p_ref, ko_ref), (o_ref, p_ref, ke_ref), (o_ref, p_ref, kb_ref), (e_ref, f_ref, kb_ref))
    ):
        right_value = right[...]
        terms[at, :aux, :] = jnp.dot(upper[...], right_value, preferred_element_type=F32)
        terms[at, aux:, :] = jnp.dot(lower[...], right_value, preferred_element_type=F32)
    own = pick_ref[0]
    own_ref[...] = jnp.where(own >= 0, terms[jnp.maximum(own, 0)], 0.0)
    for at, out in enumerate((s1, s2, s3, s4)):
        out[...] = terms[pick_ref[1 + at]].astype(BF16)


def late_body(pick_ref, c_ref, o_ref, p_ref, e_ref, f_ref, mix_ref, wide_ref, own_ref, s1, s2, s3, s4, kt, mixed, halves):
    aux = o_ref.shape[0]
    kernel_rows(c_ref, mix_ref, wide_ref, kt, mixed, halves)
    right = kt[...]
    place = pick_ref[0]
    for upper, outer, at in ((o_ref, e_ref, 0), (p_ref, f_ref, aux)):
        rows = slice(at, at + aux)
        near = jnp.dot(upper[...], right, preferred_element_type=F32)
        far = jnp.dot(outer[...], right, preferred_element_type=F32).astype(BF16)
        sent = near.astype(BF16)
        own_ref[rows, :] = jnp.where(place == 3, near, 0.0)
        for source, out in enumerate((s1, s2, s3)):
            out[rows, :] = jnp.where(place == source, sent, far)
        s4[rows, :] = far


def call(body, outs, ins, scratch=(), smem=0, flops=0, name=None):
    return pl.pallas_call(
        body,
        out_shape=outs,
        in_specs=[pl.BlockSpec(memory_space=pltpu.SMEM)] * smem
        + [pl.BlockSpec(memory_space=pltpu.VMEM)] * (len(ins) - smem),
        out_specs=jax.tree.map(lambda _: pl.BlockSpec(memory_space=pltpu.VMEM), outs),
        scratch_shapes=list(scratch),
        compiler_params=pltpu.CompilerParams(vmem_limit_bytes=VMEM_BYTES),
        cost_estimate=pl.CostEstimate(
            flops=flops, transcendentals=0, bytes_accessed=sum(x.size * x.dtype.itemsize for x in ins)
        ),
        name=name,
    )(*ins)


def shaped(*shape, dtype=BF16):
    return jax.ShapeDtypeStruct(shape, dtype)


def hub_plan(three_center, occ_src, occ_block, occ_blocks, virt_block, virt_blocks):
    aux, ntiles, area = three_center.shape
    depth = ntiles * area
    pair, red = lax.axis_index("pair"), lax.axis_index("red")
    plane, core = pair // CORES, pair % CORES
    near_end = plane < 2

    def along_z(moves):
        return [(CORES * a + c, CORES * b + c) for a, b in moves for c in range(CORES)]

    core_swap = [(i, i ^ 1) for i in range(8)]
    both = ("pair", "red")

    def everywhere(moves):
        full = list(moves) + [((3 - a, 3 - g), (3 - b, 3 - h)) for (a, g), (b, h) in moves]
        return [((CORES * a + c) * 4 + g, (CORES * b + c) * 4 + h) for (a, g), (b, h) in full for c in range(CORES)]

    own_blocks = virt_blocks[0]
    from_planes = [own_blocks] + [
        lax.ppermute(own_blocks, "pair", along_z([(a, a ^ k) for a in range(4)])) for k in (1, 2, 3)
    ]
    tiles = three_center.reshape(aux, depth)
    *from_planes, tiles = lax.optimization_barrier((*from_planes, tiles))

    outer = lax.ppermute(tiles, "pair", along_z([(0, 1), (1, 0), (2, 3), (3, 2)]))
    inner = lax.ppermute(tiles, "pair", along_z([(1, 2), (2, 1)]))
    partner = lax.ppermute(tiles, "pair", core_swap)
    cuts = [(0, 128), (128, 256), (256, aux)]
    far_move = along_z([(0, 2), (3, 1)])
    far = [lax.ppermute(tiles[a:b], "pair", far_move) for a, b in cuts]

    mine = jnp.stack(from_planes)
    theirs = lax.ppermute(mine, "pair", core_swap)
    every = jnp.stack([mine, theirs])
    held = jnp.arange(virt_blocks.shape[1], dtype=jnp.int32)
    sources = jnp.arange(4, dtype=jnp.int32)
    flips = jnp.arange(CORES, dtype=jnp.int32)
    owner = CORES * (plane ^ sources)[None, :] + (core ^ flips)[:, None]
    block_id = (owner[:, :, None] * virt_blocks.shape[1] + held).reshape(-1)
    listed = virt_block[0, :, 0]
    block_hot = (listed[:, None] == block_id[None, :]).astype(BF16)
    picked = jnp.dot(block_hot, every.reshape(-1, area), preferred_element_type=F32).astype(BF16)
    wide = call(
        prep_body, shaped(ntiles, area, area), [picked.reshape(ntiles * BLK, BLK)], name="widen"
    )
    mixing = mixing_of(occ_src, occ_block, occ_blocks, ntiles)
    mix = mixing.transpose(0, 2, 1, 3).reshape(ntiles * BLK, ntiles * BLK)

    def scratch_for(count):
        return [pltpu.VMEM((BLK, ntiles * BLK, count), BF16), pltpu.VMEM((ntiles, area, count), BF16)]

    def kernel_of(rows, name):
        count = rows.shape[0]
        return call(
            k_body, shaped(depth, count), [rows, mix, wide], scratch_for(count),
            flops=2 * count * depth * 3 * area, name=name,
        )

    k_own = kernel_of(tiles, "k_own")
    k_outer = kernel_of(outer, "k_outer")
    k_inner = kernel_of(inner, "k_inner")
    outer_partner = lax.ppermute(outer, "pair", core_swap)

    place = jnp.where(near_end, red, 3 - red)
    at_hub = (plane == 1) | (plane == 2)
    hub_term = jnp.array([1, 0, 2, -1], jnp.int32)
    end_term = jnp.array([0, 1, -1, -1], jnp.int32)
    term_of = jnp.where(at_hub, hub_term, end_term)
    chosen = [term_of[place]] + [term_of[place ^ d] for d in (1, 2, 3)] + [jnp.int32(-1)]
    picks = jnp.stack([chosen[0]] + [jnp.where(x >= 0, x, 3) for x in chosen[1:]]).astype(jnp.int32)
    flops = 2 * 8 * aux * aux * depth
    own_early, *sent = call(
        early_body,
        [shaped(2 * aux, aux, dtype=F32)] + [shaped(2 * aux, aux)] * 4,
        [picks, tiles, partner, outer, outer_partner, k_own, k_outer, k_inner],
        [pltpu.VMEM((4, 2 * aux, aux), F32)],
        smem=1, flops=flops, name="early",
    )
    arrived = []
    for d, value in zip((1, 2, 3), sent):
        moves = [((1, g), (1, g ^ d)) for g in range(4) if g ^ d != 3]
        moves += [((0, g), (0, g ^ d)) for g in range(4) if g ^ d < 2]
        moves += [((1, 3 ^ d), (0, 2))]
        arrived.append(lax.ppermute(value, both, everywhere(moves)))
    arrived.append(lax.ppermute(sent[3], both, everywhere([((1, 3), (0, 2))])))

    late_place = place[None].astype(jnp.int32)
    late_moves = [
        [((1, 0), (1, 3)), ((1, 1), (0, 3))],
        [((1, 1), (1, 3)), ((1, 2), (0, 3))],
        [((1, 2), (1, 3)), ((1, 0), (0, 3))],
        [((1, 3), (0, 3))],
    ]
    late_terms = []
    for (a, b), rows in zip(cuts, far):
        count = b - a
        own_late, *late_sent = call(
            late_body,
            [shaped(2 * aux, count, dtype=F32)] + [shaped(2 * aux, count)] * 4,
            [late_place, rows, tiles, partner, outer, outer_partner, mix, wide],
            [pltpu.VMEM((depth, count), BF16)] + scratch_for(count),
            smem=1, flops=2 * 4 * aux * count * depth, name=f"late_{a}",
        )
        at_plane = jnp.where(at_hub, own_late, 0.0)
        for moves, value in zip(late_moves, late_sent):
            at_plane = at_plane + lax.ppermute(value, both, everywhere(moves)).astype(F32)
        late_terms.append(at_plane)

    total = own_early
    for value in arrived:
        total = total + value.astype(F32)
    total = total + jnp.concatenate(late_terms, axis=1)
    other = lax.ppermute(total[aux:], "pair", core_swap)
    kept = total[:aux]
    return jnp.where(
        core == 0, jnp.concatenate([kept, other], axis=1), jnp.concatenate([other, kept], axis=1)
    )


def solution(mesh):
    placed = (
        P("pair", "red", None),
        P("red", None),
        P("red", None),
        P("red", None),
        P("red", None, None),
        P("red", "pair", None),
    )
    small = mesh.shape["pair"] == 8 and mesh.shape["red"] == 4
    return jax.shard_map(
        hub_plan if small else gather_plan,
        mesh=mesh, in_specs=placed, out_specs=P("pair", "red"), check_vma=False,
    )
```

time: 185 us -> 139 us (0.75)
  the two profiles are of different devices: /device:TPU:7 before, /device:TPU:5 now
where the time goes in v1:
time: 139 us; the launch traced here: 138 us
  starting transfers between devices  49.7 us (36%)
  waiting for transfers between devices  40.6 us (29%)
  Pallas kernels  27.1 us (19%)
  local copies, waits for them, and re-layouts  11.1 us (8%)
  between operations  4.39 us (3%)
  other arithmetic  3.94 us (3%)
    pallas_call x8, Pallas kernels, call(): pl.pallas_call(body, out_shape=outs, in_specs=[pl.BlockSpec(memory_space=...  27.1 us
    ppermute x3, waiting for transfers between devices, hub_plan(): arrived.append(lax.ppermute(value, both, everywhere(moves)))  18.5 us
    ppermute x1, starting transfers between devices, hub_plan(): other = lax.ppermute(total[aux:], 'pair', core_swap)  15.4 us
    ppermute x1, waiting for transfers between devices, hub_plan(): lax.ppermute(tiles, 'pair', along_z([(0, 1), (1, 0), (2, 3), (3, 2)]))  13.4 us
    ppermute x12, starting transfers between devices, hub_plan(): lax.ppermute(value, both, everywhere(moves)).astype(F32)  8.22 us
    ppermute x3, starting transfers between devices, hub_plan(): arrived.append(lax.ppermute(value, both, everywhere(moves)))  7.17 us
    ppermute x3, starting transfers between devices, hub_plan(): far = [lax.ppermute(tiles[a:b], 'pair', far_move) for a, b in cuts]  7.01 us
    ppermute x3, waiting for transfers between devices, hub_plan(): far = [lax.ppermute(tiles[a:b], 'pair', far_move) for a, b in cuts]  5.75 us
  transfers between devices with their start and end apart: 28, of which 8 were waited for; matrix products, arithmetic and copies ran while one was open for 9% of the time, Pallas kernels for 20%

profile of v1, /device:TPU:5, one launch (start us, length us, event | category | flops | bytes accessed | tf_op | source)
XLA Modules:
  0.0 138.0 jit_solution(17226329110896447619)
XLA Ops:
  0.0 3.3 %collective-permute-start.2 = (bf16[2,256]{1,0:T(2,128)(2,1)}, bf16[2,256]{1,0:T(2,128)(2,1)S(1)}, u32[]{:S(2)}, u32[]{:S(2)}) collective-permute-start(bf16[2,256]{1,0:T(2,128)(2,1)} %bitcast.41), channel_id=1, source_target_pairs={{0,24},{4,28},{8,16},{12,20},{16,8},{20,12},{24,0},{28,4},{1,25},{... | collective-permute-start | bytes 3080 | tf_op jit(solution)/shard_map/ppermute | solution.py:162
  3.7 1.7 %copy.11 = bf16[36,8,8,256]{3,1,2,0:T(8,128)(2,1)S(1)} copy(bf16[36,8,8,256]{3,2,1,0:T(8,128)(2,1)} %bitcast.38) | data formatting | bytes 2359296
  5.4 1.4 %collective-permute-done.1 = bf16[2,256]{1,0:T(2,128)(2,1)S(1)} collective-permute-done((bf16[2,256]{1,0:T(2,128)(2,1)}, bf16[2,256]{1,0:T(2,128)(2,1)S(1)}, u32[]{:S(2)}, u32[]{:S(2)}) %collective-permute-start.1) | collective-permute-done | bytes 1056 | tf_op jit(solution)/shard_map/ppermute | solution.py:162
  15.3 1.7 %collective-permute-start.7 = (bf16[288,2048]{1,0:T(8,128)(2,1)S(1)}, bf16[288,2048]{1,0:T(8,128)(2,1)}, u32[]{:S(2)}, u32[]{:S(2)}) collective-permute-start(bf16[288,2048]{1,0:T(8,128)(2,1)S(1)} %bitcast.29), channel_id=1, source_target_pairs={{8,16},{12,20},{16,8},{20,12},{9,17},{13,21},{17,9},{21,13},{10,18... | collective-permute-start | bytes 3538952 | tf_op jit(solution)/shard_map/ppermute | solution.py:168
  17.0 2.1 %collective-permute-start.3 = (bf16[288,2048]{1,0:T(8,128)(2,1)S(1)}, bf16[288,2048]{1,0:T(8,128)(2,1)S(1)}, u32[]{:S(2)}, u32[]{:S(2)}) collective-permute-start(bf16[288,2048]{1,0:T(8,128)(2,1)S(1)} %bitcast.30), channel_id=1, source_target_pairs={{0,4},{4,0},{8,12},{12,8},{16,20},{20,16},{24,28},{28,24},{1,5},{5... | collective-permute-start | bytes 3538952 | tf_op jit(solution)/shard_map/ppermute | solution.py:169
  19.9 13.4 %collective-permute-done.4.tile_ref.e_ref = bf16[288,2048]{1,0:T(8,128)(2,1)S(1)} collective-permute-done((bf16[288,2048]{1,0:T(8,128)(2,1)S(1)}, bf16[288,2048]{1,0:T(8,128)(2,1)S(1)}, u32[]{:S(2)}, u32[]{:S(2)}) %collective-permute-start.4) | collective-permute-done | bytes 1179680 | tf_op jit(solution)/shard_map/ppermute | solution.py:167
  33.3 3.0 %collective-permute-start.5 = (bf16[288,2048]{1,0:T(8,128)(2,1)S(1)}, bf16[288,2048]{1,0:T(8,128)(2,1)}, u32[]{:S(2)}, u32[]{:S(2)}) collective-permute-start(bf16[288,2048]{1,0:T(8,128)(2,1)S(1)} %collective-permute-done.4.tile_ref.e_ref), channel_id=1, source_target_pairs={{0,4},{4,0},{8,12},{12,8},{16,20},{20,16},{24,28},{28,24},{1,5},{5... | collective-permute-start | bytes 3538952 | tf_op jit(solution)/shard_map/ppermute | solution.py:204
  38.7 3.6 %collective-permute-start.12 = (bf16[128,2048]{1,0:T(8,128)(2,1)}, bf16[128,2048]{1,0:T(8,128)(2,1)}, u32[]{:S(2)}, u32[]{:S(2)}) collective-permute-start(bf16[128,2048]{1,0:T(8,128)(2,1)} %get-tuple-element.55), channel_id=1, source_target_pairs={{0,16},{4,20},{24,8},{28,12},{1,17},{5,21},{25,9},{29,13},{2,18},{... | collective-permute-start | bytes 1572872 | tf_op jit(solution)/shard_map/ppermute | solution.py:172
  42.3 2.1 %collective-permute-start.17 = (bf16[128,2048]{1,0:T(8,128)(2,1)}, bf16[128,2048]{1,0:T(8,128)(2,1)}, u32[]{:S(2)}, u32[]{:S(2)}) collective-permute-start(bf16[128,2048]{1,0:T(8,128)(2,1)} %get-tuple-element.56), channel_id=1, source_target_pairs={{0,16},{4,20},{24,8},{28,12},{1,17},{5,21},{25,9},{29,13},{2,18},{... | collective-permute-start | bytes 1572872 | tf_op jit(solution)/shard_map/ppermute | solution.py:172
  50.4 1.9 %k_own.1.ko_ref = bf16[2048,288]{1,0:T(8,128)(2,1)S(1)} custom-call(bf16[288,2048]{1,0:T(8,128)(2,1)S(1)} %bitcast.33, bf16[128,128]{1,0:T(8,128)(2,1)S(1)} %copy-done.1, bf16[8,256,256]{2,1,0:T(8,128)(2,1)S(1)} %widen.1.wide_ref), custom_call_target="tpu_custom_call" | custom-call | flops 905969664 | bytes 2260992 | tf_op jit(solution)/shard_map/k_own/pallas_call | solution.py:124
  52.3 1.9 %k_outer.1.ke_ref = bf16[2048,288]{1,0:T(8,128)(2,1)S(1)} custom-call(bf16[288,2048]{1,0:T(8,128)(2,1)S(1)} %collective-permute-done.4.tile_ref.e_ref, bf16[128,128]{1,0:T(8,128)(2,1)S(1)} %copy-done.1, bf16[8,256,256]{2,1,0:T(8,128)(2,1)S(1)} %widen.1.wide_ref), custom_call_target="tpu_custom_call" | custom-call | flops 905969664 | bytes 2260992 | tf_op jit(solution)/shard_map/k_outer/pallas_call | solution.py:124
  55.5 3.2 %k_inner.1.kb_ref = bf16[2048,288]{1,0:T(8,128)(2,1)S(1)} custom-call(bf16[288,2048]{1,0:T(8,128)(2,1)} %collective-permute-done.7.tile_ref, bf16[128,128]{1,0:T(8,128)(2,1)S(1)} %copy-done.1, bf16[8,256,256]{2,1,0:T(8,128)(2,1)S(1)} %widen.1.wide_ref), custom_call_target="tpu_custom_call" | custom-call | flops 905969664 | bytes 2260992 | tf_op jit(solution)/shard_map/k_inner/pallas_call | solution.py:124
  58.7 5.7 %collective-permute-done.17.c_ref = bf16[128,2048]{1,0:T(8,128)(2,1)} collective-permute-done((bf16[128,2048]{1,0:T(8,128)(2,1)}, bf16[128,2048]{1,0:T(8,128)(2,1)}, u32[]{:S(2)}, u32[]{:S(2)}) %collective-permute-start.17) | collective-permute-done | bytes 524320 | tf_op jit(solution)/shard_map/ppermute | solution.py:172
  64.5 3.8 %late_128.1 = (f32[576,128]{1,0:T(8,128)S(1)}, bf16[576,128]{1,0:T(8,128)(2,1)S(1)}, bf16[576,128]{1,0:T(8,128)(2,1)S(1)}, bf16[576,128]{1,0:T(8,128)(2,1)S(1)}, bf16[576,128]{1,0:T(8,128)(2,1)S(1)}) custom-call(s32[1]{0:T(128)} %bitcast.16.pick_ref, bf16[128,2048]{1,0:T(8,128)(2,1)} %collective-permute-done.17.c_ref, bf16[288,2048]{1,0:T(8,128)(2,1)S(1)} %bitcast.34, ...), custom_call_target="tpu_custom_call" | custom-call | flops 603979776 | bytes 6324228 | tf_op jit(solution)/shard_map/late_128/pallas_call | solution.py:124
  69.8 3.6 %late_256.1 = (f32[576,32]{1,0:T(8,128)S(1)}, bf16[576,32]{1,0:T(8,128)(2,1)S(1)}, bf16[576,32]{1,0:T(8,128)(2,1)S(1)}, bf16[576,32]{1,0:T(8,128)(2,1)S(1)}, bf16[576,32]{1,0:T(8,128)(2,1)S(1)}) custom-call(s32[1]{0:T(128)} %bitcast.16.pick_ref, bf16[32,2048]{1,0:T(8,128)(2,1)S(1)} %collective-permute-done.22.c_ref, bf16[288,2048]{1,0:T(8,128)(2,1)S(1)} %bitcast.35, ...), custom_call_target="tpu_custom_call" | custom-call | flops 150994944 | bytes 5931012 | tf_op jit(solution)/shard_map/late_256/pallas_call | solution.py:124
  74.7 8.1 %early.1 = (f32[576,288]{1,0:T(8,128)S(1)}, bf16[576,288]{1,0:T(8,128)(2,1)S(1)}, bf16[576,288]{1,0:T(8,128)(2,1)S(1)}, bf16[576,288]{1,0:T(8,128)(2,1)S(1)}, bf16[576,288]{1,0:T(8,128)(2,1)S(1)}) custom-call(s32[5]{0:T(128)S(1)} %stack.40.pick_ref, bf16[288,2048]{1,0:T(8,128)(2,1)S(1)} %bitcast.36, bf16[288,2048]{1,0:T(8,128)(2,1)S(1)} %collective-permute-done.3.p_ref, ...), custom_call_target="tpu_custom_call" | custom-call | flops 2717908992 | bytes 8257556 | tf_op jit(solution)/shard_map/early/pallas_call | solution.py:124
  84.2 3.8 %late_0.1 = (f32[576,128]{1,0:T(8,128)S(1)}, bf16[576,128]{1,0:T(8,128)(2,1)S(1)}, bf16[576,128]{1,0:T(8,128)(2,1)S(1)}, bf16[576,128]{1,0:T(8,128)(2,1)S(1)}, bf16[576,128]{1,0:T(8,128)(2,1)S(1)}) custom-call(s32[1]{0:T(128)} %bitcast.16.pick_ref, bf16[128,2048]{1,0:T(8,128)(2,1)} %collective-permute-done.12.c_ref, bf16[288,2048]{1,0:T(8,128)(2,1)S(1)} %bitcast.37, ...), custom_call_target="tpu_custom_call" | custom-call | flops 603979776 | bytes 6324228 | tf_op jit(solution)/shard_map/late_0/pallas_call | solution.py:124
  93.6 4.0 %collective-permute-start.9 = (bf16[576,288]{1,0:T(8,128)(2,1)S(1)}, bf16[576,288]{1,0:T(8,128)(2,1)S(1)}, u32[]{:S(2)}, u32[]{:S(2)}) collective-permute-start(bf16[576,288]{1,0:T(8,128)(2,1)S(1)} %get-tuple-element.37), channel_id=1, source_target_pairs={{8,10},{12,14},{10,8},{14,12},{11,9},{15,13},{2,0},{6,4},{3,1},{7,... | collective-permute-start | bytes 995336 | tf_op jit(solution)/shard_map/ppermute | solution.py:226
  97.6 1.9 %collective-permute-start.10 = (bf16[576,288]{1,0:T(8,128)(2,1)S(1)}, bf16[576,288]{1,0:T(8,128)(2,1)S(1)}, u32[]{:S(2)}, u32[]{:S(2)}) collective-permute-start(bf16[576,288]{1,0:T(8,128)(2,1)S(1)} %get-tuple-element.38), channel_id=1, source_target_pairs={{9,10},{13,14},{10,9},{14,13},{11,8},{15,12},{2,1},{6,5},{3,0},{7,... | collective-permute-start | bytes 995336 | tf_op jit(solution)/shard_map/ppermute | solution.py:226
  101.0 10.0 %collective-permute-done.8 = bf16[576,288]{1,0:T(8,128)(2,1)S(1)} collective-permute-done((bf16[576,288]{1,0:T(8,128)(2,1)S(1)}, bf16[576,288]{1,0:T(8,128)(2,1)S(1)}, u32[]{:S(2)}, u32[]{:S(2)}) %collective-permute-start.8) | collective-permute-done | bytes 331808 | tf_op jit(solution)/shard_map/ppermute | solution.py:226
  111.0 5.7 %collective-permute-done.9 = bf16[576,288]{1,0:T(8,128)(2,1)S(1)} collective-permute-done((bf16[576,288]{1,0:T(8,128)(2,1)S(1)}, bf16[576,288]{1,0:T(8,128)(2,1)S(1)}, u32[]{:S(2)}, u32[]{:S(2)}) %collective-permute-start.9) | collective-permute-done | bytes 331808 | tf_op jit(solution)/shard_map/ppermute | solution.py:226
  116.7 2.8 %collective-permute-done.10 = bf16[576,288]{1,0:T(8,128)(2,1)S(1)} collective-permute-done((bf16[576,288]{1,0:T(8,128)(2,1)S(1)}, bf16[576,288]{1,0:T(8,128)(2,1)S(1)}, u32[]{:S(2)}, u32[]{:S(2)}) %collective-permute-start.10) | collective-permute-done | bytes 331808 | tf_op jit(solution)/shard_map/ppermute | solution.py:226
  120.0 15.4 %collective-permute-start.27 = (f32[288,288]{1,0:T(8,128)S(1)}, f32[288,288]{1,0:T(8,128)S(1)}, u32[]{:S(2)}, u32[]{:S(2)}) collective-permute-start(f32[288,288]{1,0:T(8,128)S(1)} %get-tuple-element.58), channel_id=1, source_target_pairs={{0,4},{4,0},{8,12},{12,8},{16,20},{20,16},{24,28},{28,24},{1,5},{5... | collective-permute-start | bytes 995336 | tf_op jit(solution)/shard_map/ppermute | solution.py:255
  135.4 1.4 %collective-permute-done.27 = f32[288,288]{1,0:T(8,128)S(1)} collective-permute-done((f32[288,288]{1,0:T(8,128)S(1)}, f32[288,288]{1,0:T(8,128)S(1)}, u32[]{:S(2)}, u32[]{:S(2)}) %collective-permute-start.27) | collective-permute-done | bytes 331808 | tf_op jit(solution)/shard_map/ppermute | solution.py:255
  (97 shorter events, 28.1 us)
Async XLA Ops:
  0.0 5.4 %collective-permute-start.2 = (bf16[2,256]{1,0:T(2,128)(2,1)}, bf16[2,256]{1,0:T(2,128)(2,1)S(1)}, u32[]{:S(2)}, u32[]{:S(2)}) collective-permute-start(bf16[2,256]{1,0:T(2,128)(2,1)} %bitcast.41), channel_id=1, source_target_pairs={{0,24},{4,28},{8,16},{12,20},{16,8},{20,12},{24,0},{28,4},{1,25},{... | collective-permute-start | bytes 3080 | tf_op jit(solution)/shard_map/ppermute | solution.py:162
  7.9 25.4 %collective-permute-start.4 = (bf16[288,2048]{1,0:T(8,128)(2,1)S(1)}, bf16[288,2048]{1,0:T(8,128)(2,1)S(1)}, u32[]{:S(2)}, u32[]{:S(2)}) collective-permute-start(bf16[288,2048]{1,0:T(8,128)(2,1)S(1)} %bitcast.28), channel_id=1, source_target_pairs={{0,8},{4,12},{8,0},{12,4},{16,24},{20,28},{24,16},{28,20},{1,9},{5... | collective-permute-start | bytes 3538952 | tf_op jit(solution)/shard_map/ppermute | solution.py:167
  15.3 38.9 %collective-permute-start.7 = (bf16[288,2048]{1,0:T(8,128)(2,1)S(1)}, bf16[288,2048]{1,0:T(8,128)(2,1)}, u32[]{:S(2)}, u32[]{:S(2)}) collective-permute-start(bf16[288,2048]{1,0:T(8,128)(2,1)S(1)} %bitcast.29), channel_id=1, source_target_pairs={{8,16},{12,20},{16,8},{20,12},{9,17},{13,21},{17,9},{21,13},{10,18... | collective-permute-start | bytes 3538952 | tf_op jit(solution)/shard_map/ppermute | solution.py:168
  17.0 47.4 %collective-permute-start.3 = (bf16[288,2048]{1,0:T(8,128)(2,1)S(1)}, bf16[288,2048]{1,0:T(8,128)(2,1)S(1)}, u32[]{:S(2)}, u32[]{:S(2)}) collective-permute-start(bf16[288,2048]{1,0:T(8,128)(2,1)S(1)} %bitcast.30), channel_id=1, source_target_pairs={{0,4},{4,0},{8,12},{12,8},{16,20},{20,16},{24,28},{28,24},{1,5},{5... | collective-permute-start | bytes 3538952 | tf_op jit(solution)/shard_map/ppermute | solution.py:169
  19.8 22.5 %collective-permute-start.6 = (bf16[4,2,256]{2,1,0:T(2,128)(2,1)S(1)}, bf16[4,2,256]{2,1,0:T(2,128)(2,1)S(1)}, u32[]{:S(2)}, u32[]{:S(2)}) collective-permute-start(bf16[4,2,256]{2,1,0:T(2,128)(2,1)S(1)} %pad_maximum_fusion.1), channel_id=1, source_target_pairs={{0,4},{4,0},{8,12},{12,8},{16,20},{20,16},{24,28},{28,24},{1,5},{5... | collective-permute-start | bytes 12296 | tf_op jit(solution)/shard_map/ppermute | solution.py:175
  33.3 31.2 %collective-permute-start.5 = (bf16[288,2048]{1,0:T(8,128)(2,1)S(1)}, bf16[288,2048]{1,0:T(8,128)(2,1)}, u32[]{:S(2)}, u32[]{:S(2)}) collective-permute-start(bf16[288,2048]{1,0:T(8,128)(2,1)S(1)} %collective-permute-done.4.tile_ref.e_ref), channel_id=1, source_target_pairs={{0,4},{4,0},{8,12},{12,8},{16,20},{20,16},{24,28},{28,24},{1,5},{5... | collective-permute-start | bytes 3538952 | tf_op jit(solution)/shard_map/ppermute | solution.py:204
  38.7 44.2 %collective-permute-start.12 = (bf16[128,2048]{1,0:T(8,128)(2,1)}, bf16[128,2048]{1,0:T(8,128)(2,1)}, u32[]{:S(2)}, u32[]{:S(2)}) collective-permute-start(bf16[128,2048]{1,0:T(8,128)(2,1)} %get-tuple-element.55), channel_id=1, source_target_pairs={{0,16},{4,20},{24,8},{28,12},{1,17},{5,21},{25,9},{29,13},{2,18},{... | collective-permute-start | bytes 1572872 | tf_op jit(solution)/shard_map/ppermute | solution.py:172
  42.3 22.1 %collective-permute-start.17 = (bf16[128,2048]{1,0:T(8,128)(2,1)}, bf16[128,2048]{1,0:T(8,128)(2,1)}, u32[]{:S(2)}, u32[]{:S(2)}) collective-permute-start(bf16[128,2048]{1,0:T(8,128)(2,1)} %get-tuple-element.56), channel_id=1, source_target_pairs={{0,16},{4,20},{24,8},{28,12},{1,17},{5,21},{25,9},{29,13},{2,18},{... | collective-permute-start | bytes 1572872 | tf_op jit(solution)/shard_map/ppermute | solution.py:172
  54.2 15.6 %collective-permute-start.22 = (bf16[32,2048]{1,0:T(8,128)(2,1)S(1)}, bf16[32,2048]{1,0:T(8,128)(2,1)S(1)}, u32[]{:S(2)}, u32[]{:S(2)}) collective-permute-start(bf16[32,2048]{1,0:T(8,128)(2,1)S(1)} %copy-done.6), channel_id=1, source_target_pairs={{0,16},{4,20},{24,8},{28,12},{1,17},{5,21},{25,9},{29,13},{2,18},{... | collective-permute-start | bytes 393224 | tf_op jit(solution)/shard_map/ppermute | solution.py:172
  68.3 21.8 %collective-permute-start.18 = (bf16[576,128]{1,0:T(8,128)(2,1)S(1)}, bf16[576,128]{1,0:T(8,128)(2,1)S(1)}, u32[]{:S(2)}, u32[]{:S(2)}) collective-permute-start(bf16[576,128]{1,0:T(8,128)(2,1)S(1)} %get-tuple-element.46), channel_id=1, source_target_pairs={{8,11},{12,15},{9,3},{13,7},{19,16},{23,20},{18,24},{22,28}} | collective-permute-start | bytes 442376 | tf_op jit(solution)/shard_map/ppermute | solution.py:248
  68.9 21.8 %collective-permute-start.19 = (bf16[576,128]{1,0:T(8,128)(2,1)S(1)}, bf16[576,128]{1,0:T(8,128)(2,1)S(1)}, u32[]{:S(2)}, u32[]{:S(2)}) collective-permute-start(bf16[576,128]{1,0:T(8,128)(2,1)S(1)} %get-tuple-element.47), channel_id=1, source_target_pairs={{9,11},{13,15},{10,3},{14,7},{18,16},{22,20},{17,24},{21,28}} | collective-permute-start | bytes 442376 | tf_op jit(solution)/shard_map/ppermute | solution.py:248
  73.4 10.2 %collective-permute-start.23 = (bf16[576,32]{1,0:T(8,128)(2,1)S(1)}, bf16[576,32]{1,0:T(8,128)(2,1)S(1)}, u32[]{:S(2)}, u32[]{:S(2)}) collective-permute-start(bf16[576,32]{1,0:T(8,128)(2,1)S(1)} %get-tuple-element.51), channel_id=1, source_target_pairs={{8,11},{12,15},{9,3},{13,7},{19,16},{23,20},{18,24},{22,28}} | collective-permute-start | bytes 110600 | tf_op jit(solution)/shard_map/ppermute | solution.py:248
  74.1 14.0 %collective-permute-start.24 = (bf16[576,32]{1,0:T(8,128)(2,1)S(1)}, bf16[576,32]{1,0:T(8,128)(2,1)S(1)}, u32[]{:S(2)}, u32[]{:S(2)}) collective-permute-start(bf16[576,32]{1,0:T(8,128)(2,1)S(1)} %get-tuple-element.52), channel_id=1, source_target_pairs={{9,11},{13,15},{10,3},{14,7},{18,16},{22,20},{17,24},{21,28}} | collective-permute-start | bytes 110600 | tf_op jit(solution)/shard_map/ppermute | solution.py:248
  82.9 5.8 %collective-permute-start.25 = (bf16[576,32]{1,0:T(8,128)(2,1)S(1)}, bf16[576,32]{1,0:T(8,128)(2,1)S(1)}, u32[]{:S(2)}, u32[]{:S(2)}) collective-permute-start(bf16[576,32]{1,0:T(8,128)(2,1)S(1)} %get-tuple-element.53), channel_id=1, source_target_pairs={{10,11},{14,15},{8,3},{12,7},{17,16},{21,20},{19,24},{23,28}} | collective-permute-start | bytes 110600 | tf_op jit(solution)/shard_map/ppermute | solution.py:248
  83.6 5.8 %collective-permute-start.26 = (bf16[576,32]{1,0:T(8,128)(2,1)S(1)}, bf16[576,32]{1,0:T(8,128)(2,1)S(1)}, u32[]{:S(2)}, u32[]{:S(2)}) collective-permute-start(bf16[576,32]{1,0:T(8,128)(2,1)S(1)} %get-tuple-element.54), channel_id=1, source_target_pairs={{11,3},{15,7},{16,24},{20,28}} | collective-permute-start | bytes 110600 | tf_op jit(solution)/shard_map/ppermute | solution.py:248
  89.4 4.2 %collective-permute-start.13 = (bf16[576,128]{1,0:T(8,128)(2,1)S(1)}, bf16[576,128]{1,0:T(8,128)(2,1)S(1)}, u32[]{:S(2)}, u32[]{:S(2)}) collective-permute-start(bf16[576,128]{1,0:T(8,128)(2,1)S(1)} %get-tuple-element.41), channel_id=1, source_target_pairs={{8,11},{12,15},{9,3},{13,7},{19,16},{23,20},{18,24},{22,28}} | collective-permute-start | bytes 442376 | tf_op jit(solution)/shard_map/ppermute | solution.py:248
  90.1 7.4 %collective-permute-start.14 = (bf16[576,128]{1,0:T(8,128)(2,1)S(1)}, bf16[576,128]{1,0:T(8,128)(2,1)S(1)}, u32[]{:S(2)}, u32[]{:S(2)}) collective-permute-start(bf16[576,128]{1,0:T(8,128)(2,1)S(1)} %get-tuple-element.42), channel_id=1, source_target_pairs={{9,11},{13,15},{10,3},{14,7},{18,16},{22,20},{17,24},{21,28}} | collective-permute-start | bytes 442376 | tf_op jit(solution)/shard_map/ppermute | solution.py:248
  90.8 8.7 %collective-permute-start.15 = (bf16[576,128]{1,0:T(8,128)(2,1)S(1)}, bf16[576,128]{1,0:T(8,128)(2,1)S(1)}, u32[]{:S(2)}, u32[]{:S(2)}) collective-permute-start(bf16[576,128]{1,0:T(8,128)(2,1)S(1)} %get-tuple-element.43), channel_id=1, source_target_pairs={{10,11},{14,15},{8,3},{12,7},{17,16},{21,20},{19,24},{23,28}} | collective-permute-start | bytes 442376 | tf_op jit(solution)/shard_map/ppermute | solution.py:248
  91.6 9.3 %collective-permute-start.16 = (bf16[576,128]{1,0:T(8,128)(2,1)S(1)}, bf16[576,128]{1,0:T(8,128)(2,1)S(1)}, u32[]{:S(2)}, u32[]{:S(2)}) collective-permute-start(bf16[576,128]{1,0:T(8,128)(2,1)S(1)} %get-tuple-element.44), channel_id=1, source_target_pairs={{11,3},{15,7},{16,24},{20,28}} | collective-permute-start | bytes 442376 | tf_op jit(solution)/shard_map/ppermute | solution.py:248
  92.3 18.7 %collective-permute-start.8 = (bf16[576,288]{1,0:T(8,128)(2,1)S(1)}, bf16[576,288]{1,0:T(8,128)(2,1)S(1)}, u32[]{:S(2)}, u32[]{:S(2)}) collective-permute-start(bf16[576,288]{1,0:T(8,128)(2,1)S(1)} %get-tuple-element.36), channel_id=1, source_target_pairs={{8,9},{12,13},{9,8},{13,12},{11,10},{15,14},{0,1},{4,5},{1,0},{5,4... | collective-permute-start | bytes 995336 | tf_op jit(solution)/shard_map/ppermute | solution.py:226
  93.6 23.1 %collective-permute-start.9 = (bf16[576,288]{1,0:T(8,128)(2,1)S(1)}, bf16[576,288]{1,0:T(8,128)(2,1)S(1)}, u32[]{:S(2)}, u32[]{:S(2)}) collective-permute-start(bf16[576,288]{1,0:T(8,128)(2,1)S(1)} %get-tuple-element.37), channel_id=1, source_target_pairs={{8,10},{12,14},{10,8},{14,12},{11,9},{15,13},{2,0},{6,4},{3,1},{7,... | collective-permute-start | bytes 995336 | tf_op jit(solution)/shard_map/ppermute | solution.py:226
  97.6 22.0 %collective-permute-start.10 = (bf16[576,288]{1,0:T(8,128)(2,1)S(1)}, bf16[576,288]{1,0:T(8,128)(2,1)S(1)}, u32[]{:S(2)}, u32[]{:S(2)}) collective-permute-start(bf16[576,288]{1,0:T(8,128)(2,1)S(1)} %get-tuple-element.38), channel_id=1, source_target_pairs={{9,10},{13,14},{10,9},{14,13},{11,8},{15,12},{2,1},{6,5},{3,0},{7,... | collective-permute-start | bytes 995336 | tf_op jit(solution)/shard_map/ppermute | solution.py:226
  99.5 20.1 %collective-permute-start.11 = (bf16[576,288]{1,0:T(8,128)(2,1)S(1)}, bf16[576,288]{1,0:T(8,128)(2,1)S(1)}, u32[]{:S(2)}, u32[]{:S(2)}) collective-permute-start(bf16[576,288]{1,0:T(8,128)(2,1)S(1)} %get-tuple-element.39), channel_id=1, source_target_pairs={{11,2},{15,6},{16,25},{20,29}} | collective-permute-start | bytes 995336 | tf_op jit(solution)/shard_map/ppermute | solution.py:227
  120.0 16.9 %collective-permute-start.27 = (f32[288,288]{1,0:T(8,128)S(1)}, f32[288,288]{1,0:T(8,128)S(1)}, u32[]{:S(2)}, u32[]{:S(2)}) collective-permute-start(f32[288,288]{1,0:T(8,128)S(1)} %get-tuple-element.58), channel_id=1, source_target_pairs={{0,4},{4,0},{8,12},{12,8},{16,20},{20,16},{24,28},{28,24},{1,5},{5... | collective-permute-start | bytes 995336 | tf_op jit(solution)/shard_map/ppermute | solution.py:255
  (19 other events, 90.7 us)

commit v2 on v1

v2 whole, which is shorter than its diff:
```python
import functools

import jax
import jax.numpy as jnp
from jax import lax
from jax.experimental import pallas as pl
from jax.experimental.pallas import tpu as pltpu
from jax.sharding import PartitionSpec as P

BLK = 16
AREA = BLK * BLK
VMEM_BYTES = 24 * 1024 * 1024
CORES = 2
BF16 = jnp.bfloat16
F32 = jnp.float32


def mixing_of(occ_src, occ_block, occ_blocks, ntiles):
    nblocks = occ_blocks.shape[0]
    block_hot = (occ_block[:, :, None] == jnp.arange(nblocks, dtype=jnp.int32)).astype(BF16)
    picked = jnp.einsum("tsb,bk->tsk", block_hot, occ_blocks, preferred_element_type=F32).astype(BF16)
    source_hot = (occ_src[:, :, None] == jnp.arange(ntiles, dtype=jnp.int32)).astype(BF16)
    mixing = jnp.einsum("tsk,tsa->tka", source_hot, picked, preferred_element_type=F32).astype(BF16)
    return mixing.reshape(ntiles, ntiles, BLK, BLK)


def gather_plan(three_center, occ_src, occ_block, occ_blocks, virt_block, virt_blocks):
    aux_rows, ntiles, area = three_center.shape
    tpd = virt_block.shape[2]
    mixing = mixing_of(occ_src, occ_block, occ_blocks, ntiles)
    blocks = three_center.reshape(aux_rows, ntiles, BLK, BLK)
    half = jnp.einsum("tkml,pkln->ptmn", mixing, blocks, preferred_element_type=F32).astype(BF16)
    all_blocks = lax.all_gather(virt_blocks[0], "pair", axis=0, tiled=True)
    listed = virt_block[0].reshape(ntiles // tpd, tpd, tpd)
    block_hot = (listed[..., None] == jnp.arange(all_blocks.shape[0], dtype=jnp.int32)).astype(BF16)
    picked = jnp.einsum("oijb,bk->oijk", block_hot, all_blocks, preferred_element_type=F32).astype(BF16)
    picked = picked.reshape(ntiles // tpd, tpd, tpd, BLK, BLK)
    grouped = half.reshape(aux_rows, ntiles // tpd, tpd, BLK, BLK)
    kernel = jnp.einsum("pojml,oijln->poimn", grouped, picked, preferred_element_type=F32)
    kernel = kernel.reshape(aux_rows, ntiles, area).astype(BF16)
    piece = lax.all_gather(kernel, "pair", axis=0, tiled=True)
    partial_value = lax.dot_general(
        three_center.reshape(aux_rows, ntiles * area),
        piece.reshape(piece.shape[0], ntiles * area),
        (((1,), (1,)), ((), ())),
        preferred_element_type=F32,
    )
    return lax.psum_scatter(partial_value, "red", scatter_dimension=1, tiled=True)


def iota2(shape, dim):
    return lax.broadcasted_iota(jnp.int32, shape, dim)


def prep_body(src_ref, block_ref, listed_ref, blocks_ref, mine_ref, theirs_ref, mix_ref, wide_ref, density, held):
    nblocks = blocks_ref.shape[0]
    ntiles, listed_sources = src_ref.shape
    width = ntiles * BLK
    repeat = (iota2((nblocks * BLK, nblocks), 0) // BLK == iota2((nblocks * BLK, nblocks), 1)).astype(BF16)
    rows = jnp.dot(repeat, blocks_ref[...], preferred_element_type=F32)
    rows = jnp.where(iota2(rows.shape, 0) % BLK == iota2(rows.shape, 1) // BLK, rows, 0.0).astype(BF16)
    spread = (iota2((AREA, width), 0) % BLK == iota2((AREA, width), 1) % BLK).astype(BF16)
    density[...] = jnp.dot(rows, spread, preferred_element_type=F32).reshape(nblocks, BLK, width)
    column = iota2((BLK, width), 1) // BLK
    for t in range(ntiles):
        line = jnp.zeros((BLK, width), F32)
        for s in range(listed_sources):
            line = line + jnp.where(column == src_ref[t, s], density[block_ref[t, s]], 0.0)
        mix_ref[t * BLK:(t + 1) * BLK, :] = line.astype(BF16)

    pair = lax.axis_index("pair")
    plane, core = pair // CORES, pair % CORES
    planes, per_owner, _ = mine_ref.shape
    for k in range(planes):
        held[k * per_owner:(k + 1) * per_owner, :] = mine_ref[k].astype(F32)
        held[(planes + k) * per_owner:(planes + k + 1) * per_owner, :] = theirs_ref[k].astype(F32)
    pick = (iota2((AREA, AREA), 0) % BLK == iota2((AREA, AREA), 1) % BLK).astype(F32)
    place = (iota2((AREA, AREA), 0) // BLK == iota2((AREA, AREA), 1) // BLK).astype(BF16)
    same = iota2((AREA, AREA), 0) // BLK == iota2((AREA, AREA), 1) % BLK
    for t in range(ntiles):
        k, flip = plane ^ (t // CORES), core ^ (t % CORES)
        row = (flip * planes + k) * per_owner + listed_ref[0, t, 0] - t * per_owner
        chosen = (pick * held[pl.ds(row, 1), :]).astype(BF16)
        full = jnp.dot(chosen, place, preferred_element_type=F32)
        wide_ref[t] = jnp.where(same, full, 0.0).astype(BF16)


def kernel_rows(tile_ref, mix_ref, wide_ref, out_ref, mixed, halves):
    ntiles = wide_ref.shape[0]
    rows = iota2((AREA, AREA), 0)
    cols = iota2((AREA, AREA), 1)
    swap = ((rows % BLK == cols // BLK) & (rows // BLK == cols % BLK)).astype(BF16)
    for k in range(ntiles):
        turned = lax.dot_general(
            swap, tile_ref[:, k * AREA:(k + 1) * AREA], (((1,), (1,)), ((), ())), preferred_element_type=F32
        ).astype(BF16)
        for n in range(BLK):
            mixed[n, k * BLK:(k + 1) * BLK, :] = turned[n * BLK:(n + 1) * BLK, :]
    mix = mix_ref[...]
    for n in range(BLK):
        half = jnp.dot(mix, mixed[n], preferred_element_type=F32).astype(BF16)
        for t in range(ntiles):
            halves[t, n * BLK:(n + 1) * BLK, :] = half[t * BLK:(t + 1) * BLK, :]
    for t in range(ntiles):
        out_ref[t * AREA:(t + 1) * AREA, :] = jnp.dot(
            wide_ref[t], halves[t], preferred_element_type=F32
        ).astype(BF16)


def k_body(tile_ref, mix_ref, wide_ref, out_ref, mixed, halves):
    kernel_rows(tile_ref, mix_ref, wide_ref, out_ref, mixed, halves)


def place_of():
    plane, red = lax.axis_index("pair") // CORES, lax.axis_index("red")
    near = plane < 2
    return jnp.where(near, plane, 3 - plane), jnp.where(near, red, 3 - red)


def early_body(o_ref, p_ref, e_ref, f_ref, g_ref, ko_ref, ke_ref, kb_ref, own_ref, s1, s2, s3, s4, terms):
    aux = o_ref.shape[0]
    for at, right, lefts in (
        (0, ko_ref, (o_ref, p_ref)),
        (1, ke_ref, (o_ref, p_ref)),
        (2, kb_ref, (o_ref, p_ref)),
        (3, kb_ref, (e_ref, f_ref, g_ref)),
    ):
        right_value = right[...]
        row = 0
        for left in lefts:
            count = left.shape[0]
            terms[at, row:row + count, :] = jnp.dot(left[...], right_value, preferred_element_type=F32)
            row += count
    plane, red = place_of()

    def term_for(column):
        hub = jnp.where(column < 2, 1 - column, column)
        return jnp.where(plane == 1, hub, jnp.minimum(column, 1))

    mine = (plane == 1) & (red < 3) | (plane == 0) & (red < 2)
    own_ref[...] = jnp.where(mine, terms[term_for(red)], 0.0)
    for d, out in zip((1, 2, 3), (s1, s2, s3)):
        out[...] = terms[term_for(red ^ d)].astype(BF16)
    s4[...] = terms[3].astype(BF16)


def late_body(c_ref, o_ref, p_ref, e_ref, f_ref, g_ref, mix_ref, wide_ref, own_ref, s1, s2, s3, s4, near, kt, mixed, halves):
    aux = o_ref.shape[0]
    kernel_rows(c_ref, mix_ref, wide_ref, kt, mixed, halves)
    right = kt[...]
    plane, place = place_of()
    mine = (plane == 1) & (place == 3)
    half = aux // 2
    near_parts = [(o_ref, 0, aux), (p_ref, aux, aux)]
    far_parts = [(e_ref, 0, aux), (f_ref, aux, half), (g_ref, aux + half, half)]
    for left, row, count in near_parts:
        value = jnp.dot(left[...], right, preferred_element_type=F32)
        own_ref[row:row + count, :] = jnp.where(mine, value, 0.0)
        near[row:row + count, :] = value.astype(BF16)
    for left, row, count in far_parts:
        rows = slice(row, row + count)
        value = jnp.dot(left[...], right, preferred_element_type=F32).astype(BF16)
        for source, out in enumerate((s1, s2, s3)):
            out[rows, :] = jnp.where(place == source, near[rows, :], value)
        s4[rows, :] = value


def call(body, outs, ins, scratch=(), smem=0, flops=0, name=None, vmem=VMEM_BYTES):
    return pl.pallas_call(
        body,
        out_shape=outs,
        in_specs=[pl.BlockSpec(memory_space=pltpu.SMEM)] * smem
        + [pl.BlockSpec(memory_space=pltpu.VMEM)] * (len(ins) - smem),
        out_specs=jax.tree.map(lambda _: pl.BlockSpec(memory_space=pltpu.VMEM), outs),
        scratch_shapes=list(scratch),
        compiler_params=pltpu.CompilerParams(vmem_limit_bytes=vmem),
        cost_estimate=pl.CostEstimate(
            flops=1, transcendentals=0, bytes_accessed=1
        ),
        name=name,
    )(*ins)


def shaped(*shape, dtype=BF16):
    return jax.ShapeDtypeStruct(shape, dtype)


def hub_plan(three_center, occ_src, occ_block, occ_blocks, virt_block, virt_blocks):
    aux, ntiles, area = three_center.shape
    depth = ntiles * area
    core = lax.axis_index("pair") % CORES

    def along_z(moves):
        return [(CORES * a + c, CORES * b + c) for a, b in moves for c in range(CORES)]

    core_swap = [(i, i ^ 1) for i in range(8)]
    both = ("pair", "red")

    def everywhere(moves):
        full = list(moves) + [((3 - a, 3 - g), (3 - b, 3 - h)) for (a, g), (b, h) in moves]
        return [((CORES * a + c) * 4 + g, (CORES * b + c) * 4 + h) for (a, g), (b, h) in full for c in range(CORES)]

    after = lax.optimization_barrier

    def scratch_for(count):
        return [pltpu.VMEM((BLK, ntiles * BLK, count), BF16), pltpu.VMEM((ntiles, area, count), BF16)]

    def kernel_of(rows, mix, wide, name):
        count = rows.shape[0]
        return call(
            k_body, shaped(depth, count), [rows, mix, wide], scratch_for(count),
            flops=2 * count * depth * 3 * area, name=name,
        )

    from_planes = [virt_blocks] + [
        lax.ppermute(virt_blocks, "pair", along_z([(a, a ^ k) for a in range(4)])) for k in (1, 2, 3)
    ]
    tiles = three_center.reshape(aux, depth)
    *from_planes, tiles = after((*from_planes, tiles))
    inner = lax.ppermute(tiles, "pair", along_z([(1, 2), (2, 1)]))
    mine = jnp.concatenate(from_planes)
    theirs = lax.ppermute(mine, "pair", core_swap)
    partner = lax.ppermute(tiles, "pair", core_swap)
    theirs, tiles = after((theirs, tiles))
    outer = lax.ppermute(tiles, "pair", along_z([(0, 1), (1, 0), (2, 3), (3, 2)]))
    mix, wide = call(
        prep_body,
        [shaped(ntiles * BLK, ntiles * BLK), shaped(ntiles, area, area)],
        [occ_src, occ_block, virt_block, occ_blocks, mine, theirs],
        [pltpu.VMEM((occ_blocks.shape[0], BLK, ntiles * BLK), F32), pltpu.VMEM((16, area), F32)],
        smem=3, name="prep",
    )
    partner, wide, tiles = after((partner, wide, tiles))
    far = lax.ppermute(tiles, "pair", along_z([(0, 2), (3, 1)]))
    k_own = kernel_of(tiles, mix, wide, "k_own")
    outer, inner, k_own = after((outer, inner, k_own))

    outer_partner = [lax.ppermute(outer[at:at + aux // 2], "pair", core_swap) for at in (0, aux // 2)]
    k_outer = kernel_of(outer, mix, wide, "k_outer")
    k_inner = kernel_of(inner, mix, wide, "k_inner")
    own_early, *sent = call(
        early_body,
        [shaped(2 * aux, aux, dtype=F32)] + [shaped(2 * aux, aux)] * 4,
        [tiles, partner, outer, *outer_partner, k_own, k_outer, k_inner],
        [pltpu.VMEM((4, 2 * aux, aux), F32)],
        flops=2 * 8 * aux * aux * depth, name="early",
    )
    arrived = []
    for d, value in zip((1, 2, 3), sent):
        moves = [((1, g), (1, g ^ d)) for g in range(4) if g ^ d != 3]
        moves += [((0, g), (0, g ^ d)) for g in range(4) if g ^ d < 2]
        moves += [((1, 3 ^ d), (0, 2))]
        arrived.append(lax.ppermute(value, both, everywhere(moves)))
    arrived.append(lax.ppermute(sent[3], both, everywhere([((1, 3), (0, 2))])))

    far, own_early = after((far, own_early))
    own_late, *late_sent = call(
        late_body,
        [shaped(2 * aux, aux, dtype=F32)] + [shaped(2 * aux, aux)] * 4,
        [far, tiles, partner, outer, *outer_partner, mix, wide],
        [pltpu.VMEM((2 * aux, aux), BF16), pltpu.VMEM((depth, aux), BF16)] + scratch_for(aux),
        flops=2 * 4 * aux * aux * depth, name="late",
    )
    late_moves = [
        [((1, 0), (1, 3)), ((1, 1), (0, 3))],
        [((1, 1), (1, 3)), ((1, 2), (0, 3))],
        [((1, 2), (1, 3)), ((1, 0), (0, 3))],
        [((1, 3), (0, 3))],
    ]
    total = own_early
    for value in arrived:
        total = total + value.astype(F32)
    total, *late_sent = after((total, *late_sent))
    total = total + own_late
    for moves, value in zip(late_moves, late_sent):
        total = total + lax.ppermute(value, both, everywhere(moves)).astype(F32)

    other = lax.ppermute(total[aux:], "pair", core_swap)
    kept = total[:aux]
    return jnp.where(
        core == 0, jnp.concatenate([kept, other], axis=1), jnp.concatenate([other, kept], axis=1)
    )


def solution(mesh):
    placed = (
        P("pair", "red", None),
        P("red", None),
        P("red", None),
        P("red", None),
        P("red", None, None),
        P("red", "pair", None),
    )
    small = mesh.shape["pair"] == 8 and mesh.shape["red"] == 4
    return jax.shard_map(
        hub_plan if small else gather_plan,
        mesh=mesh, in_specs=placed, out_specs=P("pair", "red"), check_vma=False,
    )
```

time: 139 us -> 105 us (0.76)
  the two profiles are of different devices: /device:TPU:5 before, /device:TPU:7 now
where the time goes in v2:
time: 105 us
  waiting for transfers between devices  53.1 us (51%)
  starting transfers between devices  26.7 us (25%)
  Pallas kernels  18.1 us (17%)
  local copies, waits for them, and re-layouts  5.2 us (5%)
  other arithmetic  1.69 us (2%)
    ppermute x1, waiting for transfers between devices, hub_plan(): lax.ppermute(tiles, 'pair', along_z([(0, 1), (1, 0), (2, 3), (3, 2)]))  18.8 us
    pallas_call x6, Pallas kernels, call(): pl.pallas_call(body, out_shape=outs, in_specs=[pl.BlockSpec(memory_space=...  18.1 us
    ppermute x4, waiting for transfers between devices, hub_plan(): total = total + lax.ppermute(value, both, everywhere(moves)).astype(F32)  16.9 us
    ppermute x3, waiting for transfers between devices, hub_plan(): arrived.append(lax.ppermute(value, both, everywhere(moves)))  9.02 us
    ppermute x3, starting transfers between devices, hub_plan(): arrived.append(lax.ppermute(value, both, everywhere(moves)))  6.54 us
    ppermute x4, starting transfers between devices, hub_plan(): total = total + lax.ppermute(value, both, everywhere(moves)).astype(F32)  5.17 us
    unnamed x17, local copies, waits for them, and re-layouts  5.06 us
    ppermute x1, waiting for transfers between devices, hub_plan(): far = lax.ppermute(tiles, 'pair', along_z([(0, 2), (3, 1)]))  4.21 us
  transfers between devices with their start and end apart: 19, of which 8 were waited for; matrix products, arithmetic and copies ran while one was open for 2% of the time, Pallas kernels for 17%

profile of v2, /device:TPU:7, one launch (start us, length us, event | category | flops | bytes accessed | tf_op | source)
XLA Modules:
  0.0 104.9 jit_solution(4258389999678218358)
XLA Ops:
  0.0 1.3 %collective-permute-start = (bf16[1,2,256]{2,1,0:T(2,128)(2,1)}, bf16[1,2,256]{2,1,0:T(2,128)(2,1)S(1)}, u32[]{:S(2)}, u32[]{:S(2)}) collective-permute-start(bf16[1,2,256]{2,1,0:T(2,128)(2,1)} %param.11), channel_id=1, source_target_pairs={{0,8},{4,12},{8,0},{12,4},{16,24},{20,28},{24,16},{28,20},{1,9},{5... | collective-permute-start | bytes 3080 | tf_op jit(solution)/shard_map/ppermute | solution.py:216
  1.3 2.3 %collective-permute-start.1 = (bf16[1,2,256]{2,1,0:T(2,128)(2,1)}, bf16[1,2,256]{2,1,0:T(2,128)(2,1)S(1)}, u32[]{:S(2)}, u32[]{:S(2)}) collective-permute-start(bf16[1,2,256]{2,1,0:T(2,128)(2,1)} %param.11), channel_id=1, source_target_pairs={{0,16},{4,20},{8,24},{12,28},{16,0},{20,4},{24,8},{28,12},{1,17},{... | collective-permute-start | bytes 3080 | tf_op jit(solution)/shard_map/ppermute | solution.py:216
  3.6 1.6 %copy.8 = bf16[36,8,8,256]{3,1,2,0:T(8,128)(2,1)S(1)} copy(bf16[36,8,8,256]{3,2,1,0:T(8,128)(2,1)} %bitcast.9) | data formatting | bytes 2359296
  5.3 2.7 %collective-permute-done.2 = bf16[1,2,256]{2,1,0:T(2,128)(2,1)S(1)} collective-permute-done((bf16[1,2,256]{2,1,0:T(2,128)(2,1)}, bf16[1,2,256]{2,1,0:T(2,128)(2,1)S(1)}, u32[]{:S(2)}, u32[]{:S(2)}) %collective-permute-start.2) | collective-permute-done | bytes 1056 | tf_op jit(solution)/shard_map/ppermute | solution.py:216
  8.1 2.5 %collective-permute-start.4 = (bf16[4,2,256]{2,1,0:T(2,128)(2,1)S(1)}, bf16[4,2,256]{2,1,0:T(2,128)(2,1)S(1)}, u32[]{:S(2)}, u32[]{:S(2)}) collective-permute-start(bf16[4,2,256]{2,1,0:T(2,128)(2,1)S(1)} %constant_dynamic-update-slice_fusion.mine_ref), channel_id=1, source_target_pairs={{0,4},{4,0},{8,12},{12,8},{16,20},{20,16},{24,28},{28,24},{1,5},{5... | collective-permute-start | bytes 12296 | tf_op jit(solution)/shard_map/ppermute | solution.py:222
  10.6 1.7 %collective-permute-start.7 = (bf16[288,2048]{1,0:T(8,128)(2,1)S(1)}, bf16[288,2048]{1,0:T(8,128)(2,1)}, u32[]{:S(2)}, u32[]{:S(2)}) collective-permute-start(bf16[288,2048]{1,0:T(8,128)(2,1)S(1)} %bitcast.3), channel_id=1, source_target_pairs={{8,16},{12,20},{16,8},{20,12},{9,17},{13,21},{17,9},{21,13},{10,18... | collective-permute-start | bytes 3538952 | tf_op jit(solution)/shard_map/ppermute | solution.py:220
  15.7 1.4 %prep.1 = (bf16[128,128]{1,0:T(8,128)(2,1)S(1)}, bf16[8,256,256]{2,1,0:T(8,128)(2,1)S(1)}) custom-call(s32[8,8]{1,0:T(8,128)S(1)} %copy-done.1, s32[8,8]{1,0:T(8,128)S(1)} %copy-done.2, s32[1,8,1]{2,1,0:T(8,128)S(1)} %copy.7.listed_ref, bf16[16,256]{1,0:T(8,128)(2,1)S(1)} %copy-done, bf16[4,2,256]{2,1,0:T(2,128)(2,1)S(1)} %constant_dynamic-update-slice_fusion.mine_ref, ...), custom_call_target="tpu_custom_call" | custom-call | flops 1 | bytes 1 | tf_op jit(solution)/shard_map/prep/pallas_call | solution.py:169
  17.1 2.2 %collective-permute-start.5 = (bf16[288,2048]{1,0:T(8,128)(2,1)S(1)}, bf16[288,2048]{1,0:T(8,128)(2,1)S(1)}, u32[]{:S(2)}, u32[]{:S(2)}) collective-permute-start(bf16[288,2048]{1,0:T(8,128)(2,1)S(1)} %bitcast.5), channel_id=1, source_target_pairs={{0,16},{4,20},{24,8},{28,12},{1,17},{5,21},{25,9},{29,13},{2,18},{... | collective-permute-start | bytes 3538952 | tf_op jit(solution)/shard_map/ppermute | solution.py:234
  19.3 1.9 %k_own.1.ko_ref = bf16[2048,288]{1,0:T(8,128)(2,1)S(1)} custom-call(bf16[288,2048]{1,0:T(8,128)(2,1)S(1)} %bitcast.6, bf16[128,128]{1,0:T(8,128)(2,1)S(1)} %get-tuple-element.47.mix_ref, bf16[8,256,256]{2,1,0:T(8,128)(2,1)S(1)} %get-tuple-element.48.wide_ref), custom_call_target="tpu_custom_call" | custom-call | flops 1 | bytes 1 | tf_op jit(solution)/shard_map/k_own/pallas_call | solution.py:169
  21.2 18.8 %collective-permute-done.6.tile_ref.e_ref = bf16[288,2048]{1,0:T(8,128)(2,1)S(1)} collective-permute-done((bf16[288,2048]{1,0:T(8,128)(2,1)S(1)}, bf16[288,2048]{1,0:T(8,128)(2,1)S(1)}, u32[]{:S(2)}, u32[]{:S(2)}) %collective-permute-start.6) | collective-permute-done | bytes 1179680 | tf_op jit(solution)/shard_map/ppermute | solution.py:225
  40.1 1.3 %collective-permute-start.8 = (bf16[144,2048]{1,0:T(8,128)(2,1)S(1)}, bf16[144,2048]{1,0:T(8,128)(2,1)S(1)}, u32[]{:S(2)}, u32[]{:S(2)}) collective-permute-start(bf16[144,2048]{1,0:T(8,128)(2,1)S(1)} %get-tuple-element.70), channel_id=1, source_target_pairs={{0,4},{4,0},{8,12},{12,8},{16,20},{20,16},{24,28},{28,24},{1,5},{5... | collective-permute-start | bytes 1769480 | tf_op jit(solution)/shard_map/ppermute | solution.py:238
  41.5 1.9 %k_outer.1.ke_ref = bf16[2048,288]{1,0:T(8,128)(2,1)S(1)} custom-call(bf16[288,2048]{1,0:T(8,128)(2,1)S(1)} %collective-permute-done.6.tile_ref.e_ref, bf16[128,128]{1,0:T(8,128)(2,1)S(1)} %get-tuple-element.47.mix_ref, bf16[8,256,256]{2,1,0:T(8,128)(2,1)S(1)} %get-tuple-element.48.wide_ref), custom_call_target="tpu_custom_call" | custom-call | flops 1 | bytes 1 | tf_op jit(solution)/shard_map/k_outer/pallas_call | solution.py:169
  43.4 3.2 %k_inner.1.kb_ref = bf16[2048,288]{1,0:T(8,128)(2,1)S(1)} custom-call(bf16[288,2048]{1,0:T(8,128)(2,1)} %collective-permute-done.7.tile_ref, bf16[128,128]{1,0:T(8,128)(2,1)S(1)} %get-tuple-element.47.mix_ref, bf16[8,256,256]{2,1,0:T(8,128)(2,1)S(1)} %get-tuple-element.48.wide_ref), custom_call_target="tpu_custom_call" | custom-call | flops 1 | bytes 1 | tf_op jit(solution)/shard_map/k_inner/pallas_call | solution.py:169
  46.6 5.3 %early.1 = (f32[576,288]{1,0:T(8,128)S(1)}, bf16[576,288]{1,0:T(8,128)(2,1)S(1)}, bf16[576,288]{1,0:T(8,128)(2,1)S(1)}, bf16[576,288]{1,0:T(8,128)(2,1)S(1)}, bf16[576,288]{1,0:T(8,128)(2,1)S(1)}) custom-call(bf16[288,2048]{1,0:T(8,128)(2,1)S(1)} %bitcast.7, bf16[288,2048]{1,0:T(8,128)(2,1)S(1)} %collective-permute-done.3.p_ref, ...), custom_call_target="tpu_custom_call" | custom-call | flops 1 | bytes 1 | tf_op jit(solution)/shard_map/early/pallas_call | solution.py:169
  52.6 3.6 %collective-permute-start.11 = (bf16[576,288]{1,0:T(8,128)(2,1)S(1)}, bf16[576,288]{1,0:T(8,128)(2,1)S(1)}, u32[]{:S(2)}, u32[]{:S(2)}) collective-permute-start(bf16[576,288]{1,0:T(8,128)(2,1)S(1)} %get-tuple-element.55), channel_id=1, source_target_pairs={{8,10},{12,14},{10,8},{14,12},{11,9},{15,13},{2,0},{6,4},{3,1},{7,... | collective-permute-start | bytes 995336 | tf_op jit(solution)/shard_map/ppermute | solution.py:253
  56.3 2.2 %collective-permute-start.12 = (bf16[576,288]{1,0:T(8,128)(2,1)S(1)}, bf16[576,288]{1,0:T(8,128)(2,1)S(1)}, u32[]{:S(2)}, u32[]{:S(2)}) collective-permute-start(bf16[576,288]{1,0:T(8,128)(2,1)S(1)} %get-tuple-element.56), channel_id=1, source_target_pairs={{9,10},{13,14},{10,9},{14,13},{11,8},{15,12},{2,1},{6,5},{3,0},{7,... | collective-permute-start | bytes 995336 | tf_op jit(solution)/shard_map/ppermute | solution.py:253
  59.2 4.2 %collective-permute-done.5.c_ref = bf16[288,2048]{1,0:T(8,128)(2,1)S(1)} collective-permute-done((bf16[288,2048]{1,0:T(8,128)(2,1)S(1)}, bf16[288,2048]{1,0:T(8,128)(2,1)S(1)}, u32[]{:S(2)}, u32[]{:S(2)}) %collective-permute-start.5) | collective-permute-done | bytes 1179680 | tf_op jit(solution)/shard_map/ppermute | solution.py:234
  63.4 4.4 %late.1 = (f32[576,288]{1,0:T(8,128)S(1)}, bf16[576,288]{1,0:T(8,128)(2,1)S(1)}, bf16[576,288]{1,0:T(8,128)(2,1)S(1)}, bf16[576,288]{1,0:T(8,128)(2,1)S(1)}, bf16[576,288]{1,0:T(8,128)(2,1)S(1)}) custom-call(bf16[288,2048]{1,0:T(8,128)(2,1)S(1)} %collective-permute-done.5.c_ref, bf16[288,2048]{1,0:T(8,128)(2,1)S(1)} %bitcast.8, ...), custom_call_target="tpu_custom_call" | custom-call | flops 1 | bytes 1 | tf_op jit(solution)/shard_map/late/pallas_call | solution.py:169
  67.8 6.7 %collective-permute-done.11 = bf16[576,288]{1,0:T(8,128)(2,1)S(1)} collective-permute-done((bf16[576,288]{1,0:T(8,128)(2,1)S(1)}, bf16[576,288]{1,0:T(8,128)(2,1)S(1)}, u32[]{:S(2)}, u32[]{:S(2)}) %collective-permute-start.11) | collective-permute-done | bytes 331808 | tf_op jit(solution)/shard_map/ppermute | solution.py:253
  74.5 2.3 %collective-permute-done.12 = bf16[576,288]{1,0:T(8,128)(2,1)S(1)} collective-permute-done((bf16[576,288]{1,0:T(8,128)(2,1)S(1)}, bf16[576,288]{1,0:T(8,128)(2,1)S(1)}, u32[]{:S(2)}, u32[]{:S(2)}) %collective-permute-start.12) | collective-permute-done | bytes 331808 | tf_op jit(solution)/shard_map/ppermute | solution.py:253
  82.2 12.1 %collective-permute-done.14 = bf16[576,288]{1,0:T(8,128)(2,1)S(1)} collective-permute-done((bf16[576,288]{1,0:T(8,128)(2,1)S(1)}, bf16[576,288]{1,0:T(8,128)(2,1)S(1)}, u32[]{:S(2)}, u32[]{:S(2)}) %collective-permute-start.14) | collective-permute-done | bytes 331808 | tf_op jit(solution)/shard_map/ppermute | solution.py:276
  94.3 4.8 %collective-permute-done.16 = bf16[576,288]{1,0:T(8,128)(2,1)S(1)} collective-permute-done((bf16[576,288]{1,0:T(8,128)(2,1)S(1)}, bf16[576,288]{1,0:T(8,128)(2,1)S(1)}, u32[]{:S(2)}, u32[]{:S(2)}) %collective-permute-start.16) | collective-permute-done | bytes 331808 | tf_op jit(solution)/shard_map/ppermute | solution.py:276
  99.5 2.8 %collective-permute-start.18 = (f32[288,288]{1,0:T(8,128)S(1)}, f32[288,288]{1,0:T(8,128)S(1)}, u32[]{:S(2)}, u32[]{:S(2)}) collective-permute-start(f32[288,288]{1,0:T(8,128)S(1)} %get-tuple-element.72), channel_id=1, source_target_pairs={{0,4},{4,0},{8,12},{12,8},{16,20},{20,16},{24,28},{28,24},{1,5},{5... | collective-permute-start | bytes 995336 | tf_op jit(solution)/shard_map/ppermute | solution.py:278
  102.3 1.4 %collective-permute-done.18 = f32[288,288]{1,0:T(8,128)S(1)} collective-permute-done((f32[288,288]{1,0:T(8,128)S(1)}, f32[288,288]{1,0:T(8,128)S(1)}, u32[]{:S(2)}, u32[]{:S(2)}) %collective-permute-start.18) | collective-permute-done | bytes 331808 | tf_op jit(solution)/shard_map/ppermute | solution.py:278
  (43 shorter events, 12.0 us)
Async XLA Ops:
  0.0 5.3 %collective-permute-start = (bf16[1,2,256]{2,1,0:T(2,128)(2,1)}, bf16[1,2,256]{2,1,0:T(2,128)(2,1)S(1)}, u32[]{:S(2)}, u32[]{:S(2)}) collective-permute-start(bf16[1,2,256]{2,1,0:T(2,128)(2,1)} %param.11), channel_id=1, source_target_pairs={{0,8},{4,12},{8,0},{12,4},{16,24},{20,28},{24,16},{28,20},{1,9},{5... | collective-permute-start | bytes 3080 | tf_op jit(solution)/shard_map/ppermute | solution.py:216
  1.3 4.0 %collective-permute-start.1 = (bf16[1,2,256]{2,1,0:T(2,128)(2,1)}, bf16[1,2,256]{2,1,0:T(2,128)(2,1)S(1)}, u32[]{:S(2)}, u32[]{:S(2)}) collective-permute-start(bf16[1,2,256]{2,1,0:T(2,128)(2,1)} %param.11), channel_id=1, source_target_pairs={{0,16},{4,20},{8,24},{12,28},{16,0},{20,4},{24,8},{28,12},{1,17},{... | collective-permute-start | bytes 3080 | tf_op jit(solution)/shard_map/ppermute | solution.py:216
  3.6 4.4 %collective-permute-start.2 = (bf16[1,2,256]{2,1,0:T(2,128)(2,1)}, bf16[1,2,256]{2,1,0:T(2,128)(2,1)S(1)}, u32[]{:S(2)}, u32[]{:S(2)}) collective-permute-start(bf16[1,2,256]{2,1,0:T(2,128)(2,1)} %param.11), channel_id=1, source_target_pairs={{0,24},{4,28},{8,16},{12,20},{16,8},{20,12},{24,0},{28,4},{1,25},{... | collective-permute-start | bytes 3080 | tf_op jit(solution)/shard_map/ppermute | solution.py:216
  3.6 4.4 %copy-start.5 = (bf16[1,2,256]{2,1,0:T(2,128)(2,1)S(1)}, bf16[1,2,256]{2,1,0:T(2,128)(2,1)}, u32[]{:S(2)}) copy-start(bf16[1,2,256]{2,1,0:T(2,128)(2,1)} %param.11) | copy-start | bytes 3076
  3.6 10.0 %copy-start = (bf16[16,256]{1,0:T(8,128)(2,1)S(1)}, bf16[16,256]{1,0:T(8,128)(2,1)}, u32[]{:S(2)}) copy-start(bf16[16,256]{1,0:T(8,128)(2,1)} %blocks_ref.1) | copy-start | bytes 24580
  8.1 4.2 %collective-permute-start.4 = (bf16[4,2,256]{2,1,0:T(2,128)(2,1)S(1)}, bf16[4,2,256]{2,1,0:T(2,128)(2,1)S(1)}, u32[]{:S(2)}, u32[]{:S(2)}) collective-permute-start(bf16[4,2,256]{2,1,0:T(2,128)(2,1)S(1)} %constant_dynamic-update-slice_fusion.mine_ref), channel_id=1, source_target_pairs={{0,4},{4,0},{8,12},{12,8},{16,20},{20,16},{24,28},{28,24},{1,5},{5... | collective-permute-start | bytes 12296 | tf_op jit(solution)/shard_map/ppermute | solution.py:222
  10.5 6.6 %collective-permute-start.3 = (bf16[288,2048]{1,0:T(8,128)(2,1)S(1)}, bf16[288,2048]{1,0:T(8,128)(2,1)S(1)}, u32[]{:S(2)}, u32[]{:S(2)}) collective-permute-start(bf16[288,2048]{1,0:T(8,128)(2,1)S(1)} %bitcast.2), channel_id=1, source_target_pairs={{0,4},{4,0},{8,12},{12,8},{16,20},{20,16},{24,28},{28,24},{1,5},{5... | collective-permute-start | bytes 3538952 | tf_op jit(solution)/shard_map/ppermute | solution.py:223
  10.6 10.6 %collective-permute-start.7 = (bf16[288,2048]{1,0:T(8,128)(2,1)S(1)}, bf16[288,2048]{1,0:T(8,128)(2,1)}, u32[]{:S(2)}, u32[]{:S(2)}) collective-permute-start(bf16[288,2048]{1,0:T(8,128)(2,1)S(1)} %bitcast.3), channel_id=1, source_target_pairs={{8,16},{12,20},{16,8},{20,12},{9,17},{13,21},{17,9},{21,13},{10,18... | collective-permute-start | bytes 3538952 | tf_op jit(solution)/shard_map/ppermute | solution.py:220
  12.9 27.1 %collective-permute-start.6 = (bf16[288,2048]{1,0:T(8,128)(2,1)S(1)}, bf16[288,2048]{1,0:T(8,128)(2,1)S(1)}, u32[]{:S(2)}, u32[]{:S(2)}) collective-permute-start(bf16[288,2048]{1,0:T(8,128)(2,1)S(1)} %bitcast.4), channel_id=1, source_target_pairs={{0,8},{4,12},{8,0},{12,4},{16,24},{20,28},{24,16},{28,20},{1,9},{5... | collective-permute-start | bytes 3538952 | tf_op jit(solution)/shard_map/ppermute | solution.py:225
  13.6 0.7 copy-start.1
  14.3 0.7 copy-start.2
  15.0 0.7 copy-start.4
  17.1 46.3 %collective-permute-start.5 = (bf16[288,2048]{1,0:T(8,128)(2,1)S(1)}, bf16[288,2048]{1,0:T(8,128)(2,1)S(1)}, u32[]{:S(2)}, u32[]{:S(2)}) collective-permute-start(bf16[288,2048]{1,0:T(8,128)(2,1)S(1)} %bitcast.5), channel_id=1, source_target_pairs={{0,16},{4,20},{24,8},{28,12},{1,17},{5,21},{25,9},{29,13},{2,18},{... | collective-permute-start | bytes 3538952 | tf_op jit(solution)/shard_map/ppermute | solution.py:234
  40.1 6.5 %collective-permute-start.8 = (bf16[144,2048]{1,0:T(8,128)(2,1)S(1)}, bf16[144,2048]{1,0:T(8,128)(2,1)S(1)}, u32[]{:S(2)}, u32[]{:S(2)}) collective-permute-start(bf16[144,2048]{1,0:T(8,128)(2,1)S(1)} %get-tuple-element.70), channel_id=1, source_target_pairs={{0,4},{4,0},{8,12},{12,8},{16,20},{20,16},{24,28},{28,24},{1,5},{5... | collective-permute-start | bytes 1769480 | tf_op jit(solution)/shard_map/ppermute | solution.py:238
  41.4 5.2 %collective-permute-start.9 = (bf16[144,2048]{1,0:T(8,128)(2,1)S(1)}, bf16[144,2048]{1,0:T(8,128)(2,1)S(1)}, u32[]{:S(2)}, u32[]{:S(2)}) collective-permute-start(bf16[144,2048]{1,0:T(8,128)(2,1)S(1)} %get-tuple-element.69), channel_id=1, source_target_pairs={{0,4},{4,0},{8,12},{12,8},{16,20},{20,16},{24,28},{28,24},{1,5},{5... | collective-permute-start | bytes 1769480 | tf_op jit(solution)/shard_map/ppermute | solution.py:238
  51.9 15.9 %collective-permute-start.10 = (bf16[576,288]{1,0:T(8,128)(2,1)S(1)}, bf16[576,288]{1,0:T(8,128)(2,1)S(1)}, u32[]{:S(2)}, u32[]{:S(2)}) collective-permute-start(bf16[576,288]{1,0:T(8,128)(2,1)S(1)} %get-tuple-element.54), channel_id=1, source_target_pairs={{8,9},{12,13},{9,8},{13,12},{11,10},{15,14},{0,1},{4,5},{1,0},{5,4... | collective-permute-start | bytes 995336 | tf_op jit(solution)/shard_map/ppermute | solution.py:253
  52.6 21.9 %collective-permute-start.11 = (bf16[576,288]{1,0:T(8,128)(2,1)S(1)}, bf16[576,288]{1,0:T(8,128)(2,1)S(1)}, u32[]{:S(2)}, u32[]{:S(2)}) collective-permute-start(bf16[576,288]{1,0:T(8,128)(2,1)S(1)} %get-tuple-element.55), channel_id=1, source_target_pairs={{8,10},{12,14},{10,8},{14,12},{11,9},{15,13},{2,0},{6,4},{3,1},{7,... | collective-permute-start | bytes 995336 | tf_op jit(solution)/shard_map/ppermute | solution.py:253
  56.3 20.6 %collective-permute-start.12 = (bf16[576,288]{1,0:T(8,128)(2,1)S(1)}, bf16[576,288]{1,0:T(8,128)(2,1)S(1)}, u32[]{:S(2)}, u32[]{:S(2)}) collective-permute-start(bf16[576,288]{1,0:T(8,128)(2,1)S(1)} %get-tuple-element.56), channel_id=1, source_target_pairs={{9,10},{13,14},{10,9},{14,13},{11,8},{15,12},{2,1},{6,5},{3,0},{7,... | collective-permute-start | bytes 995336 | tf_op jit(solution)/shard_map/ppermute | solution.py:253
  58.5 18.3 %collective-permute-start.13 = (bf16[576,288]{1,0:T(8,128)(2,1)S(1)}, bf16[576,288]{1,0:T(8,128)(2,1)S(1)}, u32[]{:S(2)}, u32[]{:S(2)}) collective-permute-start(bf16[576,288]{1,0:T(8,128)(2,1)S(1)} %get-tuple-element.57), channel_id=1, source_target_pairs={{11,2},{15,6},{16,25},{20,29}} | collective-permute-start | bytes 995336 | tf_op jit(solution)/shard_map/ppermute | solution.py:254
  77.0 17.3 %collective-permute-start.14 = (bf16[576,288]{1,0:T(8,128)(2,1)S(1)}, bf16[576,288]{1,0:T(8,128)(2,1)S(1)}, u32[]{:S(2)}, u32[]{:S(2)}) collective-permute-start(bf16[576,288]{1,0:T(8,128)(2,1)S(1)} %get-tuple-element.65), channel_id=1, source_target_pairs={{8,11},{12,15},{9,3},{13,7},{19,16},{23,20},{18,24},{22,28}} | collective-permute-start | bytes 995336 | tf_op jit(solution)/shard_map/ppermute | solution.py:276
  78.3 16.0 %collective-permute-start.15 = (bf16[576,288]{1,0:T(8,128)(2,1)S(1)}, bf16[576,288]{1,0:T(8,128)(2,1)S(1)}, u32[]{:S(2)}, u32[]{:S(2)}) collective-permute-start(bf16[576,288]{1,0:T(8,128)(2,1)S(1)} %get-tuple-element.66), channel_id=1, source_target_pairs={{9,11},{13,15},{10,3},{14,7},{18,16},{22,20},{17,24},{21,28}} | collective-permute-start | bytes 995336 | tf_op jit(solution)/shard_map/ppermute | solution.py:276
  79.6 19.5 %collective-permute-start.16 = (bf16[576,288]{1,0:T(8,128)(2,1)S(1)}, bf16[576,288]{1,0:T(8,128)(2,1)S(1)}, u32[]{:S(2)}, u32[]{:S(2)}) collective-permute-start(bf16[576,288]{1,0:T(8,128)(2,1)S(1)} %get-tuple-element.67), channel_id=1, source_target_pairs={{10,11},{14,15},{8,3},{12,7},{17,16},{21,20},{19,24},{23,28}} | collective-permute-start | bytes 995336 | tf_op jit(solution)/shard_map/ppermute | solution.py:276
  80.9 18.2 %collective-permute-start.17 = (bf16[576,288]{1,0:T(8,128)(2,1)S(1)}, bf16[576,288]{1,0:T(8,128)(2,1)S(1)}, u32[]{:S(2)}, u32[]{:S(2)}) collective-permute-start(bf16[576,288]{1,0:T(8,128)(2,1)S(1)} %get-tuple-element.68), channel_id=1, source_target_pairs={{11,3},{15,7},{16,24},{20,28}} | collective-permute-start | bytes 995336 | tf_op jit(solution)/shard_map/ppermute | solution.py:276
  99.5 4.2 %collective-permute-start.18 = (f32[288,288]{1,0:T(8,128)S(1)}, f32[288,288]{1,0:T(8,128)S(1)}, u32[]{:S(2)}, u32[]{:S(2)}) collective-permute-start(f32[288,288]{1,0:T(8,128)S(1)} %get-tuple-element.72), channel_id=1, source_target_pairs={{0,4},{4,0},{8,12},{12,8},{16,20},{20,16},{24,28},{28,24},{1,5},{5... | collective-permute-start | bytes 995336 | tf_op jit(solution)/shard_map/ppermute | solution.py:278
  (1 other events, 0.6 us)

commit v3 on v2

--- a/solution.py
+++ b/solution.py
@@ -85,30 +85,52 @@
         wide_ref[t] = jnp.where(same, full, 0.0).astype(BF16)
 
 
-def kernel_rows(tile_ref, mix_ref, wide_ref, out_ref, mixed, halves):
-    ntiles = wide_ref.shape[0]
-    rows = iota2((AREA, AREA), 0)
-    cols = iota2((AREA, AREA), 1)
+NT_DIMS = (((1,), (1,)), ((), ()))
+
+
+def half_rows(tiles, mix, mixed, halves):
+    ntiles = halves.shape[0]
+    rows, cols = iota2((AREA, AREA), 0), iota2((AREA, AREA), 1)
     swap = ((rows % BLK == cols // BLK) & (rows // BLK == cols % BLK)).astype(BF16)
     for k in range(ntiles):
-        turned = lax.dot_general(
-            swap, tile_ref[:, k * AREA:(k + 1) * AREA], (((1,), (1,)), ((), ())), preferred_element_type=F32
-        ).astype(BF16)
+        block = jnp.concatenate([ref[:, k * AREA:(k + 1) * AREA] for ref in tiles], axis=0)
+        turned = lax.dot_general(swap, block, NT_DIMS, preferred_element_type=F32).astype(BF16)
         for n in range(BLK):
             mixed[n, k * BLK:(k + 1) * BLK, :] = turned[n * BLK:(n + 1) * BLK, :]
-    mix = mix_ref[...]
     for n in range(BLK):
         half = jnp.dot(mix, mixed[n], preferred_element_type=F32).astype(BF16)
         for t in range(ntiles):
             halves[t, n * BLK:(n + 1) * BLK, :] = half[t * BLK:(t + 1) * BLK, :]
-    for t in range(ntiles):
+
+
+def k_own_body(tile_ref, mix_ref, wide_ref, out_ref, mixed, halves):
+    half_rows((tile_ref,), mix_ref[...], mixed, halves)
+    for t in range(wide_ref.shape[0]):
+        out_ref[:, t * AREA:(t + 1) * AREA] = lax.dot_general(
+            halves[t], wide_ref[t], (((0,), (1,)), ((), ())), preferred_element_type=F32
+        ).astype(BF16)
+
+
+def k_moved_body(inner_ref, outer_ref, mix_ref, wide_ref, out_ref, mixed, halves):
+    half_rows((inner_ref, outer_ref), mix_ref[...], mixed, halves)
+    for t in range(wide_ref.shape[0]):
         out_ref[t * AREA:(t + 1) * AREA, :] = jnp.dot(
             wide_ref[t], halves[t], preferred_element_type=F32
         ).astype(BF16)
 
 
-def k_body(tile_ref, mix_ref, wide_ref, out_ref, mixed, halves):
-    kernel_rows(tile_ref, mix_ref, wide_ref, out_ref, mixed, halves)
+def packed(top, bottom):
+    half = top.shape[0] // 2
+    return jnp.concatenate([top[:half], top[half:], bottom[:half], bottom[half:]], axis=1)
+
+
+def dot_rows(left, right):
+    return lax.dot_general(left, right, NT_DIMS, preferred_element_type=F32)
+
+
+def near_body(o_ref, p_ref, k_ref, out_ref):
+    right = k_ref[...]
+    out_ref[...] = packed(dot_rows(o_ref[...], right), dot_rows(p_ref[...], right))
 
 
 def place_of():
@@ -117,55 +139,66 @@
     return jnp.where(near, plane, 3 - plane), jnp.where(near, red, 3 - red)
 
 
-def early_body(o_ref, p_ref, e_ref, f_ref, g_ref, ko_ref, ke_ref, kb_ref, own_ref, s1, s2, s3, s4, terms):
+def early_body(o_ref, p_ref, e_ref, f_ref, g_ref, kt_ref, near_ref, own_ref, s1, s2, s3, held_ref, terms):
     aux = o_ref.shape[0]
-    for at, right, lefts in (
-        (0, ko_ref, (o_ref, p_ref)),
-        (1, ke_ref, (o_ref, p_ref)),
-        (2, kb_ref, (o_ref, p_ref)),
-        (3, kb_ref, (e_ref, f_ref, g_ref)),
-    ):
-        right_value = right[...]
-        row = 0
-        for left in lefts:
-            count = left.shape[0]
-            terms[at, row:row + count, :] = jnp.dot(left[...], right_value, preferred_element_type=F32)
-            row += count
-    plane, red = place_of()
+    right = kt_ref[...]
+    top = jnp.dot(o_ref[...], right, preferred_element_type=F32)
+    bottom = jnp.dot(p_ref[...], right, preferred_element_type=F32)
+    terms[0] = near_ref[...]
+    terms[1] = packed(top[:, aux:], bottom[:, aux:])
+    terms[2] = packed(top[:, :aux], bottom[:, :aux])
+    inner = kt_ref[:, :aux]
+    lower = jnp.concatenate([f_ref[...], g_ref[...]], axis=0)
+    terms[3] = packed(
+        jnp.dot(e_ref[...], inner, preferred_element_type=F32), jnp.dot(lower, inner, preferred_element_type=F32)
+    )
+    plane, place = place_of()
+    hub = plane == 1
 
     def term_for(column):
-        hub = jnp.where(column < 2, 1 - column, column)
-        return jnp.where(plane == 1, hub, jnp.minimum(column, 1))
-
-    mine = (plane == 1) & (red < 3) | (plane == 0) & (red < 2)
-    own_ref[...] = jnp.where(mine, terms[term_for(red)], 0.0)
+        return jnp.where(hub, jnp.where(column < 2, 1 - column, column), jnp.minimum(column, 1))
+
+    mine = hub & (place < 3) | (plane == 0) & (place < 2)
+    own_ref[...] = jnp.where(mine, terms[term_for(place)], 0.0)
     for d, out in zip((1, 2, 3), (s1, s2, s3)):
-        out[...] = terms[term_for(red ^ d)].astype(BF16)
-    s4[...] = terms[3].astype(BF16)
-
-
-def late_body(c_ref, o_ref, p_ref, e_ref, f_ref, g_ref, mix_ref, wide_ref, own_ref, s1, s2, s3, s4, near, kt, mixed, halves):
-    aux = o_ref.shape[0]
-    kernel_rows(c_ref, mix_ref, wide_ref, kt, mixed, halves)
-    right = kt[...]
+        out[...] = terms[term_for(place ^ d)].astype(BF16)
+    held_ref[...] = terms[3].astype(BF16)
+
+
+LATE = ((2, 0, None, 1), (0, 2, None, None), (None, None, 0, 2), (None, None, 2, None))
+LATE_TO = {0: (1, 3), 1: (0, 2), 2: (0, 3)}
+
+
+def by_place(place, values):
+    chosen = jnp.int32(values[3] or 0)
+    for at in (2, 1, 0):
+        chosen = jnp.where(place == at, values[at] or 0, chosen)
+    return chosen
+
+
+def late_body(k_ref, o_ref, p_ref, e_ref, f_ref, g_ref, held_ref, own_ref, s1, s2, s3, s4, terms):
+    right = k_ref[...]
     plane, place = place_of()
-    mine = (plane == 1) & (place == 3)
-    half = aux // 2
-    near_parts = [(o_ref, 0, aux), (p_ref, aux, aux)]
-    far_parts = [(e_ref, 0, aux), (f_ref, aux, half), (g_ref, aux + half, half)]
-    for left, row, count in near_parts:
-        value = jnp.dot(left[...], right, preferred_element_type=F32)
-        own_ref[row:row + count, :] = jnp.where(mine, value, 0.0)
-        near[row:row + count, :] = value.astype(BF16)
-    for left, row, count in far_parts:
-        rows = slice(row, row + count)
-        value = jnp.dot(left[...], right, preferred_element_type=F32).astype(BF16)
-        for source, out in enumerate((s1, s2, s3)):
-            out[rows, :] = jnp.where(place == source, near[rows, :], value)
-        s4[rows, :] = value
-
-
-def call(body, outs, ins, scratch=(), smem=0, flops=0, name=None, vmem=VMEM_BYTES):
+    lower = jnp.concatenate([f_ref[...], g_ref[...]], axis=0)
+    near = packed(dot_rows(o_ref[...], right), dot_rows(p_ref[...], right))
+    own_ref[...] = jnp.where((plane == 1) & (place == 3), near, 0.0)
+    terms[0] = near.astype(BF16)
+    terms[1] = held_ref[...]
+    terms[2] = packed(dot_rows(e_ref[...], right), dot_rows(lower, right)).astype(BF16)
+    for sent, out in zip(LATE, (s1, s2, s3, s4)):
+        out[...] = terms[by_place(place, sent)]
+
+
+def join_body(kept_ref, other_ref, out_ref):
+    first = lax.axis_index("pair") % CORES == 0
+    kept, other = kept_ref[...], other_ref[...]
+    left, right = jnp.where(first, kept, other), jnp.where(first, other, kept)
+    half, width = left.shape[0], left.shape[1] // 2
+    out_ref[:half, :] = jnp.concatenate([left[:, :width], right[:, :width]], axis=1)
+    out_ref[half:, :] = jnp.concatenate([left[:, width:], right[:, width:]], axis=1)
+
+
+def call(body, outs, ins, scratch=(), smem=0, name=None):
     return pl.pallas_call(
         body,
         out_shape=outs,
@@ -173,7 +206,7 @@
         + [pl.BlockSpec(memory_space=pltpu.VMEM)] * (len(ins) - smem),
         out_specs=jax.tree.map(lambda _: pl.BlockSpec(memory_space=pltpu.VMEM), outs),
         scratch_shapes=list(scratch),
-        compiler_params=pltpu.CompilerParams(vmem_limit_bytes=vmem),
+        compiler_params=pltpu.CompilerParams(vmem_limit_bytes=VMEM_BYTES),
         cost_estimate=pl.CostEstimate(
             flops=1, transcendentals=0, bytes_accessed=1
         ),
@@ -188,7 +221,6 @@
 def hub_plan(three_center, occ_src, occ_block, occ_blocks, virt_block, virt_blocks):
     aux, ntiles, area = three_center.shape
     depth = ntiles * area
-    core = lax.axis_index("pair") % CORES
 
     def along_z(moves):
         return [(CORES * a + c, CORES * b + c) for a, b in moves for c in range(CORES)]
@@ -204,13 +236,6 @@
 
     def scratch_for(count):
         return [pltpu.VMEM((BLK, ntiles * BLK, count), BF16), pltpu.VMEM((ntiles, area, count), BF16)]
-
-    def kernel_of(rows, mix, wide, name):
-        count = rows.shape[0]
-        return call(
-            k_body, shaped(depth, count), [rows, mix, wide], scratch_for(count),
-            flops=2 * count * depth * 3 * area, name=name,
-        )
 
     from_planes = [virt_blocks] + [
         lax.ppermute(virt_blocks, "pair", along_z([(a, a ^ k) for a in range(4)])) for k in (1, 2, 3)
@@ -231,55 +256,46 @@
         smem=3, name="prep",
     )
     partner, wide, tiles = after((partner, wide, tiles))
-    far = lax.ppermute(tiles, "pair", along_z([(0, 2), (3, 1)]))
-    k_own = kernel_of(tiles, mix, wide, "k_own")
-    outer, inner, k_own = after((outer, inner, k_own))
+    k_own = call(k_own_body, shaped(aux, depth), [tiles, mix, wide], scratch_for(aux), name="k_own")
+    far = lax.ppermute(k_own, "pair", along_z([(0, 2), (3, 1)]))
+    term = (aux // 2, 4 * aux)
+    near = call(near_body, shaped(*term, dtype=F32), [tiles, partner, k_own], name="near")
+    outer, inner, near = after((outer, inner, near))
 
     outer_partner = [lax.ppermute(outer[at:at + aux // 2], "pair", core_swap) for at in (0, aux // 2)]
-    k_outer = kernel_of(outer, mix, wide, "k_outer")
-    k_inner = kernel_of(inner, mix, wide, "k_inner")
-    own_early, *sent = call(
+    k_moved = call(
+        k_moved_body, shaped(depth, 2 * aux), [inner, outer, mix, wide], scratch_for(2 * aux), name="k_moved"
+    )
+    own_early, *sent, held = call(
         early_body,
-        [shaped(2 * aux, aux, dtype=F32)] + [shaped(2 * aux, aux)] * 4,
-        [tiles, partner, outer, *outer_partner, k_own, k_outer, k_inner],
-        [pltpu.VMEM((4, 2 * aux, aux), F32)],
-        flops=2 * 8 * aux * aux * depth, name="early",
+        [shaped(*term, dtype=F32)] + [shaped(*term)] * 4,
+        [tiles, partner, outer, *outer_partner, k_moved, near],
+        [pltpu.VMEM((4, *term), F32)],
+        name="early",
     )
     arrived = []
-    for d, value in zip((1, 2, 3), sent):
+    for d, value in reversed(list(zip((1, 2, 3), sent))):
         moves = [((1, g), (1, g ^ d)) for g in range(4) if g ^ d != 3]
         moves += [((0, g), (0, g ^ d)) for g in range(4) if g ^ d < 2]
         moves += [((1, 3 ^ d), (0, 2))]
         arrived.append(lax.ppermute(value, both, everywhere(moves)))
-    arrived.append(lax.ppermute(sent[3], both, everywhere([((1, 3), (0, 2))])))
-
-    far, own_early = after((far, own_early))
+
+    far, held = after((far, held))
     own_late, *late_sent = call(
         late_body,
-        [shaped(2 * aux, aux, dtype=F32)] + [shaped(2 * aux, aux)] * 4,
-        [far, tiles, partner, outer, *outer_partner, mix, wide],
-        [pltpu.VMEM((2 * aux, aux), BF16), pltpu.VMEM((depth, aux), BF16)] + scratch_for(aux),
-        flops=2 * 4 * aux * aux * depth, name="late",
-    )
-    late_moves = [
-        [((1, 0), (1, 3)), ((1, 1), (0, 3))],
-        [((1, 1), (1, 3)), ((1, 2), (0, 3))],
-        [((1, 2), (1, 3)), ((1, 0), (0, 3))],
-        [((1, 3), (0, 3))],
-    ]
-    total = own_early
+        [shaped(*term, dtype=F32)] + [shaped(*term)] * 4,
+        [far, tiles, partner, outer, *outer_partner, held],
+        [pltpu.VMEM((3, *term), BF16)],
+        name="late",
+    )
+    for sources, value in zip(LATE, late_sent):
+        moves = [((1, g), LATE_TO[what]) for g, what in enumerate(sources) if what is not None]
+        arrived.append(lax.ppermute(value, both, everywhere(moves)))
+    total = own_early + own_late
     for value in arrived:
         total = total + value.astype(F32)
-    total, *late_sent = after((total, *late_sent))
-    total = total + own_late
-    for moves, value in zip(late_moves, late_sent):
-        total = total + lax.ppermute(value, both, everywhere(moves)).astype(F32)
-
-    other = lax.ppermute(total[aux:], "pair", core_swap)
-    kept = total[:aux]
-    return jnp.where(
-        core == 0, jnp.concatenate([kept, other], axis=1), jnp.concatenate([other, kept], axis=1)
-    )
+    other = lax.ppermute(total[:, 2 * aux:], "pair", core_swap)
+    return call(join_body, shaped(aux, 2 * aux, dtype=F32), [total[:, :2 * aux], other], name="join")
 
 
 def solution(mesh):

time: 105 us -> 90.7 us (0.86)
  waiting for transfers between devices: 53.1 us -> 45 us
  starting transfers between devices: 26.7 us -> 23.3 us
  Pallas kernels: 18.1 us -> 16.1 us
  other arithmetic: 1.69 us -> 0.43 us
    ppermute x7 -> x2, waiting for transfers between devices: 22.5 us -> 11.3 us  [the longest x1 9.98 us: hub_plan(): far = lax.ppermute(k_own, 'pair', along_z([(0, 2), (3, 1)]))]
    ppermute x7 -> x2, starting transfers between devices: 10.9 us -> 4.55 us  [the longest x1 2.35 us: hub_plan(): other = lax.ppermute(total[:, 2 * aux:], 'pair', core_swap)]
    ppermute x3 -> x7, waiting for transfers between devices: 9.02 us -> 13.5 us  [hub_plan(): arrived.append(lax.ppermute(value, both, everywhere(moves)))]
    ppermute x3 -> x7, starting transfers between devices: 6.54 us -> 9.48 us  [hub_plan(): arrived.append(lax.ppermute(value, both, everywhere(moves)))]
    pallas_call x6 -> x7, Pallas kernels: 18.1 us -> 16.1 us  [call(): pl.pallas_call(body, out_shape=outs, in_specs=[pl.BlockSpec(memory_space=...]
    ppermute x1, waiting for transfers between devices: 18.8 us -> 17.4 us  [hub_plan(): lax.ppermute(tiles, 'pair', along_z([(0, 1), (1, 0), (2, 3), (3, 2)]))]
    select_n x1 -> x0, other arithmetic: 1.16 us -> none  [hub_plan(): jnp.where(core == 0, jnp.concatenate([kept, other], axis=1), jnp.concaten...]
  transfers between devices with their start and end apart: 19 -> 18, of which waited for: 8 -> 6; matrix products, arithmetic and copies ran while one was open for 2% -> 3% of each run, Pallas kernels for 17% -> 17%
where the time goes in v3:
time: 90.7 us; the launch traced here: 90.3 us
  waiting for transfers between devices  45 us (50%)
  starting transfers between devices  23.3 us (26%)
  Pallas kernels  16.1 us (18%)
  local copies, waits for them, and re-layouts  5.32 us (6%)
    ppermute x1, waiting for transfers between devices, hub_plan(): lax.ppermute(tiles, 'pair', along_z([(0, 1), (1, 0), (2, 3), (3, 2)]))  17.4 us
    pallas_call x7, Pallas kernels, call(): pl.pallas_call(body, out_shape=outs, in_specs=[pl.BlockSpec(memory_space=...  16.1 us
    ppermute x7, waiting for transfers between devices, hub_plan(): arrived.append(lax.ppermute(value, both, everywhere(moves)))  13.5 us
    ppermute x1, waiting for transfers between devices, hub_plan(): far = lax.ppermute(k_own, 'pair', along_z([(0, 2), (3, 1)]))  9.98 us
    ppermute x7, starting transfers between devices, hub_plan(): arrived.append(lax.ppermute(value, both, everywhere(moves)))  9.48 us
    unnamed x17, local copies, waits for them, and re-layouts  5.06 us
    ppermute x3, starting transfers between devices, hub_plan(): lax.ppermute(virt_blocks, 'pair', along_z([(a, a ^ k) for a in range(4)]))  3.61 us
    ppermute x3, waiting for transfers between devices, hub_plan(): lax.ppermute(virt_blocks, 'pair', along_z([(a, a ^ k) for a in range(4)]))  2.75 us
  transfers between devices with their start and end apart: 18, of which 6 were waited for; matrix products, arithmetic and copies ran while one was open for 3% of the time, Pallas kernels for 17%

profile of v3, /device:TPU:7, one launch (start us, length us, event | category | flops | bytes accessed | tf_op | source)
XLA Modules:
  0.0 90.3 jit_solution(14097890320138932072)
XLA Ops:
  0.0 2.3 %collective-permute-start.1 = (bf16[1,2,256]{2,1,0:T(2,128)(2,1)}, bf16[1,2,256]{2,1,0:T(2,128)(2,1)S(1)}, u32[]{:S(2)}, u32[]{:S(2)}) collective-permute-start(bf16[1,2,256]{2,1,0:T(2,128)(2,1)} %param.11), channel_id=1, source_target_pairs={{0,16},{4,20},{8,24},{12,28},{16,0},{20,4},{24,8},{28,12},{1,17},{... | collective-permute-start | bytes 3080 | tf_op jit(solution)/shard_map/ppermute | solution.py:241
  2.3 1.3 %collective-permute-start = (bf16[1,2,256]{2,1,0:T(2,128)(2,1)}, bf16[1,2,256]{2,1,0:T(2,128)(2,1)S(1)}, u32[]{:S(2)}, u32[]{:S(2)}) collective-permute-start(bf16[1,2,256]{2,1,0:T(2,128)(2,1)} %param.11), channel_id=1, source_target_pairs={{0,8},{4,12},{8,0},{12,4},{16,24},{20,28},{24,16},{28,20},{1,9},{5... | collective-permute-start | bytes 3080 | tf_op jit(solution)/shard_map/ppermute | solution.py:241
  3.6 1.6 %copy.8 = bf16[36,8,8,256]{3,1,2,0:T(8,128)(2,1)S(1)} copy(bf16[36,8,8,256]{3,2,1,0:T(8,128)(2,1)} %bitcast.9) | data formatting | bytes 2359296
  5.3 2.7 %collective-permute-done.2 = bf16[1,2,256]{2,1,0:T(2,128)(2,1)S(1)} collective-permute-done((bf16[1,2,256]{2,1,0:T(2,128)(2,1)}, bf16[1,2,256]{2,1,0:T(2,128)(2,1)S(1)}, u32[]{:S(2)}, u32[]{:S(2)}) %collective-permute-start.2) | collective-permute-done | bytes 1056 | tf_op jit(solution)/shard_map/ppermute | solution.py:241
  8.1 2.5 %collective-permute-start.4 = (bf16[4,2,256]{2,1,0:T(2,128)(2,1)S(1)}, bf16[4,2,256]{2,1,0:T(2,128)(2,1)S(1)}, u32[]{:S(2)}, u32[]{:S(2)}) collective-permute-start(bf16[4,2,256]{2,1,0:T(2,128)(2,1)S(1)} %constant_dynamic-update-slice_fusion.mine_ref), channel_id=1, source_target_pairs={{0,4},{4,0},{8,12},{12,8},{16,20},{20,16},{24,28},{28,24},{1,5},{5... | collective-permute-start | bytes 12296 | tf_op jit(solution)/shard_map/ppermute | solution.py:247
  10.6 1.7 %collective-permute-start.6 = (bf16[288,2048]{1,0:T(8,128)(2,1)S(1)}, bf16[288,2048]{1,0:T(8,128)(2,1)}, u32[]{:S(2)}, u32[]{:S(2)}) collective-permute-start(bf16[288,2048]{1,0:T(8,128)(2,1)S(1)} %bitcast.3), channel_id=1, source_target_pairs={{8,16},{12,20},{16,8},{20,12},{9,17},{13,21},{17,9},{21,13},{10,18... | collective-permute-start | bytes 3538952 | tf_op jit(solution)/shard_map/ppermute | solution.py:245
  15.7 1.4 %prep.1 = (bf16[128,128]{1,0:T(8,128)(2,1)S(1)}, bf16[8,256,256]{2,1,0:T(8,128)(2,1)S(1)}) custom-call(s32[8,8]{1,0:T(8,128)S(1)} %copy-done.1, s32[8,8]{1,0:T(8,128)S(1)} %copy-done.2, s32[1,8,1]{2,1,0:T(8,128)S(1)} %copy.7.listed_ref, bf16[16,256]{1,0:T(8,128)(2,1)S(1)} %copy-done, bf16[4,2,256]{2,1,0:T(2,128)(2,1)S(1)} %constant_dynamic-update-slice_fusion.mine_ref, ...), custom_call_target="tpu_custom_call" | custom-call | flops 1 | bytes 1 | tf_op jit(solution)/shard_map/prep/pallas_call | solution.py:202
  17.1 1.8 %k_own.1.k_ref = bf16[288,2048]{1,0:T(8,128)(2,1)S(1)} custom-call(bf16[288,2048]{1,0:T(8,128)(2,1)S(1)} %bitcast.5, bf16[128,128]{1,0:T(8,128)(2,1)S(1)} %get-tuple-element.42.mix_ref, bf16[8,256,256]{2,1,0:T(8,128)(2,1)S(1)} %get-tuple-element.43.wide_ref), custom_call_target="tpu_custom_call" | custom-call | flops 1 | bytes 1 | tf_op jit(solution)/shard_map/k_own/pallas_call | solution.py:202
  18.9 2.2 %collective-permute-start.9 = (bf16[288,2048]{1,0:T(8,128)(2,1)S(1)}, bf16[288,2048]{1,0:T(8,128)(2,1)S(1)}, u32[]{:S(2)}, u32[]{:S(2)}) collective-permute-start(bf16[288,2048]{1,0:T(8,128)(2,1)S(1)} %k_own.1.k_ref), channel_id=1, source_target_pairs={{0,16},{4,20},{24,8},{28,12},{1,17},{5,21},{25,9},{29,13},{2,18},{... | collective-permute-start | bytes 3538952 | tf_op jit(solution)/shard_map/ppermute | solution.py:260
  21.1 1.4 %near.1.near_ref = f32[144,1152]{1,0:T(8,128)S(1)} custom-call(bf16[288,2048]{1,0:T(8,128)(2,1)S(1)} %bitcast.6, bf16[288,2048]{1,0:T(8,128)(2,1)S(1)} %collective-permute-done.3.p_ref, bf16[288,2048]{1,0:T(8,128)(2,1)S(1)} %k_own.1.k_ref), custom_call_target="tpu_custom_call" | custom-call | flops 1 | bytes 1 | tf_op jit(solution)/shard_map/near/pallas_call | solution.py:202
  22.6 17.4 %collective-permute-done.5.outer_ref.e_ref = bf16[288,2048]{1,0:T(8,128)(2,1)S(1)} collective-permute-done((bf16[288,2048]{1,0:T(8,128)(2,1)S(1)}, bf16[288,2048]{1,0:T(8,128)(2,1)S(1)}, u32[]{:S(2)}, u32[]{:S(2)}) %collective-permute-start.5) | collective-permute-done | bytes 1179680 | tf_op jit(solution)/shard_map/ppermute | solution.py:250
  40.1 1.3 %collective-permute-start.8 = (bf16[144,2048]{1,0:T(8,128)(2,1)S(1)}, bf16[144,2048]{1,0:T(8,128)(2,1)S(1)}, u32[]{:S(2)}, u32[]{:S(2)}) collective-permute-start(bf16[144,2048]{1,0:T(8,128)(2,1)S(1)} %get-tuple-element.59), channel_id=1, source_target_pairs={{0,4},{4,0},{8,12},{12,8},{16,20},{20,16},{24,28},{28,24},{1,5},{5... | collective-permute-start | bytes 1769480 | tf_op jit(solution)/shard_map/ppermute | solution.py:265
  41.5 4.0 %k_moved.1.kt_ref = bf16[2048,576]{1,0:T(8,128)(2,1)S(1)} custom-call(bf16[288,2048]{1,0:T(8,128)(2,1)} %collective-permute-done.6.inner_ref, bf16[288,2048]{1,0:T(8,128)(2,1)S(1)} %collective-permute-done.5.outer_ref.e_ref, bf16[128,128]{1,0:T(8,128)(2,1)S(1)} %get-tuple-element.42.mix_ref, bf16[8,256,256]{2,1,0:T(8,128)(2,1)S(1)} %get-tuple-element.43.wide_ref), custom_call_target="tpu_custom_call" | custom-call | flops 1 | bytes 1 | tf_op jit(solution)/shard_map/k_moved/pallas_call | solution.py:202
  45.5 3.6 %early.1 = (f32[144,1152]{1,0:T(8,128)S(1)}, bf16[144,1152]{1,0:T(8,128)(2,1)S(1)}, bf16[144,1152]{1,0:T(8,128)(2,1)S(1)}, bf16[144,1152]{1,0:T(8,128)(2,1)S(1)}, bf16[144,1152]{1,0:T(8,128)(2,1)S(1)}) custom-call(bf16[288,2048]{1,0:T(8,128)(2,1)S(1)} %bitcast.7, bf16[288,2048]{1,0:T(8,128)(2,1)S(1)} %collective-permute-done.3.p_ref, ...), custom_call_target="tpu_custom_call" | custom-call | flops 1 | bytes 1 | tf_op jit(solution)/shard_map/early/pallas_call | solution.py:202
  49.1 2.1 %collective-permute-start.10 = (bf16[144,1152]{1,0:T(8,128)(2,1)S(1)}, bf16[144,1152]{1,0:T(8,128)(2,1)S(1)}, u32[]{:S(2)}, u32[]{:S(2)}) collective-permute-start(bf16[144,1152]{1,0:T(8,128)(2,1)S(1)} %get-tuple-element.52), channel_id=1, source_target_pairs={{9,10},{13,14},{10,9},{14,13},{11,8},{15,12},{2,1},{6,5},{3,0},{7,... | collective-permute-start | bytes 995336 | tf_op jit(solution)/shard_map/ppermute | solution.py:281
  51.2 1.3 %collective-permute-start.11 = (bf16[144,1152]{1,0:T(8,128)(2,1)S(1)}, bf16[144,1152]{1,0:T(8,128)(2,1)S(1)}, u32[]{:S(2)}, u32[]{:S(2)}) collective-permute-start(bf16[144,1152]{1,0:T(8,128)(2,1)S(1)} %get-tuple-element.53), channel_id=1, source_target_pairs={{8,10},{12,14},{10,8},{14,12},{11,9},{15,13},{2,0},{6,4},{3,1},{7,... | collective-permute-start | bytes 995336 | tf_op jit(solution)/shard_map/ppermute | solution.py:281
  53.4 10.0 %collective-permute-done.9.k_ref = bf16[288,2048]{1,0:T(8,128)(2,1)S(1)} collective-permute-done((bf16[288,2048]{1,0:T(8,128)(2,1)S(1)}, bf16[288,2048]{1,0:T(8,128)(2,1)S(1)}, u32[]{:S(2)}, u32[]{:S(2)}) %collective-permute-start.9) | collective-permute-done | bytes 1179680 | tf_op jit(solution)/shard_map/ppermute | solution.py:260
  63.4 2.8 %late.1 = (f32[144,1152]{1,0:T(8,128)S(1)}, bf16[144,1152]{1,0:T(8,128)(2,1)S(1)}, bf16[144,1152]{1,0:T(8,128)(2,1)S(1)}, bf16[144,1152]{1,0:T(8,128)(2,1)S(1)}, bf16[144,1152]{1,0:T(8,128)(2,1)S(1)}) custom-call(bf16[288,2048]{1,0:T(8,128)(2,1)S(1)} %collective-permute-done.9.k_ref, bf16[288,2048]{1,0:T(8,128)(2,1)S(1)} %bitcast.8, ...), custom_call_target="tpu_custom_call" | custom-call | flops 1 | bytes 1 | tf_op jit(solution)/shard_map/late/pallas_call | solution.py:202
  66.3 1.3 %collective-permute-start.13 = (bf16[144,1152]{1,0:T(8,128)(2,1)S(1)}, bf16[144,1152]{1,0:T(8,128)(2,1)S(1)}, u32[]{:S(2)}, u32[]{:S(2)}) collective-permute-start(bf16[144,1152]{1,0:T(8,128)(2,1)S(1)} %get-tuple-element.55), channel_id=1, source_target_pairs={{8,3},{12,7},{9,11},{13,15},{11,2},{15,6},{19,24},{23,28},{18,16},... | collective-permute-start | bytes 995336 | tf_op jit(solution)/shard_map/ppermute | solution.py:293
  70.2 1.3 %collective-permute-start.16 = (bf16[144,1152]{1,0:T(8,128)(2,1)S(1)}, bf16[144,1152]{1,0:T(8,128)(2,1)S(1)}, u32[]{:S(2)}, u32[]{:S(2)}) collective-permute-start(bf16[144,1152]{1,0:T(8,128)(2,1)S(1)} %get-tuple-element.58), channel_id=1, source_target_pairs={{10,3},{14,7},{17,24},{21,28}} | collective-permute-start | bytes 995336 | tf_op jit(solution)/shard_map/ppermute | solution.py:293
  71.5 10.8 %collective-permute-done.13 = bf16[144,1152]{1,0:T(8,128)(2,1)S(1)} collective-permute-done((bf16[144,1152]{1,0:T(8,128)(2,1)S(1)}, bf16[144,1152]{1,0:T(8,128)(2,1)S(1)}, u32[]{:S(2)}, u32[]{:S(2)}) %collective-permute-start.13) | collective-permute-done | bytes 331808 | tf_op jit(solution)/shard_map/ppermute | solution.py:293
  82.2 2.7 %collective-permute-done.14 = bf16[144,1152]{1,0:T(8,128)(2,1)S(1)} collective-permute-done((bf16[144,1152]{1,0:T(8,128)(2,1)S(1)}, bf16[144,1152]{1,0:T(8,128)(2,1)S(1)}, u32[]{:S(2)}, u32[]{:S(2)}) %collective-permute-start.14) | collective-permute-done | bytes 331808 | tf_op jit(solution)/shard_map/ppermute | solution.py:293
  85.6 2.4 %collective-permute-start.17 = (f32[144,576]{1,0:T(8,128)S(1)}, f32[144,576]{1,0:T(8,128)S(1)}, u32[]{:S(2)}, u32[]{:S(2)}) collective-permute-start(f32[144,576]{1,0:T(8,128)S(1)} %get-tuple-element.61), channel_id=1, source_target_pairs={{0,4},{4,0},{8,12},{12,8},{16,20},{20,16},{24,28},{28,24},{1,5},{5... | collective-permute-start | bytes 995336 | tf_op jit(solution)/shard_map/ppermute | solution.py:297
  87.9 1.3 %collective-permute-done.17.other_ref = f32[144,576]{1,0:T(8,128)S(1)} collective-permute-done((f32[144,576]{1,0:T(8,128)S(1)}, f32[144,576]{1,0:T(8,128)S(1)}, u32[]{:S(2)}, u32[]{:S(2)}) %collective-permute-start.17) | collective-permute-done | bytes 331808 | tf_op jit(solution)/shard_map/ppermute | solution.py:297
  (40 shorter events, 8.8 us)
Async XLA Ops:
  0.0 5.3 %collective-permute-start.1 = (bf16[1,2,256]{2,1,0:T(2,128)(2,1)}, bf16[1,2,256]{2,1,0:T(2,128)(2,1)S(1)}, u32[]{:S(2)}, u32[]{:S(2)}) collective-permute-start(bf16[1,2,256]{2,1,0:T(2,128)(2,1)} %param.11), channel_id=1, source_target_pairs={{0,16},{4,20},{8,24},{12,28},{16,0},{20,4},{24,8},{28,12},{1,17},{... | collective-permute-start | bytes 3080 | tf_op jit(solution)/shard_map/ppermute | solution.py:241
  2.3 3.0 %collective-permute-start = (bf16[1,2,256]{2,1,0:T(2,128)(2,1)}, bf16[1,2,256]{2,1,0:T(2,128)(2,1)S(1)}, u32[]{:S(2)}, u32[]{:S(2)}) collective-permute-start(bf16[1,2,256]{2,1,0:T(2,128)(2,1)} %param.11), channel_id=1, source_target_pairs={{0,8},{4,12},{8,0},{12,4},{16,24},{20,28},{24,16},{28,20},{1,9},{5... | collective-permute-start | bytes 3080 | tf_op jit(solution)/shard_map/ppermute | solution.py:241
  3.6 4.4 %collective-permute-start.2 = (bf16[1,2,256]{2,1,0:T(2,128)(2,1)}, bf16[1,2,256]{2,1,0:T(2,128)(2,1)S(1)}, u32[]{:S(2)}, u32[]{:S(2)}) collective-permute-start(bf16[1,2,256]{2,1,0:T(2,128)(2,1)} %param.11), channel_id=1, source_target_pairs={{0,24},{4,28},{8,16},{12,20},{16,8},{20,12},{24,0},{28,4},{1,25},{... | collective-permute-start | bytes 3080 | tf_op jit(solution)/shard_map/ppermute | solution.py:241
  3.6 4.4 %copy-start.5 = (bf16[1,2,256]{2,1,0:T(2,128)(2,1)S(1)}, bf16[1,2,256]{2,1,0:T(2,128)(2,1)}, u32[]{:S(2)}) copy-start(bf16[1,2,256]{2,1,0:T(2,128)(2,1)} %param.11) | copy-start | bytes 3076
  3.6 10.0 %copy-start = (bf16[16,256]{1,0:T(8,128)(2,1)S(1)}, bf16[16,256]{1,0:T(8,128)(2,1)}, u32[]{:S(2)}) copy-start(bf16[16,256]{1,0:T(8,128)(2,1)} %blocks_ref.1) | copy-start | bytes 24580
  8.1 4.2 %collective-permute-start.4 = (bf16[4,2,256]{2,1,0:T(2,128)(2,1)S(1)}, bf16[4,2,256]{2,1,0:T(2,128)(2,1)S(1)}, u32[]{:S(2)}, u32[]{:S(2)}) collective-permute-start(bf16[4,2,256]{2,1,0:T(2,128)(2,1)S(1)} %constant_dynamic-update-slice_fusion.mine_ref), channel_id=1, source_target_pairs={{0,4},{4,0},{8,12},{12,8},{16,20},{20,16},{24,28},{28,24},{1,5},{5... | collective-permute-start | bytes 12296 | tf_op jit(solution)/shard_map/ppermute | solution.py:247
  10.5 6.6 %collective-permute-start.3 = (bf16[288,2048]{1,0:T(8,128)(2,1)S(1)}, bf16[288,2048]{1,0:T(8,128)(2,1)S(1)}, u32[]{:S(2)}, u32[]{:S(2)}) collective-permute-start(bf16[288,2048]{1,0:T(8,128)(2,1)S(1)} %bitcast.2), channel_id=1, source_target_pairs={{0,4},{4,0},{8,12},{12,8},{16,20},{20,16},{24,28},{28,24},{1,5},{5... | collective-permute-start | bytes 3538952 | tf_op jit(solution)/shard_map/ppermute | solution.py:248
  10.6 12.0 %collective-permute-start.6 = (bf16[288,2048]{1,0:T(8,128)(2,1)S(1)}, bf16[288,2048]{1,0:T(8,128)(2,1)}, u32[]{:S(2)}, u32[]{:S(2)}) collective-permute-start(bf16[288,2048]{1,0:T(8,128)(2,1)S(1)} %bitcast.3), channel_id=1, source_target_pairs={{8,16},{12,20},{16,8},{20,12},{9,17},{13,21},{17,9},{21,13},{10,18... | collective-permute-start | bytes 3538952 | tf_op jit(solution)/shard_map/ppermute | solution.py:245
  12.3 0.6 copy-start.3
  12.9 27.1 %collective-permute-start.5 = (bf16[288,2048]{1,0:T(8,128)(2,1)S(1)}, bf16[288,2048]{1,0:T(8,128)(2,1)S(1)}, u32[]{:S(2)}, u32[]{:S(2)}) collective-permute-start(bf16[288,2048]{1,0:T(8,128)(2,1)S(1)} %bitcast.4), channel_id=1, source_target_pairs={{0,8},{4,12},{8,0},{12,4},{16,24},{20,28},{24,16},{28,20},{1,9},{5... | collective-permute-start | bytes 3538952 | tf_op jit(solution)/shard_map/ppermute | solution.py:250
  13.6 0.7 copy-start.1
  14.3 0.7 copy-start.2
  15.0 0.7 copy-start.4
  18.9 44.5 %collective-permute-start.9 = (bf16[288,2048]{1,0:T(8,128)(2,1)S(1)}, bf16[288,2048]{1,0:T(8,128)(2,1)S(1)}, u32[]{:S(2)}, u32[]{:S(2)}) collective-permute-start(bf16[288,2048]{1,0:T(8,128)(2,1)S(1)} %k_own.1.k_ref), channel_id=1, source_target_pairs={{0,16},{4,20},{24,8},{28,12},{1,17},{5,21},{25,9},{29,13},{2,18},{... | collective-permute-start | bytes 3538952 | tf_op jit(solution)/shard_map/ppermute | solution.py:260
  40.1 5.4 %collective-permute-start.8 = (bf16[144,2048]{1,0:T(8,128)(2,1)S(1)}, bf16[144,2048]{1,0:T(8,128)(2,1)S(1)}, u32[]{:S(2)}, u32[]{:S(2)}) collective-permute-start(bf16[144,2048]{1,0:T(8,128)(2,1)S(1)} %get-tuple-element.59), channel_id=1, source_target_pairs={{0,4},{4,0},{8,12},{12,8},{16,20},{20,16},{24,28},{28,24},{1,5},{5... | collective-permute-start | bytes 1769480 | tf_op jit(solution)/shard_map/ppermute | solution.py:265
  41.5 4.1 %collective-permute-start.7 = (bf16[144,2048]{1,0:T(8,128)(2,1)S(1)}, bf16[144,2048]{1,0:T(8,128)(2,1)S(1)}, u32[]{:S(2)}, u32[]{:S(2)}) collective-permute-start(bf16[144,2048]{1,0:T(8,128)(2,1)S(1)} %get-tuple-element.60), channel_id=1, source_target_pairs={{0,4},{4,0},{8,12},{12,8},{16,20},{20,16},{24,28},{28,24},{1,5},{5... | collective-permute-start | bytes 1769480 | tf_op jit(solution)/shard_map/ppermute | solution.py:265
  49.1 19.7 %collective-permute-start.10 = (bf16[144,1152]{1,0:T(8,128)(2,1)S(1)}, bf16[144,1152]{1,0:T(8,128)(2,1)S(1)}, u32[]{:S(2)}, u32[]{:S(2)}) collective-permute-start(bf16[144,1152]{1,0:T(8,128)(2,1)S(1)} %get-tuple-element.52), channel_id=1, source_target_pairs={{9,10},{13,14},{10,9},{14,13},{11,8},{15,12},{2,1},{6,5},{3,0},{7,... | collective-permute-start | bytes 995336 | tf_op jit(solution)/shard_map/ppermute | solution.py:281
  51.2 18.9 %collective-permute-start.11 = (bf16[144,1152]{1,0:T(8,128)(2,1)S(1)}, bf16[144,1152]{1,0:T(8,128)(2,1)S(1)}, u32[]{:S(2)}, u32[]{:S(2)}) collective-permute-start(bf16[144,1152]{1,0:T(8,128)(2,1)S(1)} %get-tuple-element.53), channel_id=1, source_target_pairs={{8,10},{12,14},{10,8},{14,12},{11,9},{15,13},{2,0},{6,4},{3,1},{7,... | collective-permute-start | bytes 995336 | tf_op jit(solution)/shard_map/ppermute | solution.py:281
  52.6 18.9 %collective-permute-start.12 = (bf16[144,1152]{1,0:T(8,128)(2,1)S(1)}, bf16[144,1152]{1,0:T(8,128)(2,1)S(1)}, u32[]{:S(2)}, u32[]{:S(2)}) collective-permute-start(bf16[144,1152]{1,0:T(8,128)(2,1)S(1)} %get-tuple-element.54), channel_id=1, source_target_pairs={{8,9},{12,13},{9,8},{13,12},{11,10},{15,14},{0,1},{4,5},{1,0},{5,4... | collective-permute-start | bytes 995336 | tf_op jit(solution)/shard_map/ppermute | solution.py:281
  66.3 16.0 %collective-permute-start.13 = (bf16[144,1152]{1,0:T(8,128)(2,1)S(1)}, bf16[144,1152]{1,0:T(8,128)(2,1)S(1)}, u32[]{:S(2)}, u32[]{:S(2)}) collective-permute-start(bf16[144,1152]{1,0:T(8,128)(2,1)S(1)} %get-tuple-element.55), channel_id=1, source_target_pairs={{8,3},{12,7},{9,11},{13,15},{11,2},{15,6},{19,24},{23,28},{18,16},... | collective-permute-start | bytes 995336 | tf_op jit(solution)/shard_map/ppermute | solution.py:293
  67.6 17.4 %collective-permute-start.14 = (bf16[144,1152]{1,0:T(8,128)(2,1)S(1)}, bf16[144,1152]{1,0:T(8,128)(2,1)S(1)}, u32[]{:S(2)}, u32[]{:S(2)}) collective-permute-start(bf16[144,1152]{1,0:T(8,128)(2,1)S(1)} %get-tuple-element.56), channel_id=1, source_target_pairs={{8,11},{12,15},{9,3},{13,7},{19,16},{23,20},{18,24},{22,28}} | collective-permute-start | bytes 995336 | tf_op jit(solution)/shard_map/ppermute | solution.py:293
  68.9 16.1 %collective-permute-start.15 = (bf16[144,1152]{1,0:T(8,128)(2,1)S(1)}, bf16[144,1152]{1,0:T(8,128)(2,1)S(1)}, u32[]{:S(2)}, u32[]{:S(2)}) collective-permute-start(bf16[144,1152]{1,0:T(8,128)(2,1)S(1)} %get-tuple-element.57), channel_id=1, source_target_pairs={{10,11},{14,15},{11,3},{15,7},{17,16},{21,20},{16,24},{20,28}} | collective-permute-start | bytes 995336 | tf_op jit(solution)/shard_map/ppermute | solution.py:293
  70.2 14.8 %collective-permute-start.16 = (bf16[144,1152]{1,0:T(8,128)(2,1)S(1)}, bf16[144,1152]{1,0:T(8,128)(2,1)S(1)}, u32[]{:S(2)}, u32[]{:S(2)}) collective-permute-start(bf16[144,1152]{1,0:T(8,128)(2,1)S(1)} %get-tuple-element.58), channel_id=1, source_target_pairs={{10,3},{14,7},{17,24},{21,28}} | collective-permute-start | bytes 995336 | tf_op jit(solution)/shard_map/ppermute | solution.py:293
  85.6 3.7 %collective-permute-start.17 = (f32[144,576]{1,0:T(8,128)S(1)}, f32[144,576]{1,0:T(8,128)S(1)}, u32[]{:S(2)}, u32[]{:S(2)}) collective-permute-start(f32[144,576]{1,0:T(8,128)S(1)} %get-tuple-element.61), channel_id=1, source_target_pairs={{0,4},{4,0},{8,12},{12,8},{16,20},{20,16},{24,28},{28,24},{1,5},{5... | collective-permute-start | bytes 995336 | tf_op jit(solution)/shard_map/ppermute | solution.py:297

commit v4 on v3

--- a/solution.py
+++ b/solution.py
@@ -79,7 +79,7 @@
     same = iota2((AREA, AREA), 0) // BLK == iota2((AREA, AREA), 1) % BLK
     for t in range(ntiles):
         k, flip = plane ^ (t // CORES), core ^ (t % CORES)
-        row = (flip * planes + k) * per_owner + listed_ref[0, t, 0] - t * per_owner
+        row = (flip * planes + k) * per_owner + jnp.clip(listed_ref[0, t, 0] - t * per_owner, 0, per_owner - 1)
         chosen = (pick * held[pl.ds(row, 1), :]).astype(BF16)
         full = jnp.dot(chosen, place, preferred_element_type=F32)
         wide_ref[t] = jnp.where(same, full, 0.0).astype(BF16)
@@ -124,13 +124,22 @@
     return jnp.concatenate([top[:half], top[half:], bottom[:half], bottom[half:]], axis=1)
 
 
+def arranged(top, bottom):
+    cut = far_cut(top.shape[1])
+    return jnp.concatenate([packed(top[:, :cut], bottom[:, :cut]), packed(top[:, cut:], bottom[:, cut:])], axis=1)
+
+
+def far_cut(aux):
+    return aux // 256 * 256 or aux // 2
+
+
 def dot_rows(left, right):
     return lax.dot_general(left, right, NT_DIMS, preferred_element_type=F32)
 
 
 def near_body(o_ref, p_ref, k_ref, out_ref):
     right = k_ref[...]
-    out_ref[...] = packed(dot_rows(o_ref[...], right), dot_rows(p_ref[...], right))
+    out_ref[...] = arranged(dot_rows(o_ref[...], right), dot_rows(p_ref[...], right))
 
 
 def place_of():
@@ -145,11 +154,11 @@
     top = jnp.dot(o_ref[...], right, preferred_element_type=F32)
     bottom = jnp.dot(p_ref[...], right, preferred_element_type=F32)
     terms[0] = near_ref[...]
-    terms[1] = packed(top[:, aux:], bottom[:, aux:])
-    terms[2] = packed(top[:, :aux], bottom[:, :aux])
+    terms[1] = arranged(top[:, aux:], bottom[:, aux:])
+    terms[2] = arranged(top[:, :aux], bottom[:, :aux])
     inner = kt_ref[:, :aux]
     lower = jnp.concatenate([f_ref[...], g_ref[...]], axis=0)
-    terms[3] = packed(
+    terms[3] = arranged(
         jnp.dot(e_ref[...], inner, preferred_element_type=F32), jnp.dot(lower, inner, preferred_element_type=F32)
     )
     plane, place = place_of()
@@ -189,13 +198,29 @@
         out[...] = terms[by_place(place, sent)]
 
 
+def last_body(k_ref, o_ref, p_ref, e_ref, f_ref, g_ref, held_ref, *refs):
+    first, (own_ref, s1, s2, s3, s4, terms, own_part, t1, t2, t3, t4) = refs[:5], refs[5:]
+    parts = (own_part, t1, t2, t3, t4)
+    late_body(k_ref, o_ref, p_ref, e_ref, f_ref, g_ref, held_ref, *parts, terms)
+    cut = first[0].shape[1]
+    for out, before, part in zip((own_ref, s1, s2, s3, s4), first, parts):
+        out[:, :cut] = before[...]
+        out[:, cut:] = part[...]
+
+
 def join_body(kept_ref, other_ref, out_ref):
     first = lax.axis_index("pair") % CORES == 0
     kept, other = kept_ref[...], other_ref[...]
     left, right = jnp.where(first, kept, other), jnp.where(first, other, kept)
-    half, width = left.shape[0], left.shape[1] // 2
-    out_ref[:half, :] = jnp.concatenate([left[:, :width], right[:, :width]], axis=1)
-    out_ref[half:, :] = jnp.concatenate([left[:, width:], right[:, width:]], axis=1)
+    half, aux = left.shape[0], left.shape[1] // 2
+    cut = far_cut(aux)
+    for at in range(2):
+        pieces = [
+            piece
+            for side in (left, right)
+            for piece in (side[:, at * cut:(at + 1) * cut], side[:, 2 * cut + at * (aux - cut):2 * cut + (at + 1) * (aux - cut)])
+        ]
+        out_ref[at * half:(at + 1) * half, :] = jnp.concatenate(pieces, axis=1)
 
 
 def call(body, outs, ins, scratch=(), smem=0, name=None):
@@ -257,7 +282,8 @@
     )
     partner, wide, tiles = after((partner, wide, tiles))
     k_own = call(k_own_body, shaped(aux, depth), [tiles, mix, wide], scratch_for(aux), name="k_own")
-    far = lax.ppermute(k_own, "pair", along_z([(0, 2), (3, 1)]))
+    cut = far_cut(aux)
+    far = [lax.ppermute(part, "pair", along_z([(0, 2), (3, 1)])) for part in (k_own[:cut], k_own[cut:])]
     term = (aux // 2, 4 * aux)
     near = call(near_body, shaped(*term, dtype=F32), [tiles, partner, k_own], name="near")
     outer, inner, near = after((outer, inner, near))
@@ -280,13 +306,23 @@
         moves += [((1, 3 ^ d), (0, 2))]
         arrived.append(lax.ppermute(value, both, everywhere(moves)))
 
-    far, held = after((far, held))
+    far[0], held = after((far[0], held))
+    part = (aux // 2, 4 * cut)
+    first_part = call(
+        late_body,
+        [shaped(*part, dtype=F32)] + [shaped(*part)] * 4,
+        [far[0], tiles, partner, outer, *outer_partner, held[:, :4 * cut]],
+        [pltpu.VMEM((3, *part), BF16)],
+        name="late",
+    )
+    far[1], *first_part = after((far[1], *first_part))
+    rest = (aux // 2, 4 * (aux - cut))
     own_late, *late_sent = call(
-        late_body,
+        last_body,
         [shaped(*term, dtype=F32)] + [shaped(*term)] * 4,
-        [far, tiles, partner, outer, *outer_partner, held],
-        [pltpu.VMEM((3, *term), BF16)],
-        name="late",
+        [far[1], tiles, partner, outer, *outer_partner, held[:, 4 * cut:], *first_part],
+        [pltpu.VMEM((3, *rest), BF16), pltpu.VMEM(rest, F32)] + [pltpu.VMEM(rest, BF16)] * 4,
+        name="last",
     )
     for sources, value in zip(LATE, late_sent):
         moves = [((1, g), LATE_TO[what]) for g, what in enumerate(sources) if what is not None]
@@ -294,8 +330,12 @@
     total = own_early + own_late
     for value in arrived:
         total = total + value.astype(F32)
-    other = lax.ppermute(total[:, 2 * aux:], "pair", core_swap)
-    return call(join_body, shaped(aux, 2 * aux, dtype=F32), [total[:, :2 * aux], other], name="join")
+    mine, yours = (
+        jnp.concatenate([total[:, at * 2 * cut:(at + 1) * 2 * cut], total[:, 4 * cut + at * 2 * (aux - cut):4 * cut + (at + 1) * 2 * (aux - cut)]], axis=1)
+        for at in range(2)
+    )
+    other = lax.ppermute(yours, "pair", core_swap)
+    return call(join_body, shaped(aux, 2 * aux, dtype=F32), [mine, other], name="join")
 
 
 def solution(mesh):

time: 90.7 us -> 89.3 us (0.985)
  waiting for transfers between devices: 45 us -> 38.7 us
  starting transfers between devices: 23.3 us -> 28 us
    ppermute x2 -> x3, waiting for transfers between devices: 11.3 us -> 5.06 us  [the longest x2 3.77 us: hub_plan(): lax.ppermute(part, 'pair', along_z([(0, 2), (3, 1)]))]
    ppermute x2 -> x3, starting transfers between devices: 4.55 us -> 9.26 us  [the longest x2 6.91 us: hub_plan(): lax.ppermute(part, 'pair', along_z([(0, 2), (3, 1)]))]
    pallas_call x7 -> x8, Pallas kernels: 16.1 us -> 16.1 us  [call(): pl.pallas_call(body, out_shape=outs, in_specs=[pl.BlockSpec(memory_space=...]
  transfers between devices with their start and end apart: 18 -> 19, of which waited for: 6 -> 7; matrix products, arithmetic and copies ran while one was open for 3% -> 3% of each run, Pallas kernels for 17% -> 17%
where the time goes in v4:
time: 89.3 us; the launch traced here: 88.9 us
  waiting for transfers between devices  38.7 us (43%)
  starting transfers between devices  28 us (31%)
  Pallas kernels  16.1 us (18%)
  local copies, waits for them, and re-layouts  5.41 us (6%)
    ppermute x1, waiting for transfers between devices, hub_plan(): lax.ppermute(tiles, 'pair', along_z([(0, 1), (1, 0), (2, 3), (3, 2)]))  17.4 us
    pallas_call x8, Pallas kernels, call(): pl.pallas_call(body, out_shape=outs, in_specs=[pl.BlockSpec(memory_space=...  16.1 us
    ppermute x7, waiting for transfers between devices, hub_plan(): arrived.append(lax.ppermute(value, both, everywhere(moves)))  13.5 us
    ppermute x7, starting transfers between devices, hub_plan(): arrived.append(lax.ppermute(value, both, everywhere(moves)))  9.48 us
    ppermute x2, starting transfers between devices, hub_plan(): lax.ppermute(part, 'pair', along_z([(0, 2), (3, 1)]))  6.91 us
    unnamed x17, local copies, waits for them, and re-layouts  5.06 us
    ppermute x2, waiting for transfers between devices, hub_plan(): lax.ppermute(part, 'pair', along_z([(0, 2), (3, 1)]))  3.77 us
    ppermute x3, starting transfers between devices, hub_plan(): lax.ppermute(virt_blocks, 'pair', along_z([(a, a ^ k) for a in range(4)]))  3.61 us
  transfers between devices with their start and end apart: 19, of which 7 were waited for; matrix products, arithmetic and copies ran while one was open for 3% of the time, Pallas kernels for 17%

profile of v4, /device:TPU:7, one launch (start us, length us, event | category | flops | bytes accessed | tf_op | source)
XLA Modules:
  0.0 88.9 jit_solution(13107147265021476712)
XLA Ops:
  0.0 2.3 %collective-permute-start.1 = (bf16[1,2,256]{2,1,0:T(2,128)(2,1)}, bf16[1,2,256]{2,1,0:T(2,128)(2,1)S(1)}, u32[]{:S(2)}, u32[]{:S(2)}) collective-permute-start(bf16[1,2,256]{2,1,0:T(2,128)(2,1)} %param.11), channel_id=1, source_target_pairs={{0,16},{4,20},{8,24},{12,28},{16,0},{20,4},{24,8},{28,12},{1,17},{... | collective-permute-start | bytes 3080 | tf_op jit(solution)/shard_map/ppermute | solution.py:266
  2.3 1.3 %collective-permute-start = (bf16[1,2,256]{2,1,0:T(2,128)(2,1)}, bf16[1,2,256]{2,1,0:T(2,128)(2,1)S(1)}, u32[]{:S(2)}, u32[]{:S(2)}) collective-permute-start(bf16[1,2,256]{2,1,0:T(2,128)(2,1)} %param.11), channel_id=1, source_target_pairs={{0,8},{4,12},{8,0},{12,4},{16,24},{20,28},{24,16},{28,20},{1,9},{5... | collective-permute-start | bytes 3080 | tf_op jit(solution)/shard_map/ppermute | solution.py:266
  3.6 1.6 %copy.8 = bf16[36,8,8,256]{3,1,2,0:T(8,128)(2,1)S(1)} copy(bf16[36,8,8,256]{3,2,1,0:T(8,128)(2,1)} %bitcast.10) | data formatting | bytes 2359296
  5.3 2.7 %collective-permute-done.2 = bf16[1,2,256]{2,1,0:T(2,128)(2,1)S(1)} collective-permute-done((bf16[1,2,256]{2,1,0:T(2,128)(2,1)}, bf16[1,2,256]{2,1,0:T(2,128)(2,1)S(1)}, u32[]{:S(2)}, u32[]{:S(2)}) %collective-permute-start.2) | collective-permute-done | bytes 1056 | tf_op jit(solution)/shard_map/ppermute | solution.py:266
  8.1 2.5 %collective-permute-start.4 = (bf16[4,2,256]{2,1,0:T(2,128)(2,1)S(1)}, bf16[4,2,256]{2,1,0:T(2,128)(2,1)S(1)}, u32[]{:S(2)}, u32[]{:S(2)}) collective-permute-start(bf16[4,2,256]{2,1,0:T(2,128)(2,1)S(1)} %constant_dynamic-update-slice_fusion.mine_ref), channel_id=1, source_target_pairs={{0,4},{4,0},{8,12},{12,8},{16,20},{20,16},{24,28},{28,24},{1,5},{5... | collective-permute-start | bytes 12296 | tf_op jit(solution)/shard_map/ppermute | solution.py:272
  10.6 1.7 %collective-permute-start.6 = (bf16[288,2048]{1,0:T(8,128)(2,1)S(1)}, bf16[288,2048]{1,0:T(8,128)(2,1)}, u32[]{:S(2)}, u32[]{:S(2)}) collective-permute-start(bf16[288,2048]{1,0:T(8,128)(2,1)S(1)} %bitcast.3), channel_id=1, source_target_pairs={{8,16},{12,20},{16,8},{20,12},{9,17},{13,21},{17,9},{21,13},{10,18... | collective-permute-start | bytes 3538952 | tf_op jit(solution)/shard_map/ppermute | solution.py:270
  15.7 1.4 %prep.1 = (bf16[128,128]{1,0:T(8,128)(2,1)S(1)}, bf16[8,256,256]{2,1,0:T(8,128)(2,1)S(1)}) custom-call(s32[8,8]{1,0:T(8,128)S(1)} %copy-done.1, s32[8,8]{1,0:T(8,128)S(1)} %copy-done.2, s32[1,8,1]{2,1,0:T(8,128)S(1)} %copy.7.listed_ref, bf16[16,256]{1,0:T(8,128)(2,1)S(1)} %copy-done, bf16[4,2,256]{2,1,0:T(2,128)(2,1)S(1)} %constant_dynamic-update-slice_fusion.mine_ref, ...), custom_call_target="tpu_custom_call" | custom-call | flops 1 | bytes 1 | tf_op jit(solution)/shard_map/prep/pallas_call | solution.py:227
  17.1 1.8 %k_own.1.k_ref = bf16[288,2048]{1,0:T(8,128)(2,1)S(1)} custom-call(bf16[288,2048]{1,0:T(8,128)(2,1)S(1)} %bitcast.5, bf16[128,128]{1,0:T(8,128)(2,1)S(1)} %get-tuple-element.53.mix_ref, bf16[8,256,256]{2,1,0:T(8,128)(2,1)S(1)} %get-tuple-element.54.wide_ref), custom_call_target="tpu_custom_call" | custom-call | flops 1 | bytes 1 | tf_op jit(solution)/shard_map/k_own/pallas_call | solution.py:227
  18.9 1.4 %near.1.near_ref = f32[144,1152]{1,0:T(8,128)S(1)} custom-call(bf16[288,2048]{1,0:T(8,128)(2,1)S(1)} %bitcast.6, bf16[288,2048]{1,0:T(8,128)(2,1)S(1)} %collective-permute-done.3.p_ref, bf16[288,2048]{1,0:T(8,128)(2,1)S(1)} %k_own.1.k_ref), custom_call_target="tpu_custom_call" | custom-call | flops 1 | bytes 1 | tf_op jit(solution)/shard_map/near/pallas_call | solution.py:227
  20.4 2.2 %collective-permute-start.10 = (bf16[256,2048]{1,0:T(8,128)(2,1)S(1)}, bf16[256,2048]{1,0:T(8,128)(2,1)S(1)}, u32[]{:S(2)}, u32[]{:S(2)}) collective-permute-start(bf16[256,2048]{1,0:T(8,128)(2,1)S(1)} %slice.41), channel_id=1, source_target_pairs={{0,16},{4,20},{24,8},{28,12},{1,17},{5,21},{25,9},{29,13},{2,18},{... | collective-permute-start | bytes 3145736 | tf_op jit(solution)/shard_map/ppermute | solution.py:286
  22.6 17.4 %collective-permute-done.5.outer_ref.e_ref = bf16[288,2048]{1,0:T(8,128)(2,1)S(1)} collective-permute-done((bf16[288,2048]{1,0:T(8,128)(2,1)S(1)}, bf16[288,2048]{1,0:T(8,128)(2,1)S(1)}, u32[]{:S(2)}, u32[]{:S(2)}) %collective-permute-start.5) | collective-permute-done | bytes 1179680 | tf_op jit(solution)/shard_map/ppermute | solution.py:275
  40.1 1.3 %collective-permute-start.8 = (bf16[144,2048]{1,0:T(8,128)(2,1)S(1)}, bf16[144,2048]{1,0:T(8,128)(2,1)S(1)}, u32[]{:S(2)}, u32[]{:S(2)}) collective-permute-start(bf16[144,2048]{1,0:T(8,128)(2,1)S(1)} %get-tuple-element.81), channel_id=1, source_target_pairs={{0,4},{4,0},{8,12},{12,8},{16,20},{20,16},{24,28},{28,24},{1,5},{5... | collective-permute-start | bytes 1769480 | tf_op jit(solution)/shard_map/ppermute | solution.py:291
  41.5 4.0 %k_moved.1.kt_ref = bf16[2048,576]{1,0:T(8,128)(2,1)S(1)} custom-call(bf16[288,2048]{1,0:T(8,128)(2,1)} %collective-permute-done.6.inner_ref, bf16[288,2048]{1,0:T(8,128)(2,1)S(1)} %collective-permute-done.5.outer_ref.e_ref, bf16[128,128]{1,0:T(8,128)(2,1)S(1)} %get-tuple-element.53.mix_ref, bf16[8,256,256]{2,1,0:T(8,128)(2,1)S(1)} %get-tuple-element.54.wide_ref), custom_call_target="tpu_custom_call" | custom-call | flops 1 | bytes 1 | tf_op jit(solution)/shard_map/k_moved/pallas_call | solution.py:227
  45.5 3.5 %early.1 = (f32[144,1152]{1,0:T(8,128)S(1)}, bf16[144,1152]{1,0:T(8,128)(2,1)S(1)}, bf16[144,1152]{1,0:T(8,128)(2,1)S(1)}, bf16[144,1152]{1,0:T(8,128)(2,1)S(1)}, bf16[144,1152]{1,0:T(8,128)(2,1)S(1)}) custom-call(bf16[288,2048]{1,0:T(8,128)(2,1)S(1)} %bitcast.7, bf16[288,2048]{1,0:T(8,128)(2,1)S(1)} %collective-permute-done.3.p_ref, ...), custom_call_target="tpu_custom_call" | custom-call | flops 1 | bytes 1 | tf_op jit(solution)/shard_map/early/pallas_call | solution.py:227
  49.0 2.1 %collective-permute-start.11 = (bf16[144,1152]{1,0:T(8,128)(2,1)S(1)}, bf16[144,1152]{1,0:T(8,128)(2,1)S(1)}, u32[]{:S(2)}, u32[]{:S(2)}) collective-permute-start(bf16[144,1152]{1,0:T(8,128)(2,1)S(1)} %get-tuple-element.74), channel_id=1, source_target_pairs={{9,10},{13,14},{10,9},{14,13},{11,8},{15,12},{2,1},{6,5},{3,0},{7,... | collective-permute-start | bytes 995336 | tf_op jit(solution)/shard_map/ppermute | solution.py:307
  51.1 1.3 %collective-permute-start.12 = (bf16[144,1152]{1,0:T(8,128)(2,1)S(1)}, bf16[144,1152]{1,0:T(8,128)(2,1)S(1)}, u32[]{:S(2)}, u32[]{:S(2)}) collective-permute-start(bf16[144,1152]{1,0:T(8,128)(2,1)S(1)} %get-tuple-element.75), channel_id=1, source_target_pairs={{8,10},{12,14},{10,8},{14,12},{11,9},{15,13},{2,0},{6,4},{3,1},{7,... | collective-permute-start | bytes 995336 | tf_op jit(solution)/shard_map/ppermute | solution.py:307
  52.5 4.7 %collective-permute-start.9 = (bf16[32,2048]{1,0:T(8,128)(2,1)S(1)}, bf16[32,2048]{1,0:T(8,128)(2,1)S(1)}, u32[]{:S(2)}, u32[]{:S(2)}) collective-permute-start(bf16[32,2048]{1,0:T(8,128)(2,1)S(1)} %slice.40), channel_id=1, source_target_pairs={{0,16},{4,20},{24,8},{28,12},{1,17},{5,21},{25,9},{29,13},{2,18},{... | collective-permute-start | bytes 393224 | tf_op jit(solution)/shard_map/ppermute | solution.py:286
  58.1 2.5 %collective-permute-done.10.k_ref = bf16[256,2048]{1,0:T(8,128)(2,1)S(1)} collective-permute-done((bf16[256,2048]{1,0:T(8,128)(2,1)S(1)}, bf16[256,2048]{1,0:T(8,128)(2,1)S(1)}, u32[]{:S(2)}, u32[]{:S(2)}) %collective-permute-start.10) | collective-permute-done | bytes 1048608 | tf_op jit(solution)/shard_map/ppermute | solution.py:286
  60.6 1.5 %late.1 = (f32[144,1024]{1,0:T(8,128)S(1)}, bf16[144,1024]{1,0:T(8,128)(2,1)S(1)}, bf16[144,1024]{1,0:T(8,128)(2,1)S(1)}, bf16[144,1024]{1,0:T(8,128)(2,1)S(1)}, bf16[144,1024]{1,0:T(8,128)(2,1)S(1)}) custom-call(bf16[256,2048]{1,0:T(8,128)(2,1)S(1)} %collective-permute-done.10.k_ref, bf16[288,2048]{1,0:T(8,128)(2,1)S(1)} %bitcast.8, ...), custom_call_target="tpu_custom_call" | custom-call | flops 1 | bytes 1 | tf_op jit(solution)/shard_map/late/pallas_call | solution.py:227
  63.4 1.5 %last.1 = (f32[144,1152]{1,0:T(8,128)S(1)}, bf16[144,1152]{1,0:T(8,128)(2,1)S(1)}, bf16[144,1152]{1,0:T(8,128)(2,1)S(1)}, bf16[144,1152]{1,0:T(8,128)(2,1)S(1)}, bf16[144,1152]{1,0:T(8,128)(2,1)S(1)}) custom-call(bf16[32,2048]{1,0:T(8,128)(2,1)S(1)} %collective-permute-done.9.k_ref, bf16[288,2048]{1,0:T(8,128)(2,1)S(1)} %bitcast.9, ...), custom_call_target="tpu_custom_call" | custom-call | flops 1 | bytes 1 | tf_op jit(solution)/shard_map/last/pallas_call | solution.py:227
  67.5 1.3 %collective-permute-start.16 = (bf16[144,1152]{1,0:T(8,128)(2,1)S(1)}, bf16[144,1152]{1,0:T(8,128)(2,1)S(1)}, u32[]{:S(2)}, u32[]{:S(2)}) collective-permute-start(bf16[144,1152]{1,0:T(8,128)(2,1)S(1)} %get-tuple-element.79), channel_id=1, source_target_pairs={{10,11},{14,15},{11,3},{15,7},{17,16},{21,20},{16,24},{20,28}} | collective-permute-start | bytes 995336 | tf_op jit(solution)/shard_map/ppermute | solution.py:329
  70.1 10.7 %collective-permute-done.14 = bf16[144,1152]{1,0:T(8,128)(2,1)S(1)} collective-permute-done((bf16[144,1152]{1,0:T(8,128)(2,1)S(1)}, bf16[144,1152]{1,0:T(8,128)(2,1)S(1)}, u32[]{:S(2)}, u32[]{:S(2)}) %collective-permute-start.14) | collective-permute-done | bytes 331808 | tf_op jit(solution)/shard_map/ppermute | solution.py:329
  80.8 2.8 %collective-permute-done.15 = bf16[144,1152]{1,0:T(8,128)(2,1)S(1)} collective-permute-done((bf16[144,1152]{1,0:T(8,128)(2,1)S(1)}, bf16[144,1152]{1,0:T(8,128)(2,1)S(1)}, u32[]{:S(2)}, u32[]{:S(2)}) %collective-permute-start.15) | collective-permute-done | bytes 331808 | tf_op jit(solution)/shard_map/ppermute | solution.py:329
  84.1 2.4 %collective-permute-start.18 = (f32[144,576]{1,0:T(8,128)S(1)}, f32[144,576]{1,0:T(8,128)S(1)}, u32[]{:S(2)}, u32[]{:S(2)}) collective-permute-start(f32[144,576]{1,0:T(8,128)S(1)} %pad_maximum_fusion.1), channel_id=1, source_target_pairs={{0,4},{4,0},{8,12},{12,8},{16,20},{20,16},{24,28},{28,24},{1,5},{5... | collective-permute-start | bytes 995336 | tf_op jit(solution)/shard_map/ppermute | solution.py:337
  (50 shorter events, 12.7 us)
Async XLA Ops:
  0.0 5.3 %collective-permute-start.1 = (bf16[1,2,256]{2,1,0:T(2,128)(2,1)}, bf16[1,2,256]{2,1,0:T(2,128)(2,1)S(1)}, u32[]{:S(2)}, u32[]{:S(2)}) collective-permute-start(bf16[1,2,256]{2,1,0:T(2,128)(2,1)} %param.11), channel_id=1, source_target_pairs={{0,16},{4,20},{8,24},{12,28},{16,0},{20,4},{24,8},{28,12},{1,17},{... | collective-permute-start | bytes 3080 | tf_op jit(solution)/shard_map/ppermute | solution.py:266
  2.3 3.0 %collective-permute-start = (bf16[1,2,256]{2,1,0:T(2,128)(2,1)}, bf16[1,2,256]{2,1,0:T(2,128)(2,1)S(1)}, u32[]{:S(2)}, u32[]{:S(2)}) collective-permute-start(bf16[1,2,256]{2,1,0:T(2,128)(2,1)} %param.11), channel_id=1, source_target_pairs={{0,8},{4,12},{8,0},{12,4},{16,24},{20,28},{24,16},{28,20},{1,9},{5... | collective-permute-start | bytes 3080 | tf_op jit(solution)/shard_map/ppermute | solution.py:266
  3.6 4.4 %collective-permute-start.2 = (bf16[1,2,256]{2,1,0:T(2,128)(2,1)}, bf16[1,2,256]{2,1,0:T(2,128)(2,1)S(1)}, u32[]{:S(2)}, u32[]{:S(2)}) collective-permute-start(bf16[1,2,256]{2,1,0:T(2,128)(2,1)} %param.11), channel_id=1, source_target_pairs={{0,24},{4,28},{8,16},{12,20},{16,8},{20,12},{24,0},{28,4},{1,25},{... | collective-permute-start | bytes 3080 | tf_op jit(solution)/shard_map/ppermute | solution.py:266
  3.6 4.4 %copy-start.5 = (bf16[1,2,256]{2,1,0:T(2,128)(2,1)S(1)}, bf16[1,2,256]{2,1,0:T(2,128)(2,1)}, u32[]{:S(2)}) copy-start(bf16[1,2,256]{2,1,0:T(2,128)(2,1)} %param.11) | copy-start | bytes 3076
  3.6 10.0 %copy-start = (bf16[16,256]{1,0:T(8,128)(2,1)S(1)}, bf16[16,256]{1,0:T(8,128)(2,1)}, u32[]{:S(2)}) copy-start(bf16[16,256]{1,0:T(8,128)(2,1)} %blocks_ref.1) | copy-start | bytes 24580
  8.1 4.2 %collective-permute-start.4 = (bf16[4,2,256]{2,1,0:T(2,128)(2,1)S(1)}, bf16[4,2,256]{2,1,0:T(2,128)(2,1)S(1)}, u32[]{:S(2)}, u32[]{:S(2)}) collective-permute-start(bf16[4,2,256]{2,1,0:T(2,128)(2,1)S(1)} %constant_dynamic-update-slice_fusion.mine_ref), channel_id=1, source_target_pairs={{0,4},{4,0},{8,12},{12,8},{16,20},{20,16},{24,28},{28,24},{1,5},{5... | collective-permute-start | bytes 12296 | tf_op jit(solution)/shard_map/ppermute | solution.py:272
  10.5 6.6 %collective-permute-start.3 = (bf16[288,2048]{1,0:T(8,128)(2,1)S(1)}, bf16[288,2048]{1,0:T(8,128)(2,1)S(1)}, u32[]{:S(2)}, u32[]{:S(2)}) collective-permute-start(bf16[288,2048]{1,0:T(8,128)(2,1)S(1)} %bitcast.2), channel_id=1, source_target_pairs={{0,4},{4,0},{8,12},{12,8},{16,20},{20,16},{24,28},{28,24},{1,5},{5... | collective-permute-start | bytes 3538952 | tf_op jit(solution)/shard_map/ppermute | solution.py:273
  10.6 12.0 %collective-permute-start.6 = (bf16[288,2048]{1,0:T(8,128)(2,1)S(1)}, bf16[288,2048]{1,0:T(8,128)(2,1)}, u32[]{:S(2)}, u32[]{:S(2)}) collective-permute-start(bf16[288,2048]{1,0:T(8,128)(2,1)S(1)} %bitcast.3), channel_id=1, source_target_pairs={{8,16},{12,20},{16,8},{20,12},{9,17},{13,21},{17,9},{21,13},{10,18... | collective-permute-start | bytes 3538952 | tf_op jit(solution)/shard_map/ppermute | solution.py:270
  12.9 27.1 %collective-permute-start.5 = (bf16[288,2048]{1,0:T(8,128)(2,1)S(1)}, bf16[288,2048]{1,0:T(8,128)(2,1)S(1)}, u32[]{:S(2)}, u32[]{:S(2)}) collective-permute-start(bf16[288,2048]{1,0:T(8,128)(2,1)S(1)} %bitcast.4), channel_id=1, source_target_pairs={{0,8},{4,12},{8,0},{12,4},{16,24},{20,28},{24,16},{28,20},{1,9},{5... | collective-permute-start | bytes 3538952 | tf_op jit(solution)/shard_map/ppermute | solution.py:275
  13.6 0.7 copy-start.1
  14.3 0.7 copy-start.2
  15.0 0.7 copy-start.4
  20.4 40.2 %collective-permute-start.10 = (bf16[256,2048]{1,0:T(8,128)(2,1)S(1)}, bf16[256,2048]{1,0:T(8,128)(2,1)S(1)}, u32[]{:S(2)}, u32[]{:S(2)}) collective-permute-start(bf16[256,2048]{1,0:T(8,128)(2,1)S(1)} %slice.41), channel_id=1, source_target_pairs={{0,16},{4,20},{24,8},{28,12},{1,17},{5,21},{25,9},{29,13},{2,18},{... | collective-permute-start | bytes 3145736 | tf_op jit(solution)/shard_map/ppermute | solution.py:286
  40.1 5.4 %collective-permute-start.8 = (bf16[144,2048]{1,0:T(8,128)(2,1)S(1)}, bf16[144,2048]{1,0:T(8,128)(2,1)S(1)}, u32[]{:S(2)}, u32[]{:S(2)}) collective-permute-start(bf16[144,2048]{1,0:T(8,128)(2,1)S(1)} %get-tuple-element.81), channel_id=1, source_target_pairs={{0,4},{4,0},{8,12},{12,8},{16,20},{20,16},{24,28},{28,24},{1,5},{5... | collective-permute-start | bytes 1769480 | tf_op jit(solution)/shard_map/ppermute | solution.py:291
  41.4 4.1 %collective-permute-start.7 = (bf16[144,2048]{1,0:T(8,128)(2,1)S(1)}, bf16[144,2048]{1,0:T(8,128)(2,1)S(1)}, u32[]{:S(2)}, u32[]{:S(2)}) collective-permute-start(bf16[144,2048]{1,0:T(8,128)(2,1)S(1)} %get-tuple-element.82), channel_id=1, source_target_pairs={{0,4},{4,0},{8,12},{12,8},{16,20},{20,16},{24,28},{28,24},{1,5},{5... | collective-permute-start | bytes 1769480 | tf_op jit(solution)/shard_map/ppermute | solution.py:291
  49.0 18.4 %collective-permute-start.11 = (bf16[144,1152]{1,0:T(8,128)(2,1)S(1)}, bf16[144,1152]{1,0:T(8,128)(2,1)S(1)}, u32[]{:S(2)}, u32[]{:S(2)}) collective-permute-start(bf16[144,1152]{1,0:T(8,128)(2,1)S(1)} %get-tuple-element.74), channel_id=1, source_target_pairs={{9,10},{13,14},{10,9},{14,13},{11,8},{15,12},{2,1},{6,5},{3,0},{7,... | collective-permute-start | bytes 995336 | tf_op jit(solution)/shard_map/ppermute | solution.py:307
  51.1 17.6 %collective-permute-start.12 = (bf16[144,1152]{1,0:T(8,128)(2,1)S(1)}, bf16[144,1152]{1,0:T(8,128)(2,1)S(1)}, u32[]{:S(2)}, u32[]{:S(2)}) collective-permute-start(bf16[144,1152]{1,0:T(8,128)(2,1)S(1)} %get-tuple-element.75), channel_id=1, source_target_pairs={{8,10},{12,14},{10,8},{14,12},{11,9},{15,13},{2,0},{6,4},{3,1},{7,... | collective-permute-start | bytes 995336 | tf_op jit(solution)/shard_map/ppermute | solution.py:307
  52.5 10.9 %collective-permute-start.9 = (bf16[32,2048]{1,0:T(8,128)(2,1)S(1)}, bf16[32,2048]{1,0:T(8,128)(2,1)S(1)}, u32[]{:S(2)}, u32[]{:S(2)}) collective-permute-start(bf16[32,2048]{1,0:T(8,128)(2,1)S(1)} %slice.40), channel_id=1, source_target_pairs={{0,16},{4,20},{24,8},{28,12},{1,17},{5,21},{25,9},{29,13},{2,18},{... | collective-permute-start | bytes 393224 | tf_op jit(solution)/shard_map/ppermute | solution.py:286
  57.2 12.9 %collective-permute-start.13 = (bf16[144,1152]{1,0:T(8,128)(2,1)S(1)}, bf16[144,1152]{1,0:T(8,128)(2,1)S(1)}, u32[]{:S(2)}, u32[]{:S(2)}) collective-permute-start(bf16[144,1152]{1,0:T(8,128)(2,1)S(1)} %get-tuple-element.76), channel_id=1, source_target_pairs={{8,9},{12,13},{9,8},{13,12},{11,10},{15,14},{0,1},{4,5},{1,0},{5,4... | collective-permute-start | bytes 995336 | tf_op jit(solution)/shard_map/ppermute | solution.py:307
  64.9 16.0 %collective-permute-start.14 = (bf16[144,1152]{1,0:T(8,128)(2,1)S(1)}, bf16[144,1152]{1,0:T(8,128)(2,1)S(1)}, u32[]{:S(2)}, u32[]{:S(2)}) collective-permute-start(bf16[144,1152]{1,0:T(8,128)(2,1)S(1)} %get-tuple-element.77), channel_id=1, source_target_pairs={{8,3},{12,7},{9,11},{13,15},{11,2},{15,6},{19,24},{23,28},{18,16},... | collective-permute-start | bytes 995336 | tf_op jit(solution)/shard_map/ppermute | solution.py:329
  66.2 17.4 %collective-permute-start.15 = (bf16[144,1152]{1,0:T(8,128)(2,1)S(1)}, bf16[144,1152]{1,0:T(8,128)(2,1)S(1)}, u32[]{:S(2)}, u32[]{:S(2)}) collective-permute-start(bf16[144,1152]{1,0:T(8,128)(2,1)S(1)} %get-tuple-element.78), channel_id=1, source_target_pairs={{8,11},{12,15},{9,3},{13,7},{19,16},{23,20},{18,24},{22,28}} | collective-permute-start | bytes 995336 | tf_op jit(solution)/shard_map/ppermute | solution.py:329
  67.5 16.1 %collective-permute-start.16 = (bf16[144,1152]{1,0:T(8,128)(2,1)S(1)}, bf16[144,1152]{1,0:T(8,128)(2,1)S(1)}, u32[]{:S(2)}, u32[]{:S(2)}) collective-permute-start(bf16[144,1152]{1,0:T(8,128)(2,1)S(1)} %get-tuple-element.79), channel_id=1, source_target_pairs={{10,11},{14,15},{11,3},{15,7},{17,16},{21,20},{16,24},{20,28}} | collective-permute-start | bytes 995336 | tf_op jit(solution)/shard_map/ppermute | solution.py:329
  68.8 14.8 %collective-permute-start.17 = (bf16[144,1152]{1,0:T(8,128)(2,1)S(1)}, bf16[144,1152]{1,0:T(8,128)(2,1)S(1)}, u32[]{:S(2)}, u32[]{:S(2)}) collective-permute-start(bf16[144,1152]{1,0:T(8,128)(2,1)S(1)} %get-tuple-element.80), channel_id=1, source_target_pairs={{10,3},{14,7},{17,24},{21,28}} | collective-permute-start | bytes 995336 | tf_op jit(solution)/shard_map/ppermute | solution.py:329
  84.1 3.7 %collective-permute-start.18 = (f32[144,576]{1,0:T(8,128)S(1)}, f32[144,576]{1,0:T(8,128)S(1)}, u32[]{:S(2)}, u32[]{:S(2)}) collective-permute-start(f32[144,576]{1,0:T(8,128)S(1)} %pad_maximum_fusion.1), channel_id=1, source_target_pairs={{0,4},{4,0},{8,12},{12,8},{16,20},{20,16},{24,28},{28,24},{1,5},{5... | collective-permute-start | bytes 995336 | tf_op jit(solution)/shard_map/ppermute | solution.py:337
  (1 other events, 0.6 us)

commit v5 on v4

--- a/solution.py
+++ b/solution.py
@@ -208,6 +208,18 @@
         out[:, cut:] = part[...]
 
 
+def sum_body(*refs):
+    values, sides = refs[:-2], refs[-2:]
+    width = sides[0].shape[1]
+    cut = far_cut(width // 2)
+    for at, side in enumerate(sides):
+        for start, size, to in ((at * 2 * cut, 2 * cut, 0), (4 * cut + at * (width - 2 * cut), width - 2 * cut, 2 * cut)):
+            total = values[0][:, start:start + size]
+            for value in values[1:]:
+                total = total + value[:, start:start + size].astype(F32)
+            side[:, to:to + size] = total
+
+
 def join_body(kept_ref, other_ref, out_ref):
     first = lax.axis_index("pair") % CORES == 0
     kept, other = kept_ref[...], other_ref[...]
@@ -277,7 +289,10 @@
         prep_body,
         [shaped(ntiles * BLK, ntiles * BLK), shaped(ntiles, area, area)],
         [occ_src, occ_block, virt_block, occ_blocks, mine, theirs],
-        [pltpu.VMEM((occ_blocks.shape[0], BLK, ntiles * BLK), F32), pltpu.VMEM((16, area), F32)],
+        [
+            pltpu.VMEM((occ_blocks.shape[0], BLK, ntiles * BLK), F32),
+            pltpu.VMEM((CORES * mine.shape[0] * mine.shape[1], area), F32),
+        ],
         smem=3, name="prep",
     )
     partner, wide, tiles = after((partner, wide, tiles))
@@ -327,12 +342,8 @@
     for sources, value in zip(LATE, late_sent):
         moves = [((1, g), LATE_TO[what]) for g, what in enumerate(sources) if what is not None]
         arrived.append(lax.ppermute(value, both, everywhere(moves)))
-    total = own_early + own_late
-    for value in arrived:
-        total = total + value.astype(F32)
-    mine, yours = (
-        jnp.concatenate([total[:, at * 2 * cut:(at + 1) * 2 * cut], total[:, 4 * cut + at * 2 * (aux - cut):4 * cut + (at + 1) * 2 * (aux - cut)]], axis=1)
-        for at in range(2)
+    mine, yours = call(
+        sum_body, [shaped(aux // 2, 2 * aux, dtype=F32)] * 2, [own_early, own_late, *arrived], name="sum"
     )
     other = lax.ppermute(yours, "pair", core_swap)
     return call(join_body, shaped(aux, 2 * aux, dtype=F32), [mine, other], name="join")
@@ -347,8 +358,11 @@
         P("red", None, None),
         P("red", "pair", None),
     )
-    small = mesh.shape["pair"] == 8 and mesh.shape["red"] == 4
-    return jax.shard_map(
-        hub_plan if small else gather_plan,
-        mesh=mesh, in_specs=placed, out_specs=P("pair", "red"), check_vma=False,
-    )
+    line = mesh.shape["pair"] == 4 * CORES and mesh.shape["red"] == 4
+
+    def shards(three_center, occ_src, occ_block, occ_blocks, virt_block, virt_blocks):
+        owned = virt_block.shape[2] == 1 and virt_block.shape[1] == mesh.shape["pair"]
+        plan = hub_plan if line and owned and three_center.shape[0] % 32 == 0 else gather_plan
+        return plan(three_center, occ_src, occ_block, occ_blocks, virt_block, virt_blocks)
+
+    return jax.shard_map(shards, mesh=mesh, in_specs=placed, out_specs=P("pair", "red"), check_vma=False)

time: 89.3 us -> 89.3 us (level)
    pallas_call x8 -> x9, Pallas kernels: 16.1 us -> 16.6 us  [call(): pl.pallas_call(body, out_shape=outs, in_specs=[pl.BlockSpec(memory_space=...]
where the time goes in v5:
time: 89.3 us; the launch traced here: 88.8 us
  waiting for transfers between devices  38.7 us (43%)
  starting transfers between devices  27.9 us (31%)
  Pallas kernels  16.6 us (19%)
  local copies, waits for them, and re-layouts  5.29 us (6%)
    ppermute x1, waiting for transfers between devices, hub_plan(): lax.ppermute(tiles, 'pair', along_z([(0, 1), (1, 0), (2, 3), (3, 2)]))  17.4 us
    pallas_call x9, Pallas kernels, call(): pl.pallas_call(body, out_shape=outs, in_specs=[pl.BlockSpec(memory_space=...  16.6 us
    ppermute x7, waiting for transfers between devices, hub_plan(): arrived.append(lax.ppermute(value, both, everywhere(moves)))  13.5 us
    ppermute x7, starting transfers between devices, hub_plan(): arrived.append(lax.ppermute(value, both, everywhere(moves)))  9.47 us
    ppermute x2, starting transfers between devices, hub_plan(): lax.ppermute(part, 'pair', along_z([(0, 2), (3, 1)]))  6.89 us
    unnamed x17, local copies, waits for them, and re-layouts  5.06 us
    ppermute x2, waiting for transfers between devices, hub_plan(): lax.ppermute(part, 'pair', along_z([(0, 2), (3, 1)]))  3.78 us
    ppermute x3, starting transfers between devices, hub_plan(): lax.ppermute(virt_blocks, 'pair', along_z([(a, a ^ k) for a in range(4)]))  3.61 us
  transfers between devices with their start and end apart: 19, of which 7 were waited for; matrix products, arithmetic and copies ran while one was open for 3% of the time, Pallas kernels for 17%

profile of v5, /device:TPU:7, one launch (start us, length us, event | category | flops | bytes accessed | tf_op | source)
XLA Modules:
  0.0 88.8 jit_solution(14619937659520956388)
XLA Ops:
  0.0 2.3 %collective-permute-start.1 = (bf16[1,2,256]{2,1,0:T(2,128)(2,1)}, bf16[1,2,256]{2,1,0:T(2,128)(2,1)S(1)}, u32[]{:S(2)}, u32[]{:S(2)}) collective-permute-start(bf16[1,2,256]{2,1,0:T(2,128)(2,1)} %param.11), channel_id=1, source_target_pairs={{0,16},{4,20},{8,24},{12,28},{16,0},{20,4},{24,8},{28,12},{1,17},{... | collective-permute-start | bytes 3080 | tf_op jit(solution)/shard_map/ppermute | solution.py:278
  2.3 1.3 %collective-permute-start = (bf16[1,2,256]{2,1,0:T(2,128)(2,1)}, bf16[1,2,256]{2,1,0:T(2,128)(2,1)S(1)}, u32[]{:S(2)}, u32[]{:S(2)}) collective-permute-start(bf16[1,2,256]{2,1,0:T(2,128)(2,1)} %param.11), channel_id=1, source_target_pairs={{0,8},{4,12},{8,0},{12,4},{16,24},{20,28},{24,16},{28,20},{1,9},{5... | collective-permute-start | bytes 3080 | tf_op jit(solution)/shard_map/ppermute | solution.py:278
  3.6 1.6 %copy.8 = bf16[36,8,8,256]{3,1,2,0:T(8,128)(2,1)S(1)} copy(bf16[36,8,8,256]{3,2,1,0:T(8,128)(2,1)} %bitcast.10) | data formatting | bytes 2359296
  5.3 2.7 %collective-permute-done.2 = bf16[1,2,256]{2,1,0:T(2,128)(2,1)S(1)} collective-permute-done((bf16[1,2,256]{2,1,0:T(2,128)(2,1)}, bf16[1,2,256]{2,1,0:T(2,128)(2,1)S(1)}, u32[]{:S(2)}, u32[]{:S(2)}) %collective-permute-start.2) | collective-permute-done | bytes 1056 | tf_op jit(solution)/shard_map/ppermute | solution.py:278
  8.1 2.5 %collective-permute-start.4 = (bf16[4,2,256]{2,1,0:T(2,128)(2,1)S(1)}, bf16[4,2,256]{2,1,0:T(2,128)(2,1)S(1)}, u32[]{:S(2)}, u32[]{:S(2)}) collective-permute-start(bf16[4,2,256]{2,1,0:T(2,128)(2,1)S(1)} %constant_dynamic-update-slice_fusion.mine_ref), channel_id=1, source_target_pairs={{0,4},{4,0},{8,12},{12,8},{16,20},{20,16},{24,28},{28,24},{1,5},{5... | collective-permute-start | bytes 12296 | tf_op jit(solution)/shard_map/ppermute | solution.py:284
  10.6 1.7 %collective-permute-start.6 = (bf16[288,2048]{1,0:T(8,128)(2,1)S(1)}, bf16[288,2048]{1,0:T(8,128)(2,1)}, u32[]{:S(2)}, u32[]{:S(2)}) collective-permute-start(bf16[288,2048]{1,0:T(8,128)(2,1)S(1)} %bitcast.3), channel_id=1, source_target_pairs={{8,16},{12,20},{16,8},{20,12},{9,17},{13,21},{17,9},{21,13},{10,18... | collective-permute-start | bytes 3538952 | tf_op jit(solution)/shard_map/ppermute | solution.py:282
  15.7 1.4 %prep.1 = (bf16[128,128]{1,0:T(8,128)(2,1)S(1)}, bf16[8,256,256]{2,1,0:T(8,128)(2,1)S(1)}) custom-call(s32[8,8]{1,0:T(8,128)S(1)} %copy-done.1, s32[8,8]{1,0:T(8,128)S(1)} %copy-done.2, s32[1,8,1]{2,1,0:T(8,128)S(1)} %copy.7.listed_ref, bf16[16,256]{1,0:T(8,128)(2,1)S(1)} %copy-done, bf16[4,2,256]{2,1,0:T(2,128)(2,1)S(1)} %constant_dynamic-update-slice_fusion.mine_ref, ...), custom_call_target="tpu_custom_call" | custom-call | flops 1 | bytes 1 | tf_op jit(solution)/shard_map/prep/pallas_call | solution.py:239
  17.1 1.8 %k_own.1.k_ref = bf16[288,2048]{1,0:T(8,128)(2,1)S(1)} custom-call(bf16[288,2048]{1,0:T(8,128)(2,1)S(1)} %bitcast.5, bf16[128,128]{1,0:T(8,128)(2,1)S(1)} %get-tuple-element.55.mix_ref, bf16[8,256,256]{2,1,0:T(8,128)(2,1)S(1)} %get-tuple-element.56.wide_ref), custom_call_target="tpu_custom_call" | custom-call | flops 1 | bytes 1 | tf_op jit(solution)/shard_map/k_own/pallas_call | solution.py:239
  18.9 1.4 %near.1.near_ref = f32[144,1152]{1,0:T(8,128)S(1)} custom-call(bf16[288,2048]{1,0:T(8,128)(2,1)S(1)} %bitcast.6, bf16[288,2048]{1,0:T(8,128)(2,1)S(1)} %collective-permute-done.3.p_ref, bf16[288,2048]{1,0:T(8,128)(2,1)S(1)} %k_own.1.k_ref), custom_call_target="tpu_custom_call" | custom-call | flops 1 | bytes 1 | tf_op jit(solution)/shard_map/near/pallas_call | solution.py:239
  20.4 2.2 %collective-permute-start.10 = (bf16[256,2048]{1,0:T(8,128)(2,1)S(1)}, bf16[256,2048]{1,0:T(8,128)(2,1)S(1)}, u32[]{:S(2)}, u32[]{:S(2)}) collective-permute-start(bf16[256,2048]{1,0:T(8,128)(2,1)S(1)} %slice.25), channel_id=1, source_target_pairs={{0,16},{4,20},{24,8},{28,12},{1,17},{5,21},{25,9},{29,13},{2,18},{... | collective-permute-start | bytes 3145736 | tf_op jit(solution)/shard_map/ppermute | solution.py:301
  22.6 17.4 %collective-permute-done.5.outer_ref.e_ref = bf16[288,2048]{1,0:T(8,128)(2,1)S(1)} collective-permute-done((bf16[288,2048]{1,0:T(8,128)(2,1)S(1)}, bf16[288,2048]{1,0:T(8,128)(2,1)S(1)}, u32[]{:S(2)}, u32[]{:S(2)}) %collective-permute-start.5) | collective-permute-done | bytes 1179680 | tf_op jit(solution)/shard_map/ppermute | solution.py:287
  40.1 1.3 %collective-permute-start.8 = (bf16[144,2048]{1,0:T(8,128)(2,1)S(1)}, bf16[144,2048]{1,0:T(8,128)(2,1)S(1)}, u32[]{:S(2)}, u32[]{:S(2)}) collective-permute-start(bf16[144,2048]{1,0:T(8,128)(2,1)S(1)} %get-tuple-element.85), channel_id=1, source_target_pairs={{0,4},{4,0},{8,12},{12,8},{16,20},{20,16},{24,28},{28,24},{1,5},{5... | collective-permute-start | bytes 1769480 | tf_op jit(solution)/shard_map/ppermute | solution.py:306
  41.5 4.0 %k_moved.1.kt_ref = bf16[2048,576]{1,0:T(8,128)(2,1)S(1)} custom-call(bf16[288,2048]{1,0:T(8,128)(2,1)} %collective-permute-done.6.inner_ref, bf16[288,2048]{1,0:T(8,128)(2,1)S(1)} %collective-permute-done.5.outer_ref.e_ref, bf16[128,128]{1,0:T(8,128)(2,1)S(1)} %get-tuple-element.55.mix_ref, bf16[8,256,256]{2,1,0:T(8,128)(2,1)S(1)} %get-tuple-element.56.wide_ref), custom_call_target="tpu_custom_call" | custom-call | flops 1 | bytes 1 | tf_op jit(solution)/shard_map/k_moved/pallas_call | solution.py:239
  45.5 3.5 %early.1 = (f32[144,1152]{1,0:T(8,128)S(1)}, bf16[144,1152]{1,0:T(8,128)(2,1)S(1)}, bf16[144,1152]{1,0:T(8,128)(2,1)S(1)}, bf16[144,1152]{1,0:T(8,128)(2,1)S(1)}, bf16[144,1152]{1,0:T(8,128)(2,1)S(1)}) custom-call(bf16[288,2048]{1,0:T(8,128)(2,1)S(1)} %bitcast.7, bf16[288,2048]{1,0:T(8,128)(2,1)S(1)} %collective-permute-done.3.p_ref, ...), custom_call_target="tpu_custom_call" | custom-call | flops 1 | bytes 1 | tf_op jit(solution)/shard_map/early/pallas_call | solution.py:239
  49.0 2.1 %collective-permute-start.11 = (bf16[144,1152]{1,0:T(8,128)(2,1)S(1)}, bf16[144,1152]{1,0:T(8,128)(2,1)S(1)}, u32[]{:S(2)}, u32[]{:S(2)}) collective-permute-start(bf16[144,1152]{1,0:T(8,128)(2,1)S(1)} %get-tuple-element.76), channel_id=1, source_target_pairs={{9,10},{13,14},{10,9},{14,13},{11,8},{15,12},{2,1},{6,5},{3,0},{7,... | collective-permute-start | bytes 995336 | tf_op jit(solution)/shard_map/ppermute | solution.py:322
  51.2 1.3 %collective-permute-start.12 = (bf16[144,1152]{1,0:T(8,128)(2,1)S(1)}, bf16[144,1152]{1,0:T(8,128)(2,1)S(1)}, u32[]{:S(2)}, u32[]{:S(2)}) collective-permute-start(bf16[144,1152]{1,0:T(8,128)(2,1)S(1)} %get-tuple-element.77), channel_id=1, source_target_pairs={{8,10},{12,14},{10,8},{14,12},{11,9},{15,13},{2,0},{6,4},{3,1},{7,... | collective-permute-start | bytes 995336 | tf_op jit(solution)/shard_map/ppermute | solution.py:322
  52.5 4.7 %collective-permute-start.9 = (bf16[32,2048]{1,0:T(8,128)(2,1)S(1)}, bf16[32,2048]{1,0:T(8,128)(2,1)S(1)}, u32[]{:S(2)}, u32[]{:S(2)}) collective-permute-start(bf16[32,2048]{1,0:T(8,128)(2,1)S(1)} %slice.24), channel_id=1, source_target_pairs={{0,16},{4,20},{24,8},{28,12},{1,17},{5,21},{25,9},{29,13},{2,18},{... | collective-permute-start | bytes 393224 | tf_op jit(solution)/shard_map/ppermute | solution.py:301
  58.1 2.5 %collective-permute-done.10.k_ref = bf16[256,2048]{1,0:T(8,128)(2,1)S(1)} collective-permute-done((bf16[256,2048]{1,0:T(8,128)(2,1)S(1)}, bf16[256,2048]{1,0:T(8,128)(2,1)S(1)}, u32[]{:S(2)}, u32[]{:S(2)}) %collective-permute-start.10) | collective-permute-done | bytes 1048608 | tf_op jit(solution)/shard_map/ppermute | solution.py:301
  60.6 1.5 %late.1 = (f32[144,1024]{1,0:T(8,128)S(1)}, bf16[144,1024]{1,0:T(8,128)(2,1)S(1)}, bf16[144,1024]{1,0:T(8,128)(2,1)S(1)}, bf16[144,1024]{1,0:T(8,128)(2,1)S(1)}, bf16[144,1024]{1,0:T(8,128)(2,1)S(1)}) custom-call(bf16[256,2048]{1,0:T(8,128)(2,1)S(1)} %collective-permute-done.10.k_ref, bf16[288,2048]{1,0:T(8,128)(2,1)S(1)} %bitcast.8, ...), custom_call_target="tpu_custom_call" | custom-call | flops 1 | bytes 1 | tf_op jit(solution)/shard_map/late/pallas_call | solution.py:239
  63.4 1.5 %last.1 = (f32[144,1152]{1,0:T(8,128)S(1)}, bf16[144,1152]{1,0:T(8,128)(2,1)S(1)}, bf16[144,1152]{1,0:T(8,128)(2,1)S(1)}, bf16[144,1152]{1,0:T(8,128)(2,1)S(1)}, bf16[144,1152]{1,0:T(8,128)(2,1)S(1)}) custom-call(bf16[32,2048]{1,0:T(8,128)(2,1)S(1)} %collective-permute-done.9.k_ref, bf16[288,2048]{1,0:T(8,128)(2,1)S(1)} %bitcast.9, ...), custom_call_target="tpu_custom_call" | custom-call | flops 1 | bytes 1 | tf_op jit(solution)/shard_map/last/pallas_call | solution.py:239
  70.1 10.7 %collective-permute-done.14.refs_5_ = bf16[144,1152]{1,0:T(8,128)(2,1)S(1)} collective-permute-done((bf16[144,1152]{1,0:T(8,128)(2,1)S(1)}, bf16[144,1152]{1,0:T(8,128)(2,1)S(1)}, u32[]{:S(2)}, u32[]{:S(2)}) %collective-permute-start.14) | collective-permute-done | bytes 331808 | tf_op jit(solution)/shard_map/ppermute | solution.py:344
  80.8 2.8 %collective-permute-done.15.refs_6_ = bf16[144,1152]{1,0:T(8,128)(2,1)S(1)} collective-permute-done((bf16[144,1152]{1,0:T(8,128)(2,1)S(1)}, bf16[144,1152]{1,0:T(8,128)(2,1)S(1)}, u32[]{:S(2)}, u32[]{:S(2)}) %collective-permute-start.15) | collective-permute-done | bytes 331808 | tf_op jit(solution)/shard_map/ppermute | solution.py:344
  84.1 2.4 %collective-permute-start.18 = (f32[144,576]{1,0:T(8,128)S(1)}, f32[144,576]{1,0:T(8,128)S(1)}, u32[]{:S(2)}, u32[]{:S(2)}) collective-permute-start(f32[144,576]{1,0:T(8,128)S(1)} %get-tuple-element.84), channel_id=1, source_target_pairs={{0,4},{4,0},{8,12},{12,8},{16,20},{20,16},{24,28},{28,24},{1,5},{5... | collective-permute-start | bytes 995336 | tf_op jit(solution)/shard_map/ppermute | solution.py:348
  86.5 1.3 %collective-permute-done.18.other_ref = f32[144,576]{1,0:T(8,128)S(1)} collective-permute-done((f32[144,576]{1,0:T(8,128)S(1)}, f32[144,576]{1,0:T(8,128)S(1)}, u32[]{:S(2)}, u32[]{:S(2)}) %collective-permute-start.18) | collective-permute-done | bytes 331808 | tf_op jit(solution)/shard_map/ppermute | solution.py:348
  (46 shorter events, 12.7 us)
Async XLA Ops:
  0.0 5.3 %collective-permute-start.1 = (bf16[1,2,256]{2,1,0:T(2,128)(2,1)}, bf16[1,2,256]{2,1,0:T(2,128)(2,1)S(1)}, u32[]{:S(2)}, u32[]{:S(2)}) collective-permute-start(bf16[1,2,256]{2,1,0:T(2,128)(2,1)} %param.11), channel_id=1, source_target_pairs={{0,16},{4,20},{8,24},{12,28},{16,0},{20,4},{24,8},{28,12},{1,17},{... | collective-permute-start | bytes 3080 | tf_op jit(solution)/shard_map/ppermute | solution.py:278
  2.3 3.0 %collective-permute-start = (bf16[1,2,256]{2,1,0:T(2,128)(2,1)}, bf16[1,2,256]{2,1,0:T(2,128)(2,1)S(1)}, u32[]{:S(2)}, u32[]{:S(2)}) collective-permute-start(bf16[1,2,256]{2,1,0:T(2,128)(2,1)} %param.11), channel_id=1, source_target_pairs={{0,8},{4,12},{8,0},{12,4},{16,24},{20,28},{24,16},{28,20},{1,9},{5... | collective-permute-start | bytes 3080 | tf_op jit(solution)/shard_map/ppermute | solution.py:278
  3.6 4.4 %collective-permute-start.2 = (bf16[1,2,256]{2,1,0:T(2,128)(2,1)}, bf16[1,2,256]{2,1,0:T(2,128)(2,1)S(1)}, u32[]{:S(2)}, u32[]{:S(2)}) collective-permute-start(bf16[1,2,256]{2,1,0:T(2,128)(2,1)} %param.11), channel_id=1, source_target_pairs={{0,24},{4,28},{8,16},{12,20},{16,8},{20,12},{24,0},{28,4},{1,25},{... | collective-permute-start | bytes 3080 | tf_op jit(solution)/shard_map/ppermute | solution.py:278
  3.6 4.4 %copy-start.5 = (bf16[1,2,256]{2,1,0:T(2,128)(2,1)S(1)}, bf16[1,2,256]{2,1,0:T(2,128)(2,1)}, u32[]{:S(2)}) copy-start(bf16[1,2,256]{2,1,0:T(2,128)(2,1)} %param.11) | copy-start | bytes 3076
  3.6 10.0 %copy-start = (bf16[16,256]{1,0:T(8,128)(2,1)S(1)}, bf16[16,256]{1,0:T(8,128)(2,1)}, u32[]{:S(2)}) copy-start(bf16[16,256]{1,0:T(8,128)(2,1)} %blocks_ref.1) | copy-start | bytes 24580
  8.1 4.2 %collective-permute-start.4 = (bf16[4,2,256]{2,1,0:T(2,128)(2,1)S(1)}, bf16[4,2,256]{2,1,0:T(2,128)(2,1)S(1)}, u32[]{:S(2)}, u32[]{:S(2)}) collective-permute-start(bf16[4,2,256]{2,1,0:T(2,128)(2,1)S(1)} %constant_dynamic-update-slice_fusion.mine_ref), channel_id=1, source_target_pairs={{0,4},{4,0},{8,12},{12,8},{16,20},{20,16},{24,28},{28,24},{1,5},{5... | collective-permute-start | bytes 12296 | tf_op jit(solution)/shard_map/ppermute | solution.py:284
  10.5 6.6 %collective-permute-start.3 = (bf16[288,2048]{1,0:T(8,128)(2,1)S(1)}, bf16[288,2048]{1,0:T(8,128)(2,1)S(1)}, u32[]{:S(2)}, u32[]{:S(2)}) collective-permute-start(bf16[288,2048]{1,0:T(8,128)(2,1)S(1)} %bitcast.2), channel_id=1, source_target_pairs={{0,4},{4,0},{8,12},{12,8},{16,20},{20,16},{24,28},{28,24},{1,5},{5... | collective-permute-start | bytes 3538952 | tf_op jit(solution)/shard_map/ppermute | solution.py:285
  10.6 12.0 %collective-permute-start.6 = (bf16[288,2048]{1,0:T(8,128)(2,1)S(1)}, bf16[288,2048]{1,0:T(8,128)(2,1)}, u32[]{:S(2)}, u32[]{:S(2)}) collective-permute-start(bf16[288,2048]{1,0:T(8,128)(2,1)S(1)} %bitcast.3), channel_id=1, source_target_pairs={{8,16},{12,20},{16,8},{20,12},{9,17},{13,21},{17,9},{21,13},{10,18... | collective-permute-start | bytes 3538952 | tf_op jit(solution)/shard_map/ppermute | solution.py:282
  12.9 27.1 %collective-permute-start.5 = (bf16[288,2048]{1,0:T(8,128)(2,1)S(1)}, bf16[288,2048]{1,0:T(8,128)(2,1)S(1)}, u32[]{:S(2)}, u32[]{:S(2)}) collective-permute-start(bf16[288,2048]{1,0:T(8,128)(2,1)S(1)} %bitcast.4), channel_id=1, source_target_pairs={{0,8},{4,12},{8,0},{12,4},{16,24},{20,28},{24,16},{28,20},{1,9},{5... | collective-permute-start | bytes 3538952 | tf_op jit(solution)/shard_map/ppermute | solution.py:287
  13.6 0.7 copy-start.1
  14.3 0.7 copy-start.2
  15.0 0.7 copy-start.4
  20.4 40.2 %collective-permute-start.10 = (bf16[256,2048]{1,0:T(8,128)(2,1)S(1)}, bf16[256,2048]{1,0:T(8,128)(2,1)S(1)}, u32[]{:S(2)}, u32[]{:S(2)}) collective-permute-start(bf16[256,2048]{1,0:T(8,128)(2,1)S(1)} %slice.25), channel_id=1, source_target_pairs={{0,16},{4,20},{24,8},{28,12},{1,17},{5,21},{25,9},{29,13},{2,18},{... | collective-permute-start | bytes 3145736 | tf_op jit(solution)/shard_map/ppermute | solution.py:301
  40.1 5.4 %collective-permute-start.8 = (bf16[144,2048]{1,0:T(8,128)(2,1)S(1)}, bf16[144,2048]{1,0:T(8,128)(2,1)S(1)}, u32[]{:S(2)}, u32[]{:S(2)}) collective-permute-start(bf16[144,2048]{1,0:T(8,128)(2,1)S(1)} %get-tuple-element.85), channel_id=1, source_target_pairs={{0,4},{4,0},{8,12},{12,8},{16,20},{20,16},{24,28},{28,24},{1,5},{5... | collective-permute-start | bytes 1769480 | tf_op jit(solution)/shard_map/ppermute | solution.py:306
  41.4 4.1 %collective-permute-start.7 = (bf16[144,2048]{1,0:T(8,128)(2,1)S(1)}, bf16[144,2048]{1,0:T(8,128)(2,1)S(1)}, u32[]{:S(2)}, u32[]{:S(2)}) collective-permute-start(bf16[144,2048]{1,0:T(8,128)(2,1)S(1)} %get-tuple-element.86), channel_id=1, source_target_pairs={{0,4},{4,0},{8,12},{12,8},{16,20},{20,16},{24,28},{28,24},{1,5},{5... | collective-permute-start | bytes 1769480 | tf_op jit(solution)/shard_map/ppermute | solution.py:306
  49.0 18.4 %collective-permute-start.11 = (bf16[144,1152]{1,0:T(8,128)(2,1)S(1)}, bf16[144,1152]{1,0:T(8,128)(2,1)S(1)}, u32[]{:S(2)}, u32[]{:S(2)}) collective-permute-start(bf16[144,1152]{1,0:T(8,128)(2,1)S(1)} %get-tuple-element.76), channel_id=1, source_target_pairs={{9,10},{13,14},{10,9},{14,13},{11,8},{15,12},{2,1},{6,5},{3,0},{7,... | collective-permute-start | bytes 995336 | tf_op jit(solution)/shard_map/ppermute | solution.py:322
  51.2 17.6 %collective-permute-start.12 = (bf16[144,1152]{1,0:T(8,128)(2,1)S(1)}, bf16[144,1152]{1,0:T(8,128)(2,1)S(1)}, u32[]{:S(2)}, u32[]{:S(2)}) collective-permute-start(bf16[144,1152]{1,0:T(8,128)(2,1)S(1)} %get-tuple-element.77), channel_id=1, source_target_pairs={{8,10},{12,14},{10,8},{14,12},{11,9},{15,13},{2,0},{6,4},{3,1},{7,... | collective-permute-start | bytes 995336 | tf_op jit(solution)/shard_map/ppermute | solution.py:322
  52.5 10.9 %collective-permute-start.9 = (bf16[32,2048]{1,0:T(8,128)(2,1)S(1)}, bf16[32,2048]{1,0:T(8,128)(2,1)S(1)}, u32[]{:S(2)}, u32[]{:S(2)}) collective-permute-start(bf16[32,2048]{1,0:T(8,128)(2,1)S(1)} %slice.24), channel_id=1, source_target_pairs={{0,16},{4,20},{24,8},{28,12},{1,17},{5,21},{25,9},{29,13},{2,18},{... | collective-permute-start | bytes 393224 | tf_op jit(solution)/shard_map/ppermute | solution.py:301
  57.2 12.9 %collective-permute-start.13 = (bf16[144,1152]{1,0:T(8,128)(2,1)S(1)}, bf16[144,1152]{1,0:T(8,128)(2,1)S(1)}, u32[]{:S(2)}, u32[]{:S(2)}) collective-permute-start(bf16[144,1152]{1,0:T(8,128)(2,1)S(1)} %get-tuple-element.78), channel_id=1, source_target_pairs={{8,9},{12,13},{9,8},{13,12},{11,10},{15,14},{0,1},{4,5},{1,0},{5,4... | collective-permute-start | bytes 995336 | tf_op jit(solution)/shard_map/ppermute | solution.py:322
  64.9 16.0 %collective-permute-start.14 = (bf16[144,1152]{1,0:T(8,128)(2,1)S(1)}, bf16[144,1152]{1,0:T(8,128)(2,1)S(1)}, u32[]{:S(2)}, u32[]{:S(2)}) collective-permute-start(bf16[144,1152]{1,0:T(8,128)(2,1)S(1)} %get-tuple-element.79), channel_id=1, source_target_pairs={{8,3},{12,7},{9,11},{13,15},{11,2},{15,6},{19,24},{23,28},{18,16},... | collective-permute-start | bytes 995336 | tf_op jit(solution)/shard_map/ppermute | solution.py:344
  66.2 17.4 %collective-permute-start.15 = (bf16[144,1152]{1,0:T(8,128)(2,1)S(1)}, bf16[144,1152]{1,0:T(8,128)(2,1)S(1)}, u32[]{:S(2)}, u32[]{:S(2)}) collective-permute-start(bf16[144,1152]{1,0:T(8,128)(2,1)S(1)} %get-tuple-element.80), channel_id=1, source_target_pairs={{8,11},{12,15},{9,3},{13,7},{19,16},{23,20},{18,24},{22,28}} | collective-permute-start | bytes 995336 | tf_op jit(solution)/shard_map/ppermute | solution.py:344
  67.5 16.1 %collective-permute-start.16 = (bf16[144,1152]{1,0:T(8,128)(2,1)S(1)}, bf16[144,1152]{1,0:T(8,128)(2,1)S(1)}, u32[]{:S(2)}, u32[]{:S(2)}) collective-permute-start(bf16[144,1152]{1,0:T(8,128)(2,1)S(1)} %get-tuple-element.81), channel_id=1, source_target_pairs={{10,11},{14,15},{11,3},{15,7},{17,16},{21,20},{16,24},{20,28}} | collective-permute-start | bytes 995336 | tf_op jit(solution)/shard_map/ppermute | solution.py:344
  68.8 14.8 %collective-permute-start.17 = (bf16[144,1152]{1,0:T(8,128)(2,1)S(1)}, bf16[144,1152]{1,0:T(8,128)(2,1)S(1)}, u32[]{:S(2)}, u32[]{:S(2)}) collective-permute-start(bf16[144,1152]{1,0:T(8,128)(2,1)S(1)} %get-tuple-element.82), channel_id=1, source_target_pairs={{10,3},{14,7},{17,24},{21,28}} | collective-permute-start | bytes 995336 | tf_op jit(solution)/shard_map/ppermute | solution.py:344
  84.1 3.7 %collective-permute-start.18 = (f32[144,576]{1,0:T(8,128)S(1)}, f32[144,576]{1,0:T(8,128)S(1)}, u32[]{:S(2)}, u32[]{:S(2)}) collective-permute-start(f32[144,576]{1,0:T(8,128)S(1)} %get-tuple-element.84), channel_id=1, source_target_pairs={{0,4},{4,0},{8,12},{12,8},{16,20},{20,16},{24,28},{28,24},{1,5},{5... | collective-permute-start | bytes 995336 | tf_op jit(solution)/shard_map/ppermute | solution.py:348
  (1 other events, 0.6 us)

commit v6 on v5

--- a/solution.py
+++ b/solution.py
@@ -279,7 +279,7 @@
     ]
     tiles = three_center.reshape(aux, depth)
     *from_planes, tiles = after((*from_planes, tiles))
-    inner = lax.ppermute(tiles, "pair", along_z([(1, 2), (2, 1)]))
+    inner = lax.ppermute(tiles, "pair", along_z([(1, 2), (2, 1)]) + [(0, 1), (1, 0), (6, 7), (7, 6)])
     mine = jnp.concatenate(from_planes)
     theirs = lax.ppermute(mine, "pair", core_swap)
     partner = lax.ppermute(tiles, "pair", core_swap)

time: 89.3 us -> 88.4 us (0.990)
  starting transfers between devices: 27.9 us -> 25.2 us
  waiting for transfers between devices: 38.7 us -> 40.6 us
    ppermute x1, starting transfers between devices: 1.68 us -> 0.43 us  [hub_plan(): lax.ppermute(tiles, 'pair', along_z([(1, 2), (2, 1)]) + [(0, 1), (1, 0),...]
    ppermute x2, waiting for transfers between devices: 3.78 us -> 4.85 us  [hub_plan(): lax.ppermute(part, 'pair', along_z([(0, 2), (3, 1)]))]
    ppermute x2, starting transfers between devices: 6.89 us -> 5.91 us  [hub_plan(): lax.ppermute(part, 'pair', along_z([(0, 2), (3, 1)]))]
  transfers between devices with their start and end apart: 19 -> 19, of which waited for: 7 -> 8; matrix products, arithmetic and copies ran while one was open for 3% -> 3% of each run, Pallas kernels for 17% -> 17%
where the time goes in v6:
time: 88.4 us; the launch traced here: 88 us
  waiting for transfers between devices  40.6 us (46%)
  starting transfers between devices  25.2 us (29%)
  Pallas kernels  16.6 us (19%)
  local copies, waits for them, and re-layouts  5.29 us (6%)
    ppermute x1, waiting for transfers between devices, hub_plan(): lax.ppermute(tiles, 'pair', along_z([(0, 1), (1, 0), (2, 3), (3, 2)]))  17.5 us
    pallas_call x9, Pallas kernels, call(): pl.pallas_call(body, out_shape=outs, in_specs=[pl.BlockSpec(memory_space=...  16.6 us
    ppermute x7, waiting for transfers between devices, hub_plan(): arrived.append(lax.ppermute(value, both, everywhere(moves)))  13.9 us
    ppermute x7, starting transfers between devices, hub_plan(): arrived.append(lax.ppermute(value, both, everywhere(moves)))  9.49 us
    ppermute x2, starting transfers between devices, hub_plan(): lax.ppermute(part, 'pair', along_z([(0, 2), (3, 1)]))  5.91 us
    unnamed x17, local copies, waits for them, and re-layouts  5.06 us
    ppermute x2, waiting for transfers between devices, hub_plan(): lax.ppermute(part, 'pair', along_z([(0, 2), (3, 1)]))  4.85 us
    ppermute x3, starting transfers between devices, hub_plan(): lax.ppermute(virt_blocks, 'pair', along_z([(a, a ^ k) for a in range(4)]))  3.61 us
  transfers between devices with their start and end apart: 19, of which 8 were waited for; matrix products, arithmetic and copies ran while one was open for 3% of the time, Pallas kernels for 17%

profile of v6, /device:TPU:7, one launch (start us, length us, event | category | flops | bytes accessed | tf_op | source)
XLA Modules:
  0.0 88.0 jit_solution(234257963827855825)
XLA Ops:
  0.0 2.3 %collective-permute-start.1 = (bf16[1,2,256]{2,1,0:T(2,128)(2,1)}, bf16[1,2,256]{2,1,0:T(2,128)(2,1)S(1)}, u32[]{:S(2)}, u32[]{:S(2)}) collective-permute-start(bf16[1,2,256]{2,1,0:T(2,128)(2,1)} %param.11), channel_id=1, source_target_pairs={{0,16},{4,20},{8,24},{12,28},{16,0},{20,4},{24,8},{28,12},{1,17},{... | collective-permute-start | bytes 3080 | tf_op jit(solution)/shard_map/ppermute | solution.py:278
  2.3 1.3 %collective-permute-start = (bf16[1,2,256]{2,1,0:T(2,128)(2,1)}, bf16[1,2,256]{2,1,0:T(2,128)(2,1)S(1)}, u32[]{:S(2)}, u32[]{:S(2)}) collective-permute-start(bf16[1,2,256]{2,1,0:T(2,128)(2,1)} %param.11), channel_id=1, source_target_pairs={{0,8},{4,12},{8,0},{12,4},{16,24},{20,28},{24,16},{28,20},{1,9},{5... | collective-permute-start | bytes 3080 | tf_op jit(solution)/shard_map/ppermute | solution.py:278
  3.6 1.6 %copy.8 = bf16[36,8,8,256]{3,1,2,0:T(8,128)(2,1)S(1)} copy(bf16[36,8,8,256]{3,2,1,0:T(8,128)(2,1)} %bitcast.10) | data formatting | bytes 2359296
  5.3 2.7 %collective-permute-done.2 = bf16[1,2,256]{2,1,0:T(2,128)(2,1)S(1)} collective-permute-done((bf16[1,2,256]{2,1,0:T(2,128)(2,1)}, bf16[1,2,256]{2,1,0:T(2,128)(2,1)S(1)}, u32[]{:S(2)}, u32[]{:S(2)}) %collective-permute-start.2) | collective-permute-done | bytes 1056 | tf_op jit(solution)/shard_map/ppermute | solution.py:278
  8.1 2.5 %collective-permute-start.4 = (bf16[4,2,256]{2,1,0:T(2,128)(2,1)S(1)}, bf16[4,2,256]{2,1,0:T(2,128)(2,1)S(1)}, u32[]{:S(2)}, u32[]{:S(2)}) collective-permute-start(bf16[4,2,256]{2,1,0:T(2,128)(2,1)S(1)} %constant_dynamic-update-slice_fusion.mine_ref), channel_id=1, source_target_pairs={{0,4},{4,0},{8,12},{12,8},{16,20},{20,16},{24,28},{28,24},{1,5},{5... | collective-permute-start | bytes 12296 | tf_op jit(solution)/shard_map/ppermute | solution.py:284
  14.7 1.4 %prep.1 = (bf16[128,128]{1,0:T(8,128)(2,1)S(1)}, bf16[8,256,256]{2,1,0:T(8,128)(2,1)S(1)}) custom-call(s32[8,8]{1,0:T(8,128)S(1)} %copy-done.1, s32[8,8]{1,0:T(8,128)S(1)} %copy-done.2, s32[1,8,1]{2,1,0:T(8,128)S(1)} %copy.7.listed_ref, bf16[16,256]{1,0:T(8,128)(2,1)S(1)} %copy-done, bf16[4,2,256]{2,1,0:T(2,128)(2,1)S(1)} %constant_dynamic-update-slice_fusion.mine_ref, ...), custom_call_target="tpu_custom_call" | custom-call | flops 1 | bytes 1 | tf_op jit(solution)/shard_map/prep/pallas_call | solution.py:239
  16.2 1.8 %k_own.1.k_ref = bf16[288,2048]{1,0:T(8,128)(2,1)S(1)} custom-call(bf16[288,2048]{1,0:T(8,128)(2,1)S(1)} %bitcast.5, bf16[128,128]{1,0:T(8,128)(2,1)S(1)} %get-tuple-element.55.mix_ref, bf16[8,256,256]{2,1,0:T(8,128)(2,1)S(1)} %get-tuple-element.56.wide_ref), custom_call_target="tpu_custom_call" | custom-call | flops 1 | bytes 1 | tf_op jit(solution)/shard_map/k_own/pallas_call | solution.py:239
  17.9 1.4 %near.1.near_ref = f32[144,1152]{1,0:T(8,128)S(1)} custom-call(bf16[288,2048]{1,0:T(8,128)(2,1)S(1)} %bitcast.6, bf16[288,2048]{1,0:T(8,128)(2,1)S(1)} %collective-permute-done.3.p_ref, bf16[288,2048]{1,0:T(8,128)(2,1)S(1)} %k_own.1.k_ref), custom_call_target="tpu_custom_call" | custom-call | flops 1 | bytes 1 | tf_op jit(solution)/shard_map/near/pallas_call | solution.py:239
  19.5 2.2 %collective-permute-start.10 = (bf16[256,2048]{1,0:T(8,128)(2,1)S(1)}, bf16[256,2048]{1,0:T(8,128)(2,1)S(1)}, u32[]{:S(2)}, u32[]{:S(2)}) collective-permute-start(bf16[256,2048]{1,0:T(8,128)(2,1)S(1)} %slice.25), channel_id=1, source_target_pairs={{0,16},{4,20},{24,8},{28,12},{1,17},{5,21},{25,9},{29,13},{2,18},{... | collective-permute-start | bytes 3145736 | tf_op jit(solution)/shard_map/ppermute | solution.py:301
  21.7 17.5 %collective-permute-done.5.outer_ref.e_ref = bf16[288,2048]{1,0:T(8,128)(2,1)S(1)} collective-permute-done((bf16[288,2048]{1,0:T(8,128)(2,1)S(1)}, bf16[288,2048]{1,0:T(8,128)(2,1)S(1)}, u32[]{:S(2)}, u32[]{:S(2)}) %collective-permute-start.5) | collective-permute-done | bytes 1179680 | tf_op jit(solution)/shard_map/ppermute | solution.py:287
  40.6 4.0 %k_moved.1.kt_ref = bf16[2048,576]{1,0:T(8,128)(2,1)S(1)} custom-call(bf16[288,2048]{1,0:T(8,128)(2,1)} %collective-permute-done.6.inner_ref, bf16[288,2048]{1,0:T(8,128)(2,1)S(1)} %collective-permute-done.5.outer_ref.e_ref, bf16[128,128]{1,0:T(8,128)(2,1)S(1)} %get-tuple-element.55.mix_ref, bf16[8,256,256]{2,1,0:T(8,128)(2,1)S(1)} %get-tuple-element.56.wide_ref), custom_call_target="tpu_custom_call" | custom-call | flops 1 | bytes 1 | tf_op jit(solution)/shard_map/k_moved/pallas_call | solution.py:239
  44.5 3.5 %early.1 = (f32[144,1152]{1,0:T(8,128)S(1)}, bf16[144,1152]{1,0:T(8,128)(2,1)S(1)}, bf16[144,1152]{1,0:T(8,128)(2,1)S(1)}, bf16[144,1152]{1,0:T(8,128)(2,1)S(1)}, bf16[144,1152]{1,0:T(8,128)(2,1)S(1)}) custom-call(bf16[288,2048]{1,0:T(8,128)(2,1)S(1)} %bitcast.7, bf16[288,2048]{1,0:T(8,128)(2,1)S(1)} %collective-permute-done.3.p_ref, ...), custom_call_target="tpu_custom_call" | custom-call | flops 1 | bytes 1 | tf_op jit(solution)/shard_map/early/pallas_call | solution.py:239
  48.1 2.1 %collective-permute-start.11 = (bf16[144,1152]{1,0:T(8,128)(2,1)S(1)}, bf16[144,1152]{1,0:T(8,128)(2,1)S(1)}, u32[]{:S(2)}, u32[]{:S(2)}) collective-permute-start(bf16[144,1152]{1,0:T(8,128)(2,1)S(1)} %get-tuple-element.76), channel_id=1, source_target_pairs={{9,10},{13,14},{10,9},{14,13},{11,8},{15,12},{2,1},{6,5},{3,0},{7,... | collective-permute-start | bytes 995336 | tf_op jit(solution)/shard_map/ppermute | solution.py:322
  50.2 1.3 %collective-permute-start.12 = (bf16[144,1152]{1,0:T(8,128)(2,1)S(1)}, bf16[144,1152]{1,0:T(8,128)(2,1)S(1)}, u32[]{:S(2)}, u32[]{:S(2)}) collective-permute-start(bf16[144,1152]{1,0:T(8,128)(2,1)S(1)} %get-tuple-element.77), channel_id=1, source_target_pairs={{8,10},{12,14},{10,8},{14,12},{11,9},{15,13},{2,0},{6,4},{3,1},{7,... | collective-permute-start | bytes 995336 | tf_op jit(solution)/shard_map/ppermute | solution.py:322
  51.6 3.7 %collective-permute-start.9 = (bf16[32,2048]{1,0:T(8,128)(2,1)S(1)}, bf16[32,2048]{1,0:T(8,128)(2,1)S(1)}, u32[]{:S(2)}, u32[]{:S(2)}) collective-permute-start(bf16[32,2048]{1,0:T(8,128)(2,1)S(1)} %slice.24), channel_id=1, source_target_pairs={{0,16},{4,20},{24,8},{28,12},{1,17},{5,21},{25,9},{29,13},{2,18},{... | collective-permute-start | bytes 393224 | tf_op jit(solution)/shard_map/ppermute | solution.py:301
  56.2 3.6 %collective-permute-done.10.k_ref = bf16[256,2048]{1,0:T(8,128)(2,1)S(1)} collective-permute-done((bf16[256,2048]{1,0:T(8,128)(2,1)S(1)}, bf16[256,2048]{1,0:T(8,128)(2,1)S(1)}, u32[]{:S(2)}, u32[]{:S(2)}) %collective-permute-start.10) | collective-permute-done | bytes 1048608 | tf_op jit(solution)/shard_map/ppermute | solution.py:301
  59.8 1.5 %late.1 = (f32[144,1024]{1,0:T(8,128)S(1)}, bf16[144,1024]{1,0:T(8,128)(2,1)S(1)}, bf16[144,1024]{1,0:T(8,128)(2,1)S(1)}, bf16[144,1024]{1,0:T(8,128)(2,1)S(1)}, bf16[144,1024]{1,0:T(8,128)(2,1)S(1)}) custom-call(bf16[256,2048]{1,0:T(8,128)(2,1)S(1)} %collective-permute-done.10.k_ref, bf16[288,2048]{1,0:T(8,128)(2,1)S(1)} %bitcast.8, ...), custom_call_target="tpu_custom_call" | custom-call | flops 1 | bytes 1 | tf_op jit(solution)/shard_map/late/pallas_call | solution.py:239
  62.6 1.5 %last.1 = (f32[144,1152]{1,0:T(8,128)S(1)}, bf16[144,1152]{1,0:T(8,128)(2,1)S(1)}, bf16[144,1152]{1,0:T(8,128)(2,1)S(1)}, bf16[144,1152]{1,0:T(8,128)(2,1)S(1)}, bf16[144,1152]{1,0:T(8,128)(2,1)S(1)}) custom-call(bf16[32,2048]{1,0:T(8,128)(2,1)S(1)} %collective-permute-done.9.k_ref, bf16[288,2048]{1,0:T(8,128)(2,1)S(1)} %bitcast.9, ...), custom_call_target="tpu_custom_call" | custom-call | flops 1 | bytes 1 | tf_op jit(solution)/shard_map/last/pallas_call | solution.py:239
  64.0 1.3 %collective-permute-start.14 = (bf16[144,1152]{1,0:T(8,128)(2,1)S(1)}, bf16[144,1152]{1,0:T(8,128)(2,1)S(1)}, u32[]{:S(2)}, u32[]{:S(2)}) collective-permute-start(bf16[144,1152]{1,0:T(8,128)(2,1)S(1)} %get-tuple-element.79), channel_id=1, source_target_pairs={{8,3},{12,7},{9,11},{13,15},{11,2},{15,6},{19,24},{23,28},{18,16},... | collective-permute-start | bytes 995336 | tf_op jit(solution)/shard_map/ppermute | solution.py:344
  65.3 1.3 %collective-permute-start.15 = (bf16[144,1152]{1,0:T(8,128)(2,1)S(1)}, bf16[144,1152]{1,0:T(8,128)(2,1)S(1)}, u32[]{:S(2)}, u32[]{:S(2)}) collective-permute-start(bf16[144,1152]{1,0:T(8,128)(2,1)S(1)} %get-tuple-element.80), channel_id=1, source_target_pairs={{8,11},{12,15},{9,3},{13,7},{19,16},{23,20},{18,24},{22,28}} | collective-permute-start | bytes 995336 | tf_op jit(solution)/shard_map/ppermute | solution.py:344
  69.3 11.1 %collective-permute-done.14.refs_5_ = bf16[144,1152]{1,0:T(8,128)(2,1)S(1)} collective-permute-done((bf16[144,1152]{1,0:T(8,128)(2,1)S(1)}, bf16[144,1152]{1,0:T(8,128)(2,1)S(1)}, u32[]{:S(2)}, u32[]{:S(2)}) %collective-permute-start.14) | collective-permute-done | bytes 331808 | tf_op jit(solution)/shard_map/ppermute | solution.py:344
  80.4 2.8 %collective-permute-done.15.refs_6_ = bf16[144,1152]{1,0:T(8,128)(2,1)S(1)} collective-permute-done((bf16[144,1152]{1,0:T(8,128)(2,1)S(1)}, bf16[144,1152]{1,0:T(8,128)(2,1)S(1)}, u32[]{:S(2)}, u32[]{:S(2)}) %collective-permute-start.15) | collective-permute-done | bytes 331808 | tf_op jit(solution)/shard_map/ppermute | solution.py:344
  83.7 2.0 %collective-permute-start.18 = (f32[144,576]{1,0:T(8,128)S(1)}, f32[144,576]{1,0:T(8,128)S(1)}, u32[]{:S(2)}, u32[]{:S(2)}) collective-permute-start(f32[144,576]{1,0:T(8,128)S(1)} %get-tuple-element.84), channel_id=1, source_target_pairs={{0,4},{4,0},{8,12},{12,8},{16,20},{20,16},{24,28},{28,24},{1,5},{5... | collective-permute-start | bytes 995336 | tf_op jit(solution)/shard_map/ppermute | solution.py:348
  85.6 1.3 %collective-permute-done.18.other_ref = f32[144,576]{1,0:T(8,128)S(1)} collective-permute-done((f32[144,576]{1,0:T(8,128)S(1)}, f32[144,576]{1,0:T(8,128)S(1)}, u32[]{:S(2)}, u32[]{:S(2)}) %collective-permute-start.18) | collective-permute-done | bytes 331808 | tf_op jit(solution)/shard_map/ppermute | solution.py:348
  (46 shorter events, 12.1 us)
Async XLA Ops:
  0.0 5.3 %collective-permute-start.1 = (bf16[1,2,256]{2,1,0:T(2,128)(2,1)}, bf16[1,2,256]{2,1,0:T(2,128)(2,1)S(1)}, u32[]{:S(2)}, u32[]{:S(2)}) collective-permute-start(bf16[1,2,256]{2,1,0:T(2,128)(2,1)} %param.11), channel_id=1, source_target_pairs={{0,16},{4,20},{8,24},{12,28},{16,0},{20,4},{24,8},{28,12},{1,17},{... | collective-permute-start | bytes 3080 | tf_op jit(solution)/shard_map/ppermute | solution.py:278
  2.3 3.0 %collective-permute-start = (bf16[1,2,256]{2,1,0:T(2,128)(2,1)}, bf16[1,2,256]{2,1,0:T(2,128)(2,1)S(1)}, u32[]{:S(2)}, u32[]{:S(2)}) collective-permute-start(bf16[1,2,256]{2,1,0:T(2,128)(2,1)} %param.11), channel_id=1, source_target_pairs={{0,8},{4,12},{8,0},{12,4},{16,24},{20,28},{24,16},{28,20},{1,9},{5... | collective-permute-start | bytes 3080 | tf_op jit(solution)/shard_map/ppermute | solution.py:278
  3.6 4.4 %collective-permute-start.2 = (bf16[1,2,256]{2,1,0:T(2,128)(2,1)}, bf16[1,2,256]{2,1,0:T(2,128)(2,1)S(1)}, u32[]{:S(2)}, u32[]{:S(2)}) collective-permute-start(bf16[1,2,256]{2,1,0:T(2,128)(2,1)} %param.11), channel_id=1, source_target_pairs={{0,24},{4,28},{8,16},{12,20},{16,8},{20,12},{24,0},{28,4},{1,25},{... | collective-permute-start | bytes 3080 | tf_op jit(solution)/shard_map/ppermute | solution.py:278
  3.6 4.4 %copy-start.5 = (bf16[1,2,256]{2,1,0:T(2,128)(2,1)S(1)}, bf16[1,2,256]{2,1,0:T(2,128)(2,1)}, u32[]{:S(2)}) copy-start(bf16[1,2,256]{2,1,0:T(2,128)(2,1)} %param.11) | copy-start | bytes 3076
  3.6 9.1 %copy-start = (bf16[16,256]{1,0:T(8,128)(2,1)S(1)}, bf16[16,256]{1,0:T(8,128)(2,1)}, u32[]{:S(2)}) copy-start(bf16[16,256]{1,0:T(8,128)(2,1)} %blocks_ref.1) | copy-start | bytes 24580
  8.1 3.3 %collective-permute-start.4 = (bf16[4,2,256]{2,1,0:T(2,128)(2,1)S(1)}, bf16[4,2,256]{2,1,0:T(2,128)(2,1)S(1)}, u32[]{:S(2)}, u32[]{:S(2)}) collective-permute-start(bf16[4,2,256]{2,1,0:T(2,128)(2,1)S(1)} %constant_dynamic-update-slice_fusion.mine_ref), channel_id=1, source_target_pairs={{0,4},{4,0},{8,12},{12,8},{16,20},{20,16},{24,28},{28,24},{1,5},{5... | collective-permute-start | bytes 12296 | tf_op jit(solution)/shard_map/ppermute | solution.py:284
  10.5 5.6 %collective-permute-start.3 = (bf16[288,2048]{1,0:T(8,128)(2,1)S(1)}, bf16[288,2048]{1,0:T(8,128)(2,1)S(1)}, u32[]{:S(2)}, u32[]{:S(2)}) collective-permute-start(bf16[288,2048]{1,0:T(8,128)(2,1)S(1)} %bitcast.2), channel_id=1, source_target_pairs={{0,4},{4,0},{8,12},{12,8},{16,20},{20,16},{24,28},{28,24},{1,5},{5... | collective-permute-start | bytes 3538952 | tf_op jit(solution)/shard_map/ppermute | solution.py:285
  10.6 11.1 %collective-permute-start.6 = (bf16[288,2048]{1,0:T(8,128)(2,1)S(1)}, bf16[288,2048]{1,0:T(8,128)(2,1)}, u32[]{:S(2)}, u32[]{:S(2)}) collective-permute-start(bf16[288,2048]{1,0:T(8,128)(2,1)S(1)} %bitcast.3), channel_id=1, source_target_pairs={{8,16},{12,20},{16,8},{20,12},{0,4},{4,0},{24,28},{28,24},{9,17},{... | collective-permute-start | bytes 3538952 | tf_op jit(solution)/shard_map/ppermute | solution.py:282
  11.9 27.2 %collective-permute-start.5 = (bf16[288,2048]{1,0:T(8,128)(2,1)S(1)}, bf16[288,2048]{1,0:T(8,128)(2,1)S(1)}, u32[]{:S(2)}, u32[]{:S(2)}) collective-permute-start(bf16[288,2048]{1,0:T(8,128)(2,1)S(1)} %bitcast.4), channel_id=1, source_target_pairs={{0,8},{4,12},{8,0},{12,4},{16,24},{20,28},{24,16},{28,20},{1,9},{5... | collective-permute-start | bytes 3538952 | tf_op jit(solution)/shard_map/ppermute | solution.py:287
  12.7 0.7 copy-start.1
  13.4 0.7 copy-start.2
  14.1 0.7 copy-start.4
  19.5 40.3 %collective-permute-start.10 = (bf16[256,2048]{1,0:T(8,128)(2,1)S(1)}, bf16[256,2048]{1,0:T(8,128)(2,1)S(1)}, u32[]{:S(2)}, u32[]{:S(2)}) collective-permute-start(bf16[256,2048]{1,0:T(8,128)(2,1)S(1)} %slice.25), channel_id=1, source_target_pairs={{0,16},{4,20},{24,8},{28,12},{1,17},{5,21},{25,9},{29,13},{2,18},{... | collective-permute-start | bytes 3145736 | tf_op jit(solution)/shard_map/ppermute | solution.py:301
  39.2 5.3 %collective-permute-start.8 = (bf16[144,2048]{1,0:T(8,128)(2,1)S(1)}, bf16[144,2048]{1,0:T(8,128)(2,1)S(1)}, u32[]{:S(2)}, u32[]{:S(2)}) collective-permute-start(bf16[144,2048]{1,0:T(8,128)(2,1)S(1)} %get-tuple-element.85), channel_id=1, source_target_pairs={{0,4},{4,0},{8,12},{12,8},{16,20},{20,16},{24,28},{28,24},{1,5},{5... | collective-permute-start | bytes 1769480 | tf_op jit(solution)/shard_map/ppermute | solution.py:306
  40.5 4.1 %collective-permute-start.7 = (bf16[144,2048]{1,0:T(8,128)(2,1)S(1)}, bf16[144,2048]{1,0:T(8,128)(2,1)S(1)}, u32[]{:S(2)}, u32[]{:S(2)}) collective-permute-start(bf16[144,2048]{1,0:T(8,128)(2,1)S(1)} %get-tuple-element.86), channel_id=1, source_target_pairs={{0,4},{4,0},{8,12},{12,8},{16,20},{20,16},{24,28},{28,24},{1,5},{5... | collective-permute-start | bytes 1769480 | tf_op jit(solution)/shard_map/ppermute | solution.py:306
  48.1 18.6 %collective-permute-start.11 = (bf16[144,1152]{1,0:T(8,128)(2,1)S(1)}, bf16[144,1152]{1,0:T(8,128)(2,1)S(1)}, u32[]{:S(2)}, u32[]{:S(2)}) collective-permute-start(bf16[144,1152]{1,0:T(8,128)(2,1)S(1)} %get-tuple-element.76), channel_id=1, source_target_pairs={{9,10},{13,14},{10,9},{14,13},{11,8},{15,12},{2,1},{6,5},{3,0},{7,... | collective-permute-start | bytes 995336 | tf_op jit(solution)/shard_map/ppermute | solution.py:322
  50.2 17.7 %collective-permute-start.12 = (bf16[144,1152]{1,0:T(8,128)(2,1)S(1)}, bf16[144,1152]{1,0:T(8,128)(2,1)S(1)}, u32[]{:S(2)}, u32[]{:S(2)}) collective-permute-start(bf16[144,1152]{1,0:T(8,128)(2,1)S(1)} %get-tuple-element.77), channel_id=1, source_target_pairs={{8,10},{12,14},{10,8},{14,12},{11,9},{15,13},{2,0},{6,4},{3,1},{7,... | collective-permute-start | bytes 995336 | tf_op jit(solution)/shard_map/ppermute | solution.py:322
  51.6 11.0 %collective-permute-start.9 = (bf16[32,2048]{1,0:T(8,128)(2,1)S(1)}, bf16[32,2048]{1,0:T(8,128)(2,1)S(1)}, u32[]{:S(2)}, u32[]{:S(2)}) collective-permute-start(bf16[32,2048]{1,0:T(8,128)(2,1)S(1)} %slice.24), channel_id=1, source_target_pairs={{0,16},{4,20},{24,8},{28,12},{1,17},{5,21},{25,9},{29,13},{2,18},{... | collective-permute-start | bytes 393224 | tf_op jit(solution)/shard_map/ppermute | solution.py:301
  55.3 14.0 %collective-permute-start.13 = (bf16[144,1152]{1,0:T(8,128)(2,1)S(1)}, bf16[144,1152]{1,0:T(8,128)(2,1)S(1)}, u32[]{:S(2)}, u32[]{:S(2)}) collective-permute-start(bf16[144,1152]{1,0:T(8,128)(2,1)S(1)} %get-tuple-element.78), channel_id=1, source_target_pairs={{8,9},{12,13},{9,8},{13,12},{11,10},{15,14},{0,1},{4,5},{1,0},{5,4... | collective-permute-start | bytes 995336 | tf_op jit(solution)/shard_map/ppermute | solution.py:322
  64.0 16.3 %collective-permute-start.14 = (bf16[144,1152]{1,0:T(8,128)(2,1)S(1)}, bf16[144,1152]{1,0:T(8,128)(2,1)S(1)}, u32[]{:S(2)}, u32[]{:S(2)}) collective-permute-start(bf16[144,1152]{1,0:T(8,128)(2,1)S(1)} %get-tuple-element.79), channel_id=1, source_target_pairs={{8,3},{12,7},{9,11},{13,15},{11,2},{15,6},{19,24},{23,28},{18,16},... | collective-permute-start | bytes 995336 | tf_op jit(solution)/shard_map/ppermute | solution.py:344
  65.3 17.8 %collective-permute-start.15 = (bf16[144,1152]{1,0:T(8,128)(2,1)S(1)}, bf16[144,1152]{1,0:T(8,128)(2,1)S(1)}, u32[]{:S(2)}, u32[]{:S(2)}) collective-permute-start(bf16[144,1152]{1,0:T(8,128)(2,1)S(1)} %get-tuple-element.80), channel_id=1, source_target_pairs={{8,11},{12,15},{9,3},{13,7},{19,16},{23,20},{18,24},{22,28}} | collective-permute-start | bytes 995336 | tf_op jit(solution)/shard_map/ppermute | solution.py:344
  66.6 16.5 %collective-permute-start.16 = (bf16[144,1152]{1,0:T(8,128)(2,1)S(1)}, bf16[144,1152]{1,0:T(8,128)(2,1)S(1)}, u32[]{:S(2)}, u32[]{:S(2)}) collective-permute-start(bf16[144,1152]{1,0:T(8,128)(2,1)S(1)} %get-tuple-element.81), channel_id=1, source_target_pairs={{10,11},{14,15},{11,3},{15,7},{17,16},{21,20},{16,24},{20,28}} | collective-permute-start | bytes 995336 | tf_op jit(solution)/shard_map/ppermute | solution.py:344
  68.0 15.2 %collective-permute-start.17 = (bf16[144,1152]{1,0:T(8,128)(2,1)S(1)}, bf16[144,1152]{1,0:T(8,128)(2,1)S(1)}, u32[]{:S(2)}, u32[]{:S(2)}) collective-permute-start(bf16[144,1152]{1,0:T(8,128)(2,1)S(1)} %get-tuple-element.82), channel_id=1, source_target_pairs={{10,3},{14,7},{17,24},{21,28}} | collective-permute-start | bytes 995336 | tf_op jit(solution)/shard_map/ppermute | solution.py:344
  83.7 3.3 %collective-permute-start.18 = (f32[144,576]{1,0:T(8,128)S(1)}, f32[144,576]{1,0:T(8,128)S(1)}, u32[]{:S(2)}, u32[]{:S(2)}) collective-permute-start(f32[144,576]{1,0:T(8,128)S(1)} %get-tuple-element.84), channel_id=1, source_target_pairs={{0,4},{4,0},{8,12},{12,8},{16,20},{20,16},{24,28},{28,24},{1,5},{5... | collective-permute-start | bytes 995336 | tf_op jit(solution)/shard_map/ppermute | solution.py:348
  (1 other events, 0.6 us)

commit v7 on v6

--- a/solution.py
+++ b/solution.py
@@ -175,6 +175,7 @@
 
 
 LATE = ((2, 0, None, 1), (0, 2, None, None), (None, None, 0, 2), (None, None, 2, None))
+FILLED = (0,)
 LATE_TO = {0: (1, 3), 1: (0, 2), 2: (0, 3)}
 
 
@@ -208,15 +209,38 @@
         out[:, cut:] = part[...]
 
 
+def late_moves(sources):
+    return [((1, g), LATE_TO[what]) for g, what in enumerate(sources) if what is not None]
+
+
+def filled(moves):
+    every = [(plane, g) for plane in range(2) for g in range(4)]
+    sending, taking = [a for a, _ in moves], [b for _, b in moves]
+    swaps = [at for at in every if at not in sending and at not in taking]
+    rest = [at for at in every if at not in sending and at not in swaps]
+    open_places = [at for at in every if at not in taking and at not in swaps]
+    return moves + list(zip(rest, open_places)), swaps
+
+
 def sum_body(*refs):
     values, sides = refs[:-2], refs[-2:]
+    plane, place = place_of()
+
+    def taken(index):
+        found = jnp.bool_(False)
+        for _, (a, g) in late_moves(LATE[index]):
+            found = found | (plane == a) & (place == g)
+        return found
+
+    use = [None] * (len(values) - len(LATE)) + [taken(index) for index in range(len(LATE))]
     width = sides[0].shape[1]
     cut = far_cut(width // 2)
     for at, side in enumerate(sides):
         for start, size, to in ((at * 2 * cut, 2 * cut, 0), (4 * cut + at * (width - 2 * cut), width - 2 * cut, 2 * cut)):
             total = values[0][:, start:start + size]
-            for value in values[1:]:
-                total = total + value[:, start:start + size].astype(F32)
+            for value, wanted in zip(values[1:], use[1:]):
+                piece = value[:, start:start + size].astype(F32)
+                total = total + (piece if wanted is None else jnp.where(wanted, piece, 0.0))
             side[:, to:to + size] = total
 
 
@@ -265,9 +289,15 @@
     core_swap = [(i, i ^ 1) for i in range(8)]
     both = ("pair", "red")
 
-    def everywhere(moves):
-        full = list(moves) + [((3 - a, 3 - g), (3 - b, 3 - h)) for (a, g), (b, h) in moves]
-        return [((CORES * a + c) * 4 + g, (CORES * b + c) * 4 + h) for (a, g), (b, h) in full for c in range(CORES)]
+    def everywhere(moves, swaps=()):
+        def pairs(found, flip):
+            full = list(found) + [((3 - a, 3 - g), (3 - b, 3 - h)) for (a, g), (b, h) in found]
+            return [
+                ((CORES * a + c) * 4 + g, (CORES * b + (c ^ flip)) * 4 + h)
+                for (a, g), (b, h) in full for c in range(CORES)
+            ]
+
+        return pairs(moves, 0) + pairs([(at, at) for at in swaps], 1)
 
     after = lax.optimization_barrier
 
@@ -339,9 +369,9 @@
         [pltpu.VMEM((3, *rest), BF16), pltpu.VMEM(rest, F32)] + [pltpu.VMEM(rest, BF16)] * 4,
         name="last",
     )
-    for sources, value in zip(LATE, late_sent):
-        moves = [((1, g), LATE_TO[what]) for g, what in enumerate(sources) if what is not None]
-        arrived.append(lax.ppermute(value, both, everywhere(moves)))
+    for index, (sources, value) in enumerate(zip(LATE, late_sent)):
+        moves = late_moves(sources)
+        arrived.append(lax.ppermute(value, both, everywhere(*(filled(moves) if index in FILLED else (moves,)))))
     mine, yours = call(
         sum_body, [shaped(aux // 2, 2 * aux, dtype=F32)] * 2, [own_early, own_late, *arrived], name="sum"
     )

time: 88.4 us -> 86.7 us (0.981)
  waiting for transfers between devices: 40.6 us -> 39.3 us
    ppermute x7 -> x3, waiting for transfers between devices: 13.9 us -> 0.01 us  [hub_plan(): arrived.append(lax.ppermute(value, both, everywhere(moves)))]
    ppermute x0 -> x4, waiting for transfers between devices: none -> 12.6 us  [hub_plan(): lax.ppermute(value, both, everywhere(*(filled(moves) if index in FILLED e...]
    ppermute x7 -> x3, starting transfers between devices: 9.49 us -> 4.32 us  [hub_plan(): arrived.append(lax.ppermute(value, both, everywhere(moves)))]
    ppermute x0 -> x4, starting transfers between devices: none -> 4.04 us  [hub_plan(): lax.ppermute(value, both, everywhere(*(filled(moves) if index in FILLED e...]
where the time goes in v7:
time: 86.7 us; the launch traced here: 86.3 us
  waiting for transfers between devices  39.3 us (45%)
  starting transfers between devices  24.7 us (28%)
  Pallas kernels  16.7 us (19%)
  local copies, waits for them, and re-layouts  5.29 us (6%)
    ppermute x1, waiting for transfers between devices, hub_plan(): lax.ppermute(tiles, 'pair', along_z([(0, 1), (1, 0), (2, 3), (3, 2)]))  17.5 us
    pallas_call x9, Pallas kernels, call(): pl.pallas_call(body, out_shape=outs, in_specs=[pl.BlockSpec(memory_space=...  16.7 us
    ppermute x4, waiting for transfers between devices, hub_plan(): lax.ppermute(value, both, everywhere(*(filled(moves) if index in FILLED e...  12.6 us
    ppermute x2, starting transfers between devices, hub_plan(): lax.ppermute(part, 'pair', along_z([(0, 2), (3, 1)]))  5.93 us
    unnamed x17, local copies, waits for them, and re-layouts  5.06 us
    ppermute x2, waiting for transfers between devices, hub_plan(): lax.ppermute(part, 'pair', along_z([(0, 2), (3, 1)]))  4.85 us
    ppermute x3, starting transfers between devices, hub_plan(): arrived.append(lax.ppermute(value, both, everywhere(moves)))  4.32 us
    ppermute x4, starting transfers between devices, hub_plan(): lax.ppermute(value, both, everywhere(*(filled(moves) if index in FILLED e...  4.04 us
  transfers between devices with their start and end apart: 19, of which 8 were waited for; matrix products, arithmetic and copies ran while one was open for 3% of the time, Pallas kernels for 17%

profile of v7, /device:TPU:7, one launch (start us, length us, event | category | flops | bytes accessed | tf_op | source)
XLA Modules:
  0.0 86.3 jit_solution(11212809445069052506)
XLA Ops:
  0.0 2.3 %collective-permute-start.1 = (bf16[1,2,256]{2,1,0:T(2,128)(2,1)}, bf16[1,2,256]{2,1,0:T(2,128)(2,1)S(1)}, u32[]{:S(2)}, u32[]{:S(2)}) collective-permute-start(bf16[1,2,256]{2,1,0:T(2,128)(2,1)} %param.11), channel_id=1, source_target_pairs={{0,16},{4,20},{8,24},{12,28},{16,0},{20,4},{24,8},{28,12},{1,17},{... | collective-permute-start | bytes 3080 | tf_op jit(solution)/shard_map/ppermute | solution.py:308
  2.3 1.3 %collective-permute-start = (bf16[1,2,256]{2,1,0:T(2,128)(2,1)}, bf16[1,2,256]{2,1,0:T(2,128)(2,1)S(1)}, u32[]{:S(2)}, u32[]{:S(2)}) collective-permute-start(bf16[1,2,256]{2,1,0:T(2,128)(2,1)} %param.11), channel_id=1, source_target_pairs={{0,8},{4,12},{8,0},{12,4},{16,24},{20,28},{24,16},{28,20},{1,9},{5... | collective-permute-start | bytes 3080 | tf_op jit(solution)/shard_map/ppermute | solution.py:308
  3.6 1.6 %copy.8 = bf16[36,8,8,256]{3,1,2,0:T(8,128)(2,1)S(1)} copy(bf16[36,8,8,256]{3,2,1,0:T(8,128)(2,1)} %bitcast.10) | data formatting | bytes 2359296
  5.3 2.7 %collective-permute-done.2 = bf16[1,2,256]{2,1,0:T(2,128)(2,1)S(1)} collective-permute-done((bf16[1,2,256]{2,1,0:T(2,128)(2,1)}, bf16[1,2,256]{2,1,0:T(2,128)(2,1)S(1)}, u32[]{:S(2)}, u32[]{:S(2)}) %collective-permute-start.2) | collective-permute-done | bytes 1056 | tf_op jit(solution)/shard_map/ppermute | solution.py:308
  8.1 2.5 %collective-permute-start.4 = (bf16[4,2,256]{2,1,0:T(2,128)(2,1)S(1)}, bf16[4,2,256]{2,1,0:T(2,128)(2,1)S(1)}, u32[]{:S(2)}, u32[]{:S(2)}) collective-permute-start(bf16[4,2,256]{2,1,0:T(2,128)(2,1)S(1)} %constant_dynamic-update-slice_fusion.mine_ref), channel_id=1, source_target_pairs={{0,4},{4,0},{8,12},{12,8},{16,20},{20,16},{24,28},{28,24},{1,5},{5... | collective-permute-start | bytes 12296 | tf_op jit(solution)/shard_map/ppermute | solution.py:314
  14.7 1.4 %prep.1 = (bf16[128,128]{1,0:T(8,128)(2,1)S(1)}, bf16[8,256,256]{2,1,0:T(8,128)(2,1)S(1)}) custom-call(s32[8,8]{1,0:T(8,128)S(1)} %copy-done.1, s32[8,8]{1,0:T(8,128)S(1)} %copy-done.2, s32[1,8,1]{2,1,0:T(8,128)S(1)} %copy.7.listed_ref, bf16[16,256]{1,0:T(8,128)(2,1)S(1)} %copy-done, bf16[4,2,256]{2,1,0:T(2,128)(2,1)S(1)} %constant_dynamic-update-slice_fusion.mine_ref, ...), custom_call_target="tpu_custom_call" | custom-call | flops 1 | bytes 1 | tf_op jit(solution)/shard_map/prep/pallas_call | solution.py:263
  16.2 1.8 %k_own.1.k_ref = bf16[288,2048]{1,0:T(8,128)(2,1)S(1)} custom-call(bf16[288,2048]{1,0:T(8,128)(2,1)S(1)} %bitcast.5, bf16[128,128]{1,0:T(8,128)(2,1)S(1)} %get-tuple-element.55.mix_ref, bf16[8,256,256]{2,1,0:T(8,128)(2,1)S(1)} %get-tuple-element.56.wide_ref), custom_call_target="tpu_custom_call" | custom-call | flops 1 | bytes 1 | tf_op jit(solution)/shard_map/k_own/pallas_call | solution.py:263
  17.9 1.4 %near.1.near_ref = f32[144,1152]{1,0:T(8,128)S(1)} custom-call(bf16[288,2048]{1,0:T(8,128)(2,1)S(1)} %bitcast.6, bf16[288,2048]{1,0:T(8,128)(2,1)S(1)} %collective-permute-done.3.p_ref, bf16[288,2048]{1,0:T(8,128)(2,1)S(1)} %k_own.1.k_ref), custom_call_target="tpu_custom_call" | custom-call | flops 1 | bytes 1 | tf_op jit(solution)/shard_map/near/pallas_call | solution.py:263
  19.5 2.2 %collective-permute-start.10 = (bf16[256,2048]{1,0:T(8,128)(2,1)S(1)}, bf16[256,2048]{1,0:T(8,128)(2,1)S(1)}, u32[]{:S(2)}, u32[]{:S(2)}) collective-permute-start(bf16[256,2048]{1,0:T(8,128)(2,1)S(1)} %slice.25), channel_id=1, source_target_pairs={{0,16},{4,20},{24,8},{28,12},{1,17},{5,21},{25,9},{29,13},{2,18},{... | collective-permute-start | bytes 3145736 | tf_op jit(solution)/shard_map/ppermute | solution.py:331
  21.7 17.5 %collective-permute-done.5.outer_ref.e_ref = bf16[288,2048]{1,0:T(8,128)(2,1)S(1)} collective-permute-done((bf16[288,2048]{1,0:T(8,128)(2,1)S(1)}, bf16[288,2048]{1,0:T(8,128)(2,1)S(1)}, u32[]{:S(2)}, u32[]{:S(2)}) %collective-permute-start.5) | collective-permute-done | bytes 1179680 | tf_op jit(solution)/shard_map/ppermute | solution.py:317
  40.6 4.0 %k_moved.1.kt_ref = bf16[2048,576]{1,0:T(8,128)(2,1)S(1)} custom-call(bf16[288,2048]{1,0:T(8,128)(2,1)} %collective-permute-done.6.inner_ref, bf16[288,2048]{1,0:T(8,128)(2,1)S(1)} %collective-permute-done.5.outer_ref.e_ref, bf16[128,128]{1,0:T(8,128)(2,1)S(1)} %get-tuple-element.55.mix_ref, bf16[8,256,256]{2,1,0:T(8,128)(2,1)S(1)} %get-tuple-element.56.wide_ref), custom_call_target="tpu_custom_call" | custom-call | flops 1 | bytes 1 | tf_op jit(solution)/shard_map/k_moved/pallas_call | solution.py:263
  44.5 3.5 %early.1 = (f32[144,1152]{1,0:T(8,128)S(1)}, bf16[144,1152]{1,0:T(8,128)(2,1)S(1)}, bf16[144,1152]{1,0:T(8,128)(2,1)S(1)}, bf16[144,1152]{1,0:T(8,128)(2,1)S(1)}, bf16[144,1152]{1,0:T(8,128)(2,1)S(1)}) custom-call(bf16[288,2048]{1,0:T(8,128)(2,1)S(1)} %bitcast.7, bf16[288,2048]{1,0:T(8,128)(2,1)S(1)} %collective-permute-done.3.p_ref, ...), custom_call_target="tpu_custom_call" | custom-call | flops 1 | bytes 1 | tf_op jit(solution)/shard_map/early/pallas_call | solution.py:263
  48.1 2.1 %collective-permute-start.11 = (bf16[144,1152]{1,0:T(8,128)(2,1)S(1)}, bf16[144,1152]{1,0:T(8,128)(2,1)S(1)}, u32[]{:S(2)}, u32[]{:S(2)}) collective-permute-start(bf16[144,1152]{1,0:T(8,128)(2,1)S(1)} %get-tuple-element.76), channel_id=1, source_target_pairs={{9,10},{13,14},{10,9},{14,13},{11,8},{15,12},{2,1},{6,5},{3,0},{7,... | collective-permute-start | bytes 995336 | tf_op jit(solution)/shard_map/ppermute | solution.py:352
  50.2 1.3 %collective-permute-start.12 = (bf16[144,1152]{1,0:T(8,128)(2,1)S(1)}, bf16[144,1152]{1,0:T(8,128)(2,1)S(1)}, u32[]{:S(2)}, u32[]{:S(2)}) collective-permute-start(bf16[144,1152]{1,0:T(8,128)(2,1)S(1)} %get-tuple-element.77), channel_id=1, source_target_pairs={{8,10},{12,14},{10,8},{14,12},{11,9},{15,13},{2,0},{6,4},{3,1},{7,... | collective-permute-start | bytes 995336 | tf_op jit(solution)/shard_map/ppermute | solution.py:352
  51.6 3.7 %collective-permute-start.9 = (bf16[32,2048]{1,0:T(8,128)(2,1)S(1)}, bf16[32,2048]{1,0:T(8,128)(2,1)S(1)}, u32[]{:S(2)}, u32[]{:S(2)}) collective-permute-start(bf16[32,2048]{1,0:T(8,128)(2,1)S(1)} %slice.24), channel_id=1, source_target_pairs={{0,16},{4,20},{24,8},{28,12},{1,17},{5,21},{25,9},{29,13},{2,18},{... | collective-permute-start | bytes 393224 | tf_op jit(solution)/shard_map/ppermute | solution.py:331
  56.2 3.6 %collective-permute-done.10.k_ref = bf16[256,2048]{1,0:T(8,128)(2,1)S(1)} collective-permute-done((bf16[256,2048]{1,0:T(8,128)(2,1)S(1)}, bf16[256,2048]{1,0:T(8,128)(2,1)S(1)}, u32[]{:S(2)}, u32[]{:S(2)}) %collective-permute-start.10) | collective-permute-done | bytes 1048608 | tf_op jit(solution)/shard_map/ppermute | solution.py:331
  59.8 1.5 %late.1 = (f32[144,1024]{1,0:T(8,128)S(1)}, bf16[144,1024]{1,0:T(8,128)(2,1)S(1)}, bf16[144,1024]{1,0:T(8,128)(2,1)S(1)}, bf16[144,1024]{1,0:T(8,128)(2,1)S(1)}, bf16[144,1024]{1,0:T(8,128)(2,1)S(1)}) custom-call(bf16[256,2048]{1,0:T(8,128)(2,1)S(1)} %collective-permute-done.10.k_ref, bf16[288,2048]{1,0:T(8,128)(2,1)S(1)} %bitcast.8, ...), custom_call_target="tpu_custom_call" | custom-call | flops 1 | bytes 1 | tf_op jit(solution)/shard_map/late/pallas_call | solution.py:263
  62.6 1.5 %last.1 = (f32[144,1152]{1,0:T(8,128)S(1)}, bf16[144,1152]{1,0:T(8,128)(2,1)S(1)}, bf16[144,1152]{1,0:T(8,128)(2,1)S(1)}, bf16[144,1152]{1,0:T(8,128)(2,1)S(1)}, bf16[144,1152]{1,0:T(8,128)(2,1)S(1)}) custom-call(bf16[32,2048]{1,0:T(8,128)(2,1)S(1)} %collective-permute-done.9.k_ref, bf16[288,2048]{1,0:T(8,128)(2,1)S(1)} %bitcast.9, ...), custom_call_target="tpu_custom_call" | custom-call | flops 1 | bytes 1 | tf_op jit(solution)/shard_map/last/pallas_call | solution.py:263
  65.5 1.3 %collective-permute-start.16 = (bf16[144,1152]{1,0:T(8,128)(2,1)S(1)}, bf16[144,1152]{1,0:T(8,128)(2,1)S(1)}, u32[]{:S(2)}, u32[]{:S(2)}) collective-permute-start(bf16[144,1152]{1,0:T(8,128)(2,1)S(1)} %get-tuple-element.81), channel_id=1, source_target_pairs={{10,11},{14,15},{11,3},{15,7},{17,16},{21,20},{16,24},{20,28}} | collective-permute-start | bytes 995336 | tf_op jit(solution)/shard_map/ppermute | solution.py:374
  66.8 1.3 %collective-permute-start.17 = (bf16[144,1152]{1,0:T(8,128)(2,1)S(1)}, bf16[144,1152]{1,0:T(8,128)(2,1)S(1)}, u32[]{:S(2)}, u32[]{:S(2)}) collective-permute-start(bf16[144,1152]{1,0:T(8,128)(2,1)S(1)} %get-tuple-element.82), channel_id=1, source_target_pairs={{10,3},{14,7},{17,24},{21,28}} | collective-permute-start | bytes 995336 | tf_op jit(solution)/shard_map/ppermute | solution.py:374
  68.1 9.8 %collective-permute-done.14.refs_5_ = bf16[144,1152]{1,0:T(8,128)(2,1)S(1)} collective-permute-done((bf16[144,1152]{1,0:T(8,128)(2,1)S(1)}, bf16[144,1152]{1,0:T(8,128)(2,1)S(1)}, u32[]{:S(2)}, u32[]{:S(2)}) %collective-permute-start.14) | collective-permute-done | bytes 331808 | tf_op jit(solution)/shard_map/ppermute | solution.py:374
  78.0 2.8 %collective-permute-done.15.refs_6_ = bf16[144,1152]{1,0:T(8,128)(2,1)S(1)} collective-permute-done((bf16[144,1152]{1,0:T(8,128)(2,1)S(1)}, bf16[144,1152]{1,0:T(8,128)(2,1)S(1)}, u32[]{:S(2)}, u32[]{:S(2)}) %collective-permute-start.15) | collective-permute-done | bytes 331808 | tf_op jit(solution)/shard_map/ppermute | solution.py:374
  81.4 2.5 %collective-permute-start.18 = (f32[144,576]{1,0:T(8,128)S(1)}, f32[144,576]{1,0:T(8,128)S(1)}, u32[]{:S(2)}, u32[]{:S(2)}) collective-permute-start(f32[144,576]{1,0:T(8,128)S(1)} %get-tuple-element.84), channel_id=1, source_target_pairs={{0,4},{4,0},{8,12},{12,8},{16,20},{20,16},{24,28},{28,24},{1,5},{5... | collective-permute-start | bytes 995336 | tf_op jit(solution)/shard_map/ppermute | solution.py:378
  83.9 1.3 %collective-permute-done.18.other_ref = f32[144,576]{1,0:T(8,128)S(1)} collective-permute-done((f32[144,576]{1,0:T(8,128)S(1)}, f32[144,576]{1,0:T(8,128)S(1)}, u32[]{:S(2)}, u32[]{:S(2)}) %collective-permute-start.18) | collective-permute-done | bytes 331808 | tf_op jit(solution)/shard_map/ppermute | solution.py:378
  (46 shorter events, 11.1 us)
Async XLA Ops:
  0.0 5.3 %collective-permute-start.1 = (bf16[1,2,256]{2,1,0:T(2,128)(2,1)}, bf16[1,2,256]{2,1,0:T(2,128)(2,1)S(1)}, u32[]{:S(2)}, u32[]{:S(2)}) collective-permute-start(bf16[1,2,256]{2,1,0:T(2,128)(2,1)} %param.11), channel_id=1, source_target_pairs={{0,16},{4,20},{8,24},{12,28},{16,0},{20,4},{24,8},{28,12},{1,17},{... | collective-permute-start | bytes 3080 | tf_op jit(solution)/shard_map/ppermute | solution.py:308
  2.3 3.0 %collective-permute-start = (bf16[1,2,256]{2,1,0:T(2,128)(2,1)}, bf16[1,2,256]{2,1,0:T(2,128)(2,1)S(1)}, u32[]{:S(2)}, u32[]{:S(2)}) collective-permute-start(bf16[1,2,256]{2,1,0:T(2,128)(2,1)} %param.11), channel_id=1, source_target_pairs={{0,8},{4,12},{8,0},{12,4},{16,24},{20,28},{24,16},{28,20},{1,9},{5... | collective-permute-start | bytes 3080 | tf_op jit(solution)/shard_map/ppermute | solution.py:308
  3.6 4.4 %collective-permute-start.2 = (bf16[1,2,256]{2,1,0:T(2,128)(2,1)}, bf16[1,2,256]{2,1,0:T(2,128)(2,1)S(1)}, u32[]{:S(2)}, u32[]{:S(2)}) collective-permute-start(bf16[1,2,256]{2,1,0:T(2,128)(2,1)} %param.11), channel_id=1, source_target_pairs={{0,24},{4,28},{8,16},{12,20},{16,8},{20,12},{24,0},{28,4},{1,25},{... | collective-permute-start | bytes 3080 | tf_op jit(solution)/shard_map/ppermute | solution.py:308
  3.6 4.4 %copy-start.5 = (bf16[1,2,256]{2,1,0:T(2,128)(2,1)S(1)}, bf16[1,2,256]{2,1,0:T(2,128)(2,1)}, u32[]{:S(2)}) copy-start(bf16[1,2,256]{2,1,0:T(2,128)(2,1)} %param.11) | copy-start | bytes 3076
  3.6 9.1 %copy-start = (bf16[16,256]{1,0:T(8,128)(2,1)S(1)}, bf16[16,256]{1,0:T(8,128)(2,1)}, u32[]{:S(2)}) copy-start(bf16[16,256]{1,0:T(8,128)(2,1)} %blocks_ref.1) | copy-start | bytes 24580
  8.1 3.3 %collective-permute-start.4 = (bf16[4,2,256]{2,1,0:T(2,128)(2,1)S(1)}, bf16[4,2,256]{2,1,0:T(2,128)(2,1)S(1)}, u32[]{:S(2)}, u32[]{:S(2)}) collective-permute-start(bf16[4,2,256]{2,1,0:T(2,128)(2,1)S(1)} %constant_dynamic-update-slice_fusion.mine_ref), channel_id=1, source_target_pairs={{0,4},{4,0},{8,12},{12,8},{16,20},{20,16},{24,28},{28,24},{1,5},{5... | collective-permute-start | bytes 12296 | tf_op jit(solution)/shard_map/ppermute | solution.py:314
  10.5 5.6 %collective-permute-start.3 = (bf16[288,2048]{1,0:T(8,128)(2,1)S(1)}, bf16[288,2048]{1,0:T(8,128)(2,1)S(1)}, u32[]{:S(2)}, u32[]{:S(2)}) collective-permute-start(bf16[288,2048]{1,0:T(8,128)(2,1)S(1)} %bitcast.2), channel_id=1, source_target_pairs={{0,4},{4,0},{8,12},{12,8},{16,20},{20,16},{24,28},{28,24},{1,5},{5... | collective-permute-start | bytes 3538952 | tf_op jit(solution)/shard_map/ppermute | solution.py:315
  10.6 11.1 %collective-permute-start.6 = (bf16[288,2048]{1,0:T(8,128)(2,1)S(1)}, bf16[288,2048]{1,0:T(8,128)(2,1)}, u32[]{:S(2)}, u32[]{:S(2)}) collective-permute-start(bf16[288,2048]{1,0:T(8,128)(2,1)S(1)} %bitcast.3), channel_id=1, source_target_pairs={{8,16},{12,20},{16,8},{20,12},{0,4},{4,0},{24,28},{28,24},{9,17},{... | collective-permute-start | bytes 3538952 | tf_op jit(solution)/shard_map/ppermute | solution.py:312
  11.9 27.2 %collective-permute-start.5 = (bf16[288,2048]{1,0:T(8,128)(2,1)S(1)}, bf16[288,2048]{1,0:T(8,128)(2,1)S(1)}, u32[]{:S(2)}, u32[]{:S(2)}) collective-permute-start(bf16[288,2048]{1,0:T(8,128)(2,1)S(1)} %bitcast.4), channel_id=1, source_target_pairs={{0,8},{4,12},{8,0},{12,4},{16,24},{20,28},{24,16},{28,20},{1,9},{5... | collective-permute-start | bytes 3538952 | tf_op jit(solution)/shard_map/ppermute | solution.py:317
  12.7 0.7 copy-start.1
  13.4 0.7 copy-start.2
  14.1 0.7 copy-start.4
  19.5 40.3 %collective-permute-start.10 = (bf16[256,2048]{1,0:T(8,128)(2,1)S(1)}, bf16[256,2048]{1,0:T(8,128)(2,1)S(1)}, u32[]{:S(2)}, u32[]{:S(2)}) collective-permute-start(bf16[256,2048]{1,0:T(8,128)(2,1)S(1)} %slice.25), channel_id=1, source_target_pairs={{0,16},{4,20},{24,8},{28,12},{1,17},{5,21},{25,9},{29,13},{2,18},{... | collective-permute-start | bytes 3145736 | tf_op jit(solution)/shard_map/ppermute | solution.py:331
  39.2 5.3 %collective-permute-start.8 = (bf16[144,2048]{1,0:T(8,128)(2,1)S(1)}, bf16[144,2048]{1,0:T(8,128)(2,1)S(1)}, u32[]{:S(2)}, u32[]{:S(2)}) collective-permute-start(bf16[144,2048]{1,0:T(8,128)(2,1)S(1)} %get-tuple-element.85), channel_id=1, source_target_pairs={{0,4},{4,0},{8,12},{12,8},{16,20},{20,16},{24,28},{28,24},{1,5},{5... | collective-permute-start | bytes 1769480 | tf_op jit(solution)/shard_map/ppermute | solution.py:336
  40.5 4.1 %collective-permute-start.7 = (bf16[144,2048]{1,0:T(8,128)(2,1)S(1)}, bf16[144,2048]{1,0:T(8,128)(2,1)S(1)}, u32[]{:S(2)}, u32[]{:S(2)}) collective-permute-start(bf16[144,2048]{1,0:T(8,128)(2,1)S(1)} %get-tuple-element.86), channel_id=1, source_target_pairs={{0,4},{4,0},{8,12},{12,8},{16,20},{20,16},{24,28},{28,24},{1,5},{5... | collective-permute-start | bytes 1769480 | tf_op jit(solution)/shard_map/ppermute | solution.py:336
  48.1 17.4 %collective-permute-start.11 = (bf16[144,1152]{1,0:T(8,128)(2,1)S(1)}, bf16[144,1152]{1,0:T(8,128)(2,1)S(1)}, u32[]{:S(2)}, u32[]{:S(2)}) collective-permute-start(bf16[144,1152]{1,0:T(8,128)(2,1)S(1)} %get-tuple-element.76), channel_id=1, source_target_pairs={{9,10},{13,14},{10,9},{14,13},{11,8},{15,12},{2,1},{6,5},{3,0},{7,... | collective-permute-start | bytes 995336 | tf_op jit(solution)/shard_map/ppermute | solution.py:352
  50.2 16.6 %collective-permute-start.12 = (bf16[144,1152]{1,0:T(8,128)(2,1)S(1)}, bf16[144,1152]{1,0:T(8,128)(2,1)S(1)}, u32[]{:S(2)}, u32[]{:S(2)}) collective-permute-start(bf16[144,1152]{1,0:T(8,128)(2,1)S(1)} %get-tuple-element.77), channel_id=1, source_target_pairs={{8,10},{12,14},{10,8},{14,12},{11,9},{15,13},{2,0},{6,4},{3,1},{7,... | collective-permute-start | bytes 995336 | tf_op jit(solution)/shard_map/ppermute | solution.py:352
  51.6 11.0 %collective-permute-start.9 = (bf16[32,2048]{1,0:T(8,128)(2,1)S(1)}, bf16[32,2048]{1,0:T(8,128)(2,1)S(1)}, u32[]{:S(2)}, u32[]{:S(2)}) collective-permute-start(bf16[32,2048]{1,0:T(8,128)(2,1)S(1)} %slice.24), channel_id=1, source_target_pairs={{0,16},{4,20},{24,8},{28,12},{1,17},{5,21},{25,9},{29,13},{2,18},{... | collective-permute-start | bytes 393224 | tf_op jit(solution)/shard_map/ppermute | solution.py:331
  55.3 12.8 %collective-permute-start.13 = (bf16[144,1152]{1,0:T(8,128)(2,1)S(1)}, bf16[144,1152]{1,0:T(8,128)(2,1)S(1)}, u32[]{:S(2)}, u32[]{:S(2)}) collective-permute-start(bf16[144,1152]{1,0:T(8,128)(2,1)S(1)} %get-tuple-element.78), channel_id=1, source_target_pairs={{8,9},{12,13},{9,8},{13,12},{11,10},{15,14},{0,1},{4,5},{1,0},{5,4... | collective-permute-start | bytes 995336 | tf_op jit(solution)/shard_map/ppermute | solution.py:352
  64.0 13.9 %collective-permute-start.14 = (bf16[144,1152]{1,0:T(8,128)(2,1)S(1)}, bf16[144,1152]{1,0:T(8,128)(2,1)S(1)}, u32[]{:S(2)}, u32[]{:S(2)}) collective-permute-start(bf16[144,1152]{1,0:T(8,128)(2,1)S(1)} %get-tuple-element.79), channel_id=1, source_target_pairs={{8,3},{12,7},{9,11},{13,15},{11,2},{15,6},{2,8},{6,12},{3,9},{7,13... | collective-permute-start | bytes 995336 | tf_op jit(solution)/shard_map/ppermute | solution.py:374
  64.2 16.5 %collective-permute-start.15 = (bf16[144,1152]{1,0:T(8,128)(2,1)S(1)}, bf16[144,1152]{1,0:T(8,128)(2,1)S(1)}, u32[]{:S(2)}, u32[]{:S(2)}) collective-permute-start(bf16[144,1152]{1,0:T(8,128)(2,1)S(1)} %get-tuple-element.80), channel_id=1, source_target_pairs={{8,11},{12,15},{9,3},{13,7},{19,16},{23,20},{18,24},{22,28}} | collective-permute-start | bytes 995336 | tf_op jit(solution)/shard_map/ppermute | solution.py:374
  65.5 15.2 %collective-permute-start.16 = (bf16[144,1152]{1,0:T(8,128)(2,1)S(1)}, bf16[144,1152]{1,0:T(8,128)(2,1)S(1)}, u32[]{:S(2)}, u32[]{:S(2)}) collective-permute-start(bf16[144,1152]{1,0:T(8,128)(2,1)S(1)} %get-tuple-element.81), channel_id=1, source_target_pairs={{10,11},{14,15},{11,3},{15,7},{17,16},{21,20},{16,24},{20,28}} | collective-permute-start | bytes 995336 | tf_op jit(solution)/shard_map/ppermute | solution.py:374
  66.8 13.9 %collective-permute-start.17 = (bf16[144,1152]{1,0:T(8,128)(2,1)S(1)}, bf16[144,1152]{1,0:T(8,128)(2,1)S(1)}, u32[]{:S(2)}, u32[]{:S(2)}) collective-permute-start(bf16[144,1152]{1,0:T(8,128)(2,1)S(1)} %get-tuple-element.82), channel_id=1, source_target_pairs={{10,3},{14,7},{17,24},{21,28}} | collective-permute-start | bytes 995336 | tf_op jit(solution)/shard_map/ppermute | solution.py:374
  81.4 3.9 %collective-permute-start.18 = (f32[144,576]{1,0:T(8,128)S(1)}, f32[144,576]{1,0:T(8,128)S(1)}, u32[]{:S(2)}, u32[]{:S(2)}) collective-permute-start(f32[144,576]{1,0:T(8,128)S(1)} %get-tuple-element.84), channel_id=1, source_target_pairs={{0,4},{4,0},{8,12},{12,8},{16,20},{20,16},{24,28},{28,24},{1,5},{5... | collective-permute-start | bytes 995336 | tf_op jit(solution)/shard_map/ppermute | solution.py:378
  (1 other events, 0.6 us)

commit v8 on v7

--- a/solution.py
+++ b/solution.py
@@ -174,7 +174,7 @@
     held_ref[...] = terms[3].astype(BF16)
 
 
-LATE = ((2, 0, None, 1), (0, 2, None, None), (None, None, 0, 2), (None, None, 2, None))
+LATE = ((0, 2, None, 1), (2, 0, None, None), (None, None, 0, 2), (None, None, 2, None))
 FILLED = (0,)
 LATE_TO = {0: (1, 3), 1: (0, 2), 2: (0, 3)}
 

time: 86.7 us -> 86.6 us (level)
  waiting for transfers between devices: 39.3 us -> 38.2 us
    ppermute x4, waiting for transfers between devices: 12.6 us -> 11.5 us  [hub_plan(): lax.ppermute(value, both, everywhere(*(filled(moves) if index in FILLED e...]
  transfers between devices with their start and end apart: 19 -> 19, of which waited for: 8 -> 9; matrix products, arithmetic and copies ran while one was open for 3% -> 3% of each run, Pallas kernels for 17% -> 18%
where the time goes in v8:
time: 86.6 us; the launch traced here: 85.4 us
  waiting for transfers between devices  38.2 us (44%)
  starting transfers between devices  24.9 us (29%)
  Pallas kernels  16.7 us (19%)
  local copies, waits for them, and re-layouts  5.29 us (6%)
    ppermute x1, waiting for transfers between devices, hub_plan(): lax.ppermute(tiles, 'pair', along_z([(0, 1), (1, 0), (2, 3), (3, 2)]))  17.5 us
    pallas_call x9, Pallas kernels, call(): pl.pallas_call(body, out_shape=outs, in_specs=[pl.BlockSpec(memory_space=...  16.7 us
    ppermute x4, waiting for transfers between devices, hub_plan(): lax.ppermute(value, both, everywhere(*(filled(moves) if index in FILLED e...  11.5 us
    ppermute x2, starting transfers between devices, hub_plan(): lax.ppermute(part, 'pair', along_z([(0, 2), (3, 1)]))  5.93 us
    unnamed x17, local copies, waits for them, and re-layouts  5.06 us
    ppermute x2, waiting for transfers between devices, hub_plan(): lax.ppermute(part, 'pair', along_z([(0, 2), (3, 1)]))  4.85 us
    ppermute x3, starting transfers between devices, hub_plan(): arrived.append(lax.ppermute(value, both, everywhere(moves)))  4.32 us
    ppermute x4, starting transfers between devices, hub_plan(): lax.ppermute(value, both, everywhere(*(filled(moves) if index in FILLED e...  4.04 us
  transfers between devices with their start and end apart: 19, of which 9 were waited for; matrix products, arithmetic and copies ran while one was open for 3% of the time, Pallas kernels for 18%

profile of v8, /device:TPU:7, one launch (start us, length us, event | category | flops | bytes accessed | tf_op | source)
XLA Modules:
  0.0 85.4 jit_solution(420650704649404653)
XLA Ops:
  0.0 2.3 %collective-permute-start.1 = (bf16[1,2,256]{2,1,0:T(2,128)(2,1)}, bf16[1,2,256]{2,1,0:T(2,128)(2,1)S(1)}, u32[]{:S(2)}, u32[]{:S(2)}) collective-permute-start(bf16[1,2,256]{2,1,0:T(2,128)(2,1)} %param.11), channel_id=1, source_target_pairs={{0,16},{4,20},{8,24},{12,28},{16,0},{20,4},{24,8},{28,12},{1,17},{... | collective-permute-start | bytes 3080 | tf_op jit(solution)/shard_map/ppermute | solution.py:308
  2.3 1.3 %collective-permute-start = (bf16[1,2,256]{2,1,0:T(2,128)(2,1)}, bf16[1,2,256]{2,1,0:T(2,128)(2,1)S(1)}, u32[]{:S(2)}, u32[]{:S(2)}) collective-permute-start(bf16[1,2,256]{2,1,0:T(2,128)(2,1)} %param.11), channel_id=1, source_target_pairs={{0,8},{4,12},{8,0},{12,4},{16,24},{20,28},{24,16},{28,20},{1,9},{5... | collective-permute-start | bytes 3080 | tf_op jit(solution)/shard_map/ppermute | solution.py:308
  3.6 1.6 %copy.8 = bf16[36,8,8,256]{3,1,2,0:T(8,128)(2,1)S(1)} copy(bf16[36,8,8,256]{3,2,1,0:T(8,128)(2,1)} %bitcast.10) | data formatting | bytes 2359296
  5.3 2.7 %collective-permute-done.2 = bf16[1,2,256]{2,1,0:T(2,128)(2,1)S(1)} collective-permute-done((bf16[1,2,256]{2,1,0:T(2,128)(2,1)}, bf16[1,2,256]{2,1,0:T(2,128)(2,1)S(1)}, u32[]{:S(2)}, u32[]{:S(2)}) %collective-permute-start.2) | collective-permute-done | bytes 1056 | tf_op jit(solution)/shard_map/ppermute | solution.py:308
  8.1 2.5 %collective-permute-start.4 = (bf16[4,2,256]{2,1,0:T(2,128)(2,1)S(1)}, bf16[4,2,256]{2,1,0:T(2,128)(2,1)S(1)}, u32[]{:S(2)}, u32[]{:S(2)}) collective-permute-start(bf16[4,2,256]{2,1,0:T(2,128)(2,1)S(1)} %constant_dynamic-update-slice_fusion.mine_ref), channel_id=1, source_target_pairs={{0,4},{4,0},{8,12},{12,8},{16,20},{20,16},{24,28},{28,24},{1,5},{5... | collective-permute-start | bytes 12296 | tf_op jit(solution)/shard_map/ppermute | solution.py:314
  14.7 1.4 %prep.1 = (bf16[128,128]{1,0:T(8,128)(2,1)S(1)}, bf16[8,256,256]{2,1,0:T(8,128)(2,1)S(1)}) custom-call(s32[8,8]{1,0:T(8,128)S(1)} %copy-done.1, s32[8,8]{1,0:T(8,128)S(1)} %copy-done.2, s32[1,8,1]{2,1,0:T(8,128)S(1)} %copy.7.listed_ref, bf16[16,256]{1,0:T(8,128)(2,1)S(1)} %copy-done, bf16[4,2,256]{2,1,0:T(2,128)(2,1)S(1)} %constant_dynamic-update-slice_fusion.mine_ref, ...), custom_call_target="tpu_custom_call" | custom-call | flops 1 | bytes 1 | tf_op jit(solution)/shard_map/prep/pallas_call | solution.py:263
  16.2 1.8 %k_own.1.k_ref = bf16[288,2048]{1,0:T(8,128)(2,1)S(1)} custom-call(bf16[288,2048]{1,0:T(8,128)(2,1)S(1)} %bitcast.5, bf16[128,128]{1,0:T(8,128)(2,1)S(1)} %get-tuple-element.55.mix_ref, bf16[8,256,256]{2,1,0:T(8,128)(2,1)S(1)} %get-tuple-element.56.wide_ref), custom_call_target="tpu_custom_call" | custom-call | flops 1 | bytes 1 | tf_op jit(solution)/shard_map/k_own/pallas_call | solution.py:263
  17.9 1.4 %near.1.near_ref = f32[144,1152]{1,0:T(8,128)S(1)} custom-call(bf16[288,2048]{1,0:T(8,128)(2,1)S(1)} %bitcast.6, bf16[288,2048]{1,0:T(8,128)(2,1)S(1)} %collective-permute-done.3.p_ref, bf16[288,2048]{1,0:T(8,128)(2,1)S(1)} %k_own.1.k_ref), custom_call_target="tpu_custom_call" | custom-call | flops 1 | bytes 1 | tf_op jit(solution)/shard_map/near/pallas_call | solution.py:263
  19.5 2.2 %collective-permute-start.10 = (bf16[256,2048]{1,0:T(8,128)(2,1)S(1)}, bf16[256,2048]{1,0:T(8,128)(2,1)S(1)}, u32[]{:S(2)}, u32[]{:S(2)}) collective-permute-start(bf16[256,2048]{1,0:T(8,128)(2,1)S(1)} %slice.25), channel_id=1, source_target_pairs={{0,16},{4,20},{24,8},{28,12},{1,17},{5,21},{25,9},{29,13},{2,18},{... | collective-permute-start | bytes 3145736 | tf_op jit(solution)/shard_map/ppermute | solution.py:331
  21.7 17.5 %collective-permute-done.5.outer_ref.e_ref = bf16[288,2048]{1,0:T(8,128)(2,1)S(1)} collective-permute-done((bf16[288,2048]{1,0:T(8,128)(2,1)S(1)}, bf16[288,2048]{1,0:T(8,128)(2,1)S(1)}, u32[]{:S(2)}, u32[]{:S(2)}) %collective-permute-start.5) | collective-permute-done | bytes 1179680 | tf_op jit(solution)/shard_map/ppermute | solution.py:317
  40.6 4.0 %k_moved.1.kt_ref = bf16[2048,576]{1,0:T(8,128)(2,1)S(1)} custom-call(bf16[288,2048]{1,0:T(8,128)(2,1)} %collective-permute-done.6.inner_ref, bf16[288,2048]{1,0:T(8,128)(2,1)S(1)} %collective-permute-done.5.outer_ref.e_ref, bf16[128,128]{1,0:T(8,128)(2,1)S(1)} %get-tuple-element.55.mix_ref, bf16[8,256,256]{2,1,0:T(8,128)(2,1)S(1)} %get-tuple-element.56.wide_ref), custom_call_target="tpu_custom_call" | custom-call | flops 1 | bytes 1 | tf_op jit(solution)/shard_map/k_moved/pallas_call | solution.py:263
  44.5 3.5 %early.1 = (f32[144,1152]{1,0:T(8,128)S(1)}, bf16[144,1152]{1,0:T(8,128)(2,1)S(1)}, bf16[144,1152]{1,0:T(8,128)(2,1)S(1)}, bf16[144,1152]{1,0:T(8,128)(2,1)S(1)}, bf16[144,1152]{1,0:T(8,128)(2,1)S(1)}) custom-call(bf16[288,2048]{1,0:T(8,128)(2,1)S(1)} %bitcast.7, bf16[288,2048]{1,0:T(8,128)(2,1)S(1)} %collective-permute-done.3.p_ref, ...), custom_call_target="tpu_custom_call" | custom-call | flops 1 | bytes 1 | tf_op jit(solution)/shard_map/early/pallas_call | solution.py:263
  48.1 2.1 %collective-permute-start.11 = (bf16[144,1152]{1,0:T(8,128)(2,1)S(1)}, bf16[144,1152]{1,0:T(8,128)(2,1)S(1)}, u32[]{:S(2)}, u32[]{:S(2)}) collective-permute-start(bf16[144,1152]{1,0:T(8,128)(2,1)S(1)} %get-tuple-element.76), channel_id=1, source_target_pairs={{9,10},{13,14},{10,9},{14,13},{11,8},{15,12},{2,1},{6,5},{3,0},{7,... | collective-permute-start | bytes 995336 | tf_op jit(solution)/shard_map/ppermute | solution.py:352
  50.2 1.3 %collective-permute-start.12 = (bf16[144,1152]{1,0:T(8,128)(2,1)S(1)}, bf16[144,1152]{1,0:T(8,128)(2,1)S(1)}, u32[]{:S(2)}, u32[]{:S(2)}) collective-permute-start(bf16[144,1152]{1,0:T(8,128)(2,1)S(1)} %get-tuple-element.77), channel_id=1, source_target_pairs={{8,10},{12,14},{10,8},{14,12},{11,9},{15,13},{2,0},{6,4},{3,1},{7,... | collective-permute-start | bytes 995336 | tf_op jit(solution)/shard_map/ppermute | solution.py:352
  51.6 3.7 %collective-permute-start.9 = (bf16[32,2048]{1,0:T(8,128)(2,1)S(1)}, bf16[32,2048]{1,0:T(8,128)(2,1)S(1)}, u32[]{:S(2)}, u32[]{:S(2)}) collective-permute-start(bf16[32,2048]{1,0:T(8,128)(2,1)S(1)} %slice.24), channel_id=1, source_target_pairs={{0,16},{4,20},{24,8},{28,12},{1,17},{5,21},{25,9},{29,13},{2,18},{... | collective-permute-start | bytes 393224 | tf_op jit(solution)/shard_map/ppermute | solution.py:331
  56.2 3.6 %collective-permute-done.10.k_ref = bf16[256,2048]{1,0:T(8,128)(2,1)S(1)} collective-permute-done((bf16[256,2048]{1,0:T(8,128)(2,1)S(1)}, bf16[256,2048]{1,0:T(8,128)(2,1)S(1)}, u32[]{:S(2)}, u32[]{:S(2)}) %collective-permute-start.10) | collective-permute-done | bytes 1048608 | tf_op jit(solution)/shard_map/ppermute | solution.py:331
  59.8 1.5 %late.1 = (f32[144,1024]{1,0:T(8,128)S(1)}, bf16[144,1024]{1,0:T(8,128)(2,1)S(1)}, bf16[144,1024]{1,0:T(8,128)(2,1)S(1)}, bf16[144,1024]{1,0:T(8,128)(2,1)S(1)}, bf16[144,1024]{1,0:T(8,128)(2,1)S(1)}) custom-call(bf16[256,2048]{1,0:T(8,128)(2,1)S(1)} %collective-permute-done.10.k_ref, bf16[288,2048]{1,0:T(8,128)(2,1)S(1)} %bitcast.8, ...), custom_call_target="tpu_custom_call" | custom-call | flops 1 | bytes 1 | tf_op jit(solution)/shard_map/late/pallas_call | solution.py:263
  62.6 1.5 %last.1 = (f32[144,1152]{1,0:T(8,128)S(1)}, bf16[144,1152]{1,0:T(8,128)(2,1)S(1)}, bf16[144,1152]{1,0:T(8,128)(2,1)S(1)}, bf16[144,1152]{1,0:T(8,128)(2,1)S(1)}, bf16[144,1152]{1,0:T(8,128)(2,1)S(1)}) custom-call(bf16[32,2048]{1,0:T(8,128)(2,1)S(1)} %collective-permute-done.9.k_ref, bf16[288,2048]{1,0:T(8,128)(2,1)S(1)} %bitcast.9, ...), custom_call_target="tpu_custom_call" | custom-call | flops 1 | bytes 1 | tf_op jit(solution)/shard_map/last/pallas_call | solution.py:263
  65.5 1.3 %collective-permute-start.16 = (bf16[144,1152]{1,0:T(8,128)(2,1)S(1)}, bf16[144,1152]{1,0:T(8,128)(2,1)S(1)}, u32[]{:S(2)}, u32[]{:S(2)}) collective-permute-start(bf16[144,1152]{1,0:T(8,128)(2,1)S(1)} %get-tuple-element.81), channel_id=1, source_target_pairs={{10,11},{14,15},{11,3},{15,7},{17,16},{21,20},{16,24},{20,28}} | collective-permute-start | bytes 995336 | tf_op jit(solution)/shard_map/ppermute | solution.py:374
  66.8 1.3 %collective-permute-start.17 = (bf16[144,1152]{1,0:T(8,128)(2,1)S(1)}, bf16[144,1152]{1,0:T(8,128)(2,1)S(1)}, u32[]{:S(2)}, u32[]{:S(2)}) collective-permute-start(bf16[144,1152]{1,0:T(8,128)(2,1)S(1)} %get-tuple-element.82), channel_id=1, source_target_pairs={{10,3},{14,7},{17,24},{21,28}} | collective-permute-start | bytes 995336 | tf_op jit(solution)/shard_map/ppermute | solution.py:374
  68.1 8.4 %collective-permute-done.14.refs_5_ = bf16[144,1152]{1,0:T(8,128)(2,1)S(1)} collective-permute-done((bf16[144,1152]{1,0:T(8,128)(2,1)S(1)}, bf16[144,1152]{1,0:T(8,128)(2,1)S(1)}, u32[]{:S(2)}, u32[]{:S(2)}) %collective-permute-start.14) | collective-permute-done | bytes 331808 | tf_op jit(solution)/shard_map/ppermute | solution.py:374
  76.5 2.7 %collective-permute-done.15.refs_6_ = bf16[144,1152]{1,0:T(8,128)(2,1)S(1)} collective-permute-done((bf16[144,1152]{1,0:T(8,128)(2,1)S(1)}, bf16[144,1152]{1,0:T(8,128)(2,1)S(1)}, u32[]{:S(2)}, u32[]{:S(2)}) %collective-permute-start.15) | collective-permute-done | bytes 331808 | tf_op jit(solution)/shard_map/ppermute | solution.py:374
  80.3 2.7 %collective-permute-start.18 = (f32[144,576]{1,0:T(8,128)S(1)}, f32[144,576]{1,0:T(8,128)S(1)}, u32[]{:S(2)}, u32[]{:S(2)}) collective-permute-start(f32[144,576]{1,0:T(8,128)S(1)} %get-tuple-element.84), channel_id=1, source_target_pairs={{0,4},{4,0},{8,12},{12,8},{16,20},{20,16},{24,28},{28,24},{1,5},{5... | collective-permute-start | bytes 995336 | tf_op jit(solution)/shard_map/ppermute | solution.py:378
  83.0 1.3 %collective-permute-done.18.other_ref = f32[144,576]{1,0:T(8,128)S(1)} collective-permute-done((f32[144,576]{1,0:T(8,128)S(1)}, f32[144,576]{1,0:T(8,128)S(1)}, u32[]{:S(2)}, u32[]{:S(2)}) %collective-permute-start.18) | collective-permute-done | bytes 331808 | tf_op jit(solution)/shard_map/ppermute | solution.py:378
  (46 shorter events, 11.6 us)
Async XLA Ops:
  0.0 5.3 %collective-permute-start.1 = (bf16[1,2,256]{2,1,0:T(2,128)(2,1)}, bf16[1,2,256]{2,1,0:T(2,128)(2,1)S(1)}, u32[]{:S(2)}, u32[]{:S(2)}) collective-permute-start(bf16[1,2,256]{2,1,0:T(2,128)(2,1)} %param.11), channel_id=1, source_target_pairs={{0,16},{4,20},{8,24},{12,28},{16,0},{20,4},{24,8},{28,12},{1,17},{... | collective-permute-start | bytes 3080 | tf_op jit(solution)/shard_map/ppermute | solution.py:308
  2.3 3.0 %collective-permute-start = (bf16[1,2,256]{2,1,0:T(2,128)(2,1)}, bf16[1,2,256]{2,1,0:T(2,128)(2,1)S(1)}, u32[]{:S(2)}, u32[]{:S(2)}) collective-permute-start(bf16[1,2,256]{2,1,0:T(2,128)(2,1)} %param.11), channel_id=1, source_target_pairs={{0,8},{4,12},{8,0},{12,4},{16,24},{20,28},{24,16},{28,20},{1,9},{5... | collective-permute-start | bytes 3080 | tf_op jit(solution)/shard_map/ppermute | solution.py:308
  3.6 4.4 %collective-permute-start.2 = (bf16[1,2,256]{2,1,0:T(2,128)(2,1)}, bf16[1,2,256]{2,1,0:T(2,128)(2,1)S(1)}, u32[]{:S(2)}, u32[]{:S(2)}) collective-permute-start(bf16[1,2,256]{2,1,0:T(2,128)(2,1)} %param.11), channel_id=1, source_target_pairs={{0,24},{4,28},{8,16},{12,20},{16,8},{20,12},{24,0},{28,4},{1,25},{... | collective-permute-start | bytes 3080 | tf_op jit(solution)/shard_map/ppermute | solution.py:308
  3.6 4.4 %copy-start.5 = (bf16[1,2,256]{2,1,0:T(2,128)(2,1)S(1)}, bf16[1,2,256]{2,1,0:T(2,128)(2,1)}, u32[]{:S(2)}) copy-start(bf16[1,2,256]{2,1,0:T(2,128)(2,1)} %param.11) | copy-start | bytes 3076
  3.6 9.1 %copy-start = (bf16[16,256]{1,0:T(8,128)(2,1)S(1)}, bf16[16,256]{1,0:T(8,128)(2,1)}, u32[]{:S(2)}) copy-start(bf16[16,256]{1,0:T(8,128)(2,1)} %blocks_ref.1) | copy-start | bytes 24580
  8.1 3.3 %collective-permute-start.4 = (bf16[4,2,256]{2,1,0:T(2,128)(2,1)S(1)}, bf16[4,2,256]{2,1,0:T(2,128)(2,1)S(1)}, u32[]{:S(2)}, u32[]{:S(2)}) collective-permute-start(bf16[4,2,256]{2,1,0:T(2,128)(2,1)S(1)} %constant_dynamic-update-slice_fusion.mine_ref), channel_id=1, source_target_pairs={{0,4},{4,0},{8,12},{12,8},{16,20},{20,16},{24,28},{28,24},{1,5},{5... | collective-permute-start | bytes 12296 | tf_op jit(solution)/shard_map/ppermute | solution.py:314
  10.5 5.6 %collective-permute-start.3 = (bf16[288,2048]{1,0:T(8,128)(2,1)S(1)}, bf16[288,2048]{1,0:T(8,128)(2,1)S(1)}, u32[]{:S(2)}, u32[]{:S(2)}) collective-permute-start(bf16[288,2048]{1,0:T(8,128)(2,1)S(1)} %bitcast.2), channel_id=1, source_target_pairs={{0,4},{4,0},{8,12},{12,8},{16,20},{20,16},{24,28},{28,24},{1,5},{5... | collective-permute-start | bytes 3538952 | tf_op jit(solution)/shard_map/ppermute | solution.py:315
  10.6 11.1 %collective-permute-start.6 = (bf16[288,2048]{1,0:T(8,128)(2,1)S(1)}, bf16[288,2048]{1,0:T(8,128)(2,1)}, u32[]{:S(2)}, u32[]{:S(2)}) collective-permute-start(bf16[288,2048]{1,0:T(8,128)(2,1)S(1)} %bitcast.3), channel_id=1, source_target_pairs={{8,16},{12,20},{16,8},{20,12},{0,4},{4,0},{24,28},{28,24},{9,17},{... | collective-permute-start | bytes 3538952 | tf_op jit(solution)/shard_map/ppermute | solution.py:312
  11.9 27.2 %collective-permute-start.5 = (bf16[288,2048]{1,0:T(8,128)(2,1)S(1)}, bf16[288,2048]{1,0:T(8,128)(2,1)S(1)}, u32[]{:S(2)}, u32[]{:S(2)}) collective-permute-start(bf16[288,2048]{1,0:T(8,128)(2,1)S(1)} %bitcast.4), channel_id=1, source_target_pairs={{0,8},{4,12},{8,0},{12,4},{16,24},{20,28},{24,16},{28,20},{1,9},{5... | collective-permute-start | bytes 3538952 | tf_op jit(solution)/shard_map/ppermute | solution.py:317
  12.7 0.7 copy-start.1
  13.4 0.7 copy-start.2
  14.1 0.7 copy-start.4
  19.5 40.3 %collective-permute-start.10 = (bf16[256,2048]{1,0:T(8,128)(2,1)S(1)}, bf16[256,2048]{1,0:T(8,128)(2,1)S(1)}, u32[]{:S(2)}, u32[]{:S(2)}) collective-permute-start(bf16[256,2048]{1,0:T(8,128)(2,1)S(1)} %slice.25), channel_id=1, source_target_pairs={{0,16},{4,20},{24,8},{28,12},{1,17},{5,21},{25,9},{29,13},{2,18},{... | collective-permute-start | bytes 3145736 | tf_op jit(solution)/shard_map/ppermute | solution.py:331
  39.2 5.3 %collective-permute-start.8 = (bf16[144,2048]{1,0:T(8,128)(2,1)S(1)}, bf16[144,2048]{1,0:T(8,128)(2,1)S(1)}, u32[]{:S(2)}, u32[]{:S(2)}) collective-permute-start(bf16[144,2048]{1,0:T(8,128)(2,1)S(1)} %get-tuple-element.85), channel_id=1, source_target_pairs={{0,4},{4,0},{8,12},{12,8},{16,20},{20,16},{24,28},{28,24},{1,5},{5... | collective-permute-start | bytes 1769480 | tf_op jit(solution)/shard_map/ppermute | solution.py:336
  40.5 4.1 %collective-permute-start.7 = (bf16[144,2048]{1,0:T(8,128)(2,1)S(1)}, bf16[144,2048]{1,0:T(8,128)(2,1)S(1)}, u32[]{:S(2)}, u32[]{:S(2)}) collective-permute-start(bf16[144,2048]{1,0:T(8,128)(2,1)S(1)} %get-tuple-element.86), channel_id=1, source_target_pairs={{0,4},{4,0},{8,12},{12,8},{16,20},{20,16},{24,28},{28,24},{1,5},{5... | collective-permute-start | bytes 1769480 | tf_op jit(solution)/shard_map/ppermute | solution.py:336
  48.1 17.4 %collective-permute-start.11 = (bf16[144,1152]{1,0:T(8,128)(2,1)S(1)}, bf16[144,1152]{1,0:T(8,128)(2,1)S(1)}, u32[]{:S(2)}, u32[]{:S(2)}) collective-permute-start(bf16[144,1152]{1,0:T(8,128)(2,1)S(1)} %get-tuple-element.76), channel_id=1, source_target_pairs={{9,10},{13,14},{10,9},{14,13},{11,8},{15,12},{2,1},{6,5},{3,0},{7,... | collective-permute-start | bytes 995336 | tf_op jit(solution)/shard_map/ppermute | solution.py:352
  50.2 16.6 %collective-permute-start.12 = (bf16[144,1152]{1,0:T(8,128)(2,1)S(1)}, bf16[144,1152]{1,0:T(8,128)(2,1)S(1)}, u32[]{:S(2)}, u32[]{:S(2)}) collective-permute-start(bf16[144,1152]{1,0:T(8,128)(2,1)S(1)} %get-tuple-element.77), channel_id=1, source_target_pairs={{8,10},{12,14},{10,8},{14,12},{11,9},{15,13},{2,0},{6,4},{3,1},{7,... | collective-permute-start | bytes 995336 | tf_op jit(solution)/shard_map/ppermute | solution.py:352
  51.6 11.0 %collective-permute-start.9 = (bf16[32,2048]{1,0:T(8,128)(2,1)S(1)}, bf16[32,2048]{1,0:T(8,128)(2,1)S(1)}, u32[]{:S(2)}, u32[]{:S(2)}) collective-permute-start(bf16[32,2048]{1,0:T(8,128)(2,1)S(1)} %slice.24), channel_id=1, source_target_pairs={{0,16},{4,20},{24,8},{28,12},{1,17},{5,21},{25,9},{29,13},{2,18},{... | collective-permute-start | bytes 393224 | tf_op jit(solution)/shard_map/ppermute | solution.py:331
  55.3 12.8 %collective-permute-start.13 = (bf16[144,1152]{1,0:T(8,128)(2,1)S(1)}, bf16[144,1152]{1,0:T(8,128)(2,1)S(1)}, u32[]{:S(2)}, u32[]{:S(2)}) collective-permute-start(bf16[144,1152]{1,0:T(8,128)(2,1)S(1)} %get-tuple-element.78), channel_id=1, source_target_pairs={{8,9},{12,13},{9,8},{13,12},{11,10},{15,14},{0,1},{4,5},{1,0},{5,4... | collective-permute-start | bytes 995336 | tf_op jit(solution)/shard_map/ppermute | solution.py:352
  64.0 12.5 %collective-permute-start.14 = (bf16[144,1152]{1,0:T(8,128)(2,1)S(1)}, bf16[144,1152]{1,0:T(8,128)(2,1)S(1)}, u32[]{:S(2)}, u32[]{:S(2)}) collective-permute-start(bf16[144,1152]{1,0:T(8,128)(2,1)S(1)} %get-tuple-element.79), channel_id=1, source_target_pairs={{8,11},{12,15},{9,3},{13,7},{11,2},{15,6},{2,8},{6,12},{3,9},{7,13... | collective-permute-start | bytes 995336 | tf_op jit(solution)/shard_map/ppermute | solution.py:374
  64.2 15.0 %collective-permute-start.15 = (bf16[144,1152]{1,0:T(8,128)(2,1)S(1)}, bf16[144,1152]{1,0:T(8,128)(2,1)S(1)}, u32[]{:S(2)}, u32[]{:S(2)}) collective-permute-start(bf16[144,1152]{1,0:T(8,128)(2,1)S(1)} %get-tuple-element.80), channel_id=1, source_target_pairs={{8,3},{12,7},{9,11},{13,15},{19,24},{23,28},{18,16},{22,20}} | collective-permute-start | bytes 995336 | tf_op jit(solution)/shard_map/ppermute | solution.py:374
  65.5 14.1 %collective-permute-start.16 = (bf16[144,1152]{1,0:T(8,128)(2,1)S(1)}, bf16[144,1152]{1,0:T(8,128)(2,1)S(1)}, u32[]{:S(2)}, u32[]{:S(2)}) collective-permute-start(bf16[144,1152]{1,0:T(8,128)(2,1)S(1)} %get-tuple-element.81), channel_id=1, source_target_pairs={{10,11},{14,15},{11,3},{15,7},{17,16},{21,20},{16,24},{20,28}} | collective-permute-start | bytes 995336 | tf_op jit(solution)/shard_map/ppermute | solution.py:374
  66.8 12.8 %collective-permute-start.17 = (bf16[144,1152]{1,0:T(8,128)(2,1)S(1)}, bf16[144,1152]{1,0:T(8,128)(2,1)S(1)}, u32[]{:S(2)}, u32[]{:S(2)}) collective-permute-start(bf16[144,1152]{1,0:T(8,128)(2,1)S(1)} %get-tuple-element.82), channel_id=1, source_target_pairs={{10,3},{14,7},{17,24},{21,28}} | collective-permute-start | bytes 995336 | tf_op jit(solution)/shard_map/ppermute | solution.py:374
  80.3 4.1 %collective-permute-start.18 = (f32[144,576]{1,0:T(8,128)S(1)}, f32[144,576]{1,0:T(8,128)S(1)}, u32[]{:S(2)}, u32[]{:S(2)}) collective-permute-start(f32[144,576]{1,0:T(8,128)S(1)} %get-tuple-element.84), channel_id=1, source_target_pairs={{0,4},{4,0},{8,12},{12,8},{16,20},{20,16},{24,28},{28,24},{1,5},{5... | collective-permute-start | bytes 995336 | tf_op jit(solution)/shard_map/ppermute | solution.py:378
  (1 other events, 0.6 us)
